TPU v7x, 32 devices: a whole 2x2x4 slice. The times are simulated.
32 devices in a mesh: gx: 2 (over core), gy: 4 (over z), gz: 4 (over y, x).
Axes of the slice: x: 2, y: 2, z: 4, core: 2. Of those that a mesh axis runs over, the one named last changes fastest.
Arguments:
- populations: float32 [19, 4, 16, 1024], P(None, 'gx', 'gy', 'gz'), as said below
- grain_cell: int32 [2, 2, 8, 512], P(None, 'gx', 'gy', 'gz'), may hold values from 0 to 7, as said below
- grain_offset: float32 [3, 2, 2, 8, 512], P(None, None, 'gx', 'gy', 'gz'), may hold values from 0 to 1
- grain_radius: float32 [2, 2, 8, 512], P(None, 'gx', 'gy', 'gz'), may hold values from 0 to 0.95, as said below
- grain_velocity: float32 [3, 2, 2, 8, 512], P(None, None, 'gx', 'gy', 'gz'), may hold values from -0.5 to 0.5
- grain_spin: float32 [3, 2, 2, 8, 512], P(None, None, 'gx', 'gy', 'gz'), may hold values from -1 to 1
- intersection: float32 [27, 2, 2, 8, 512], P(None, None, 'gx', 'gy', 'gz'), may hold values from 0 to 1, as said below
Outputs:
- new_populations: float32 [19, 4, 16, 1024], P(None, 'gx', 'gy', 'gz')
- grain_loads: float32 [6, 2, 2, 8, 512], P(None, None, 'gx', 'gy', 'gz')
Inputs may be any that keep to these rules, and one draw needn't show every extreme that they name: `populations`: every entry is positive. `grain_cell`: the 2 slots of one bin name different cells. `grain_radius`: 0 marks an empty slot; an occupied slot has a radius of 0.6 or more. `intersection`: all 27 values are 0 for an empty slot and 0.1 or more for an occupied one.
All inputs are finite; a program needn't handle non-finite values.
Results may differ from a plain program's by a relative error of at most 0.0001.
Values sent between devices are 32-bit elements; how exact they have to be, the bound alone decides.
No kernel may reach another device: no remote copies, remote signals or barrier semaphores. Data moves between devices by JAX's collectives and lax.ppermute only.
A program may use at most 64 MiB of HBM per device.

v0:
```python
import jax
import jax.numpy as jnp
from jax import lax
from jax.sharding import PartitionSpec as P

VELOCITIES = [
    (0, 0, 0),
    (1, 0, 0),
    (-1, 0, 0),
    (0, 1, 0),
    (0, -1, 0),
    (0, 0, 1),
    (0, 0, -1),
    (1, 1, 0),
    (-1, -1, 0),
    (1, -1, 0),
    (-1, 1, 0),
    (1, 0, 1),
    (-1, 0, -1),
    (1, 0, -1),
    (-1, 0, 1),
    (0, 1, 1),
    (0, -1, -1),
    (0, 1, -1),
    (0, -1, 1),
]
WEIGHTS = [1.0 / 3.0] + [1.0 / 18.0] * 6 + [1.0 / 36.0] * 12
OPPOSITE = [0, 2, 1, 4, 3, 6, 5, 8, 7, 10, 9, 12, 11, 14, 13, 16, 15, 18, 17]
NEIGHBOURS = [
    (step_x, step_y, step_z)
    for step_x in (-1, 0, 1)
    for step_y in (-1, 0, 1)
    for step_z in (-1, 0, 1)
]
relax_time = 0.8
fraction_floor = 0.1
distance_floor = 0.5
damp_normal = 2.0
damp_tangent = 1.0


def padded(block, sides, width):
    for axis, dim in sides:
        count = lax.axis_size(axis)
        forward = [(i, i + 1) for i in range(count - 1)]
        forward.append((count - 1, 0))
        backward = [(target, source) for source, target in forward]
        low = lax.ppermute(
            lax.slice_in_dim(block, block.shape[dim] - width, None, axis=dim), axis, forward
        )
        high = lax.ppermute(lax.slice_in_dim(block, 0, width, axis=dim), axis, backward)
        block = jnp.concatenate([low, block, high], axis=dim)
    return block


def slot_table(grain_cell):
    cell_codes = jnp.arange(8, dtype=jnp.int32)
    return (grain_cell[:, None] == cell_codes[None, :, None, None, None]).astype(jnp.float32)


def place_cells(values, slot_onehot):
    spreading = jnp.sum(values[:, :, None] * slot_onehot[None], axis=1)
    channels = spreading.shape[0]
    bins_x, bins_y, bins_z = (spreading.shape[2], spreading.shape[3], spreading.shape[4])
    spreading = spreading.reshape(channels, 2, 2, 2, bins_x, bins_y, bins_z).transpose(
        0, 4, 1, 5, 2, 6, 3
    )
    return spreading.reshape(channels, 2 * bins_x, 2 * bins_y, 2 * bins_z)


def pick_slots(values, slot_onehot):
    channels = values.shape[0]
    bins_x, bins_y, bins_z = (values.shape[1] // 2, values.shape[2] // 2, values.shape[3] // 2)
    grouped = values.reshape(channels, bins_x, 2, bins_y, 2, bins_z, 2).transpose(
        0, 2, 4, 6, 1, 3, 5
    )
    grouped = grouped.reshape(channels, 8, bins_x, bins_y, bins_z)
    return jnp.sum(grouped[:, None] * slot_onehot[None], axis=2)


def cross_product(first_vector, second_vector):
    return jnp.stack(
        [
            first_vector[1] * second_vector[2] - first_vector[2] * second_vector[1],
            first_vector[2] * second_vector[0] - first_vector[0] * second_vector[2],
            first_vector[0] * second_vector[1] - first_vector[1] * second_vector[0],
        ]
    )


def grain_payload(grain_cell, grain_offset, grain_radius, grain_velocity, grain_spin):
    corner = jnp.stack([grain_cell // 4, grain_cell // 2 % 2, grain_cell % 2]).astype(jnp.float32)
    return jnp.concatenate([corner + grain_offset, grain_radius[None], grain_velocity, grain_spin])


def contact_loads(local_state, neighbour):
    own_state = local_state[:, :, None]
    running = jnp.zeros((6,) + local_state.shape[1:], jnp.float32)
    for offset in NEIGHBOURS:
        other_state = neighbour(offset)[:, None]
        separation = jnp.stack(
            [
                2.0 * offset[component] + other_state[component] - own_state[component]
                for component in range(3)
            ]
        )
        distance = jnp.sqrt(jnp.sum(separation * separation, axis=0))
        normal = separation / jnp.maximum(distance, distance_floor)
        intersection_depth = jnp.maximum(own_state[3] + other_state[3] - distance, 0.0)
        strength = own_state[3] * other_state[3] * intersection_depth
        turning = own_state[3] * own_state[7:10] + other_state[3] * other_state[7:10]
        relative = own_state[4:7] - other_state[4:7] + cross_product(turning, normal)
        normal_speed = jnp.sum(relative * normal, axis=0)
        contact_force = strength * (
            -normal
            - damp_normal * normal_speed * normal
            - damp_tangent * (relative - normal_speed * normal)
        )
        contact_torque = cross_product(own_state[3] * normal, contact_force)
        running = running + jnp.sum(jnp.concatenate([contact_force, contact_torque]), axis=2)
    return running


def deposit_term(weight_cells, motion_cells, offset):
    lever = jnp.stack(
        [offset[component] + 0.5 - motion_cells[6 + component] for component in range(3)]
    )
    moving = motion_cells[0:3] + cross_product(motion_cells[3:6], lever)
    return jnp.concatenate([weight_cells, weight_cells * moving])


def solid_fields(solid_sums):
    fraction = 1.0 - jnp.exp(-solid_sums[0])
    excess = relax_time - 0.5
    weight = fraction * excess / (1.0 - fraction + excess)
    divisor = jnp.maximum(solid_sums[0], fraction_floor)
    return (weight, solid_sums[1:4] / divisor, divisor)


def equilibrium(member, density, velocity):
    vector = VELOCITIES[member]
    projected = vector[0] * velocity[0] + vector[1] * velocity[1] + vector[2] * velocity[2]
    squared = velocity[0] * velocity[0] + velocity[1] * velocity[1] + velocity[2] * velocity[2]
    return (
        WEIGHTS[member]
        * density
        * (1.0 + 3.0 * projected + 4.5 * projected * projected - 1.5 * squared)
    )


def collide(populations, weight, solid_velocity):
    density = sum(populations)
    momentum = [
        sum((VELOCITIES[member][component] * populations[member] for member in range(19)))
        for component in range(3)
    ]
    fluid_velocity = [momentum[component] / density for component in range(3)]
    fluid_state = [equilibrium(member, density, fluid_velocity) for member in range(19)]
    solid_state = [equilibrium(member, density, solid_velocity) for member in range(19)]
    collided = []
    transfer = [0.0, 0.0, 0.0]
    for member in range(19):
        reverse = OPPOSITE[member]
        exchange_term = (
            populations[reverse]
            - fluid_state[reverse]
            - (populations[member] - solid_state[member])
        )
        relaxed = (
            populations[member]
            - (1.0 - weight) * (populations[member] - fluid_state[member]) / relax_time
        )
        collided.append(relaxed + weight * exchange_term)
        for component in range(3):
            transfer[component] = (
                transfer[component] + VELOCITIES[member][component] * exchange_term
            )
    cell_force = jnp.stack([-weight * transfer[component] for component in range(3)])
    return (collided, cell_force)


def hydro_loads(shifted, weight_list, motion_cells, slot_onehot):
    force_sum = jnp.zeros_like(motion_cells[0:3])
    moment_sum = jnp.zeros_like(motion_cells[0:3])
    for member, offset in enumerate(NEIGHBOURS):
        weighted = weight_list[member] * shifted(offset)
        force_sum = force_sum + weighted
        moment_sum = moment_sum + cross_product(
            (offset[0] + 0.5, offset[1] + 0.5, offset[2] + 0.5), weighted
        )
    torque_sum = moment_sum - cross_product(motion_cells[6:9], force_sum)
    return pick_slots(jnp.concatenate([force_sum, torque_sum]), slot_onehot)


def fold_margin(block, dimension):
    interior = block.shape[dimension] - 4
    interior_part = lax.slice_in_dim(block, 2, 2 + interior, axis=dimension)
    lower_rim = lax.slice_in_dim(block, 0, 1, axis=dimension)
    upper_rim = lax.slice_in_dim(block, interior + 3, interior + 4, axis=dimension)
    widths_low = [(0, 0)] * block.ndim
    widths_high = [(0, 0)] * block.ndim
    widths_low[dimension] = (0, interior - 1)
    widths_high[dimension] = (interior - 1, 0)
    return interior_part + jnp.pad(lower_rim, widths_low) + jnp.pad(upper_rim, widths_high)


def body(
    populations, grain_cell, grain_offset, grain_radius, grain_velocity, grain_spin, intersection
):
    cell_shape = populations.shape[1:]
    slot_onehot = slot_table(grain_cell)
    payload = grain_payload(grain_cell, grain_offset, grain_radius, grain_velocity, grain_spin)
    bin_shape = payload.shape[2:]
    ghosts = padded(payload, (("gx", 2), ("gy", 3), ("gz", 4)), 1)

    def neighbour(offset):
        return ghosts[
            :,
            :,
            1 + offset[0] : 1 + offset[0] + bin_shape[0],
            1 + offset[1] : 1 + offset[1] + bin_shape[1],
            1 + offset[2] : 1 + offset[2] + bin_shape[2],
        ]

    motion_cells = place_cells(
        jnp.concatenate([grain_velocity, grain_spin, grain_offset]), slot_onehot
    )
    weight_list = [
        place_cells(intersection[member : member + 1], slot_onehot) for member in range(27)
    ]
    extended = jnp.zeros((4, cell_shape[0] + 2, cell_shape[1] + 2, cell_shape[2] + 2), jnp.float32)
    for member, offset in enumerate(NEIGHBOURS):
        deposit = deposit_term(weight_list[member], motion_cells, offset)
        extended = extended + jnp.pad(
            deposit,
            (
                (0, 0),
                (1 + offset[0], 1 - offset[0]),
                (1 + offset[1], 1 - offset[1]),
                (1 + offset[2], 1 - offset[2]),
            ),
        )
    margin = padded(extended, (("gx", 1), ("gy", 2), ("gz", 3)), 1)
    solid_sums = fold_margin(fold_margin(fold_margin(margin, 1), 2), 3)
    contact = contact_loads(payload, neighbour)
    weight, solid_velocity, divisor = solid_fields(solid_sums)
    collided, cell_force = collide(
        [populations[member] for member in range(19)], weight, solid_velocity
    )
    force_share = cell_force / divisor
    stacked = jnp.stack(collided + [force_share[0], force_share[1], force_share[2]])
    extended_layers = padded(stacked, (("gx", 1), ("gy", 2), ("gz", 3)), 1)
    passed = []
    for member in range(19):
        vector = VELOCITIES[member]
        passed.append(
            extended_layers[
                member,
                1 - vector[0] : 1 - vector[0] + cell_shape[0],
                1 - vector[1] : 1 - vector[1] + cell_shape[1],
                1 - vector[2] : 1 - vector[2] + cell_shape[2],
            ]
        )

    def shifted(offset):
        return extended_layers[
            19:22,
            1 + offset[0] : 1 + offset[0] + cell_shape[0],
            1 + offset[1] : 1 + offset[1] + cell_shape[1],
            1 + offset[2] : 1 + offset[2] + cell_shape[2],
        ]

    hydro_part = hydro_loads(shifted, weight_list, motion_cells, slot_onehot)
    return (jnp.stack(passed), hydro_part + contact)


def solution(mesh):
    placed = (
        P(None, "gx", "gy", "gz"),
        P(None, "gx", "gy", "gz"),
        P(None, None, "gx", "gy", "gz"),
        P(None, "gx", "gy", "gz"),
        P(None, None, "gx", "gy", "gz"),
        P(None, None, "gx", "gy", "gz"),
        P(None, None, "gx", "gy", "gz"),
    )
    return jax.shard_map(
        body,
        mesh=mesh,
        in_specs=placed,
        out_specs=(P(None, "gx", "gy", "gz"), P(None, None, "gx", "gy", "gz")),
        check_vma=False,
    )
```

profile of v0, /device:TPU:0, one launch (start us, length us, event | category | flops | bytes accessed | tf_op | source)
XLA Modules:
  0.0 100.1 jit_solution(14066875622640961761)
XLA Ops:
  3.4 0.7 maximum_bitcast_fusion
  4.1 0.8 slice_bitcast_fusion.102
  4.9 0.9 slice_bitcast_fusion.103
  6.5 0.8 select_reduce_fusion.26
  33.3 0.8 slice.1856
  34.5 1.1 %fusion.24 = f32[4,4,6,258]{3,2,1,0:T(8,128)S(1)} fusion(f32[3,2,4,256]{3,2,1,0:T(4,128)S(1)} %get-tuple-element.394, f32[1,2,4,256]{3,2,1,0:T(4,128)S(1)} %reshape.11165, f32[3,2,4,256]{3,2,1,0:T(4,128)S(1)} %get-tuple-element.390, f32[1,2,4,256]{3,2,1,0:T(4,128)S(1)} %reshape.11163, f32[3,2,4,256]{3,2,1,0:T(4,128)S(1)} %get-tuple-element.386, ...), kind=kLoop, calls=%fused_computation.35 | loop fusion | flops 6835968 | bytes 983808 | tf_op jit(solution)/shard_map/add | solution.py:234
  37.5 2.8 %collective-permute-start.2 = (f32[4,6,1,258]{3,2,1,0:T(1,128)S(1)}, f32[4,6,1,258]{3,2,1,0:T(1,128)S(1)}, u32[]{:S(2)}, u32[]{:S(2)}) collective-permute-start(f32[4,6,1,258]{3,2,1,0:T(1,128)S(1)} %get-tuple-element.192), channel_id=1, source_target_pairs={{0,4},{4,8},{8,12},{12,0},{1,5},{5,9},{9,13},{13,1},{2,6},{6,10},{... | collective-permute-start | bytes 74312 | tf_op jit(solution)/shard_map/ppermute | solution.py:48
  40.2 2.1 %collective-permute-start.3 = (f32[4,6,1,258]{3,2,1,0:T(1,128)S(1)}, f32[4,6,1,258]{3,2,1,0:T(1,128)S(1)}, u32[]{:S(2)}, u32[]{:S(2)}) collective-permute-start(f32[4,6,1,258]{3,2,1,0:T(1,128)S(1)} %get-tuple-element.193), channel_id=1, source_target_pairs={{4,0},{8,4},{12,8},{0,12},{5,1},{9,5},{13,9},{1,13},{6,2},{10,6},{... | collective-permute-start | bytes 74312 | tf_op jit(solution)/shard_map/ppermute | solution.py:51
  42.4 1.9 %collective-permute-done.2 = f32[4,6,1,258]{3,2,1,0:T(1,128)S(1)} collective-permute-done((f32[4,6,1,258]{3,2,1,0:T(1,128)S(1)}, f32[4,6,1,258]{3,2,1,0:T(1,128)S(1)}, u32[]{:S(2)}, u32[]{:S(2)}) %collective-permute-start.2) | collective-permute-done | bytes 24800 | tf_op jit(solution)/shard_map/ppermute | solution.py:48
  44.8 1.5 %collective-permute-start.4 = (f32[4,6,8,1]{3,2,1,0:T(8,128)S(1)}, f32[4,6,8,1]{3,2,1,0:T(8,128)S(1)}, u32[]{:S(2)}, u32[]{:S(2)}) collective-permute-start(f32[4,6,8,1]{3,2,1,0:T(8,128)S(1)} %get-tuple-element.188), channel_id=1, source_target_pairs={{0,1},{1,2},{2,3},{3,0},{4,5},{5,6},{6,7},{7,4},{8,9},{9,10},{10,1... | collective-permute-start | bytes 2312 | tf_op jit(solution)/shard_map/ppermute | solution.py:48
  46.4 1.4 %collective-permute-start.5 = (f32[4,6,8,1]{3,2,1,0:T(8,128)S(1)}, f32[4,6,8,1]{3,2,1,0:T(8,128)S(1)}, u32[]{:S(2)}, u32[]{:S(2)}) collective-permute-start(f32[4,6,8,1]{3,2,1,0:T(8,128)S(1)} %get-tuple-element.189), channel_id=1, source_target_pairs={{1,0},{2,1},{3,2},{0,3},{5,4},{6,5},{7,6},{4,7},{9,8},{10,9},{11,1... | collective-permute-start | bytes 2312 | tf_op jit(solution)/shard_map/ppermute | solution.py:51
  47.8 1.2 %collective-permute-start.14 = (f32[10,2,3,1,128]{4,3,2,1,0:T(1,128)S(1)}, f32[10,2,3,1,128]{4,3,2,1,0:T(1,128)S(1)}, u32[]{:S(2)}, u32[]{:S(2)}) collective-permute-start(f32[10,2,3,1,128]{4,3,2,1,0:T(1,128)S(1)} %get-tuple-element.352), channel_id=1, source_target_pairs={{0,4},{4,8},{8,12},{12,0},{1,5},{5,9},{9,13},{13,1},{2,6},{6,10},{... | collective-permute-start | bytes 92168 | tf_op jit(solution)/shard_map/ppermute | solution.py:48
  49.0 2.7 %collective-permute-start.15 = (f32[10,2,3,1,128]{4,3,2,1,0:T(1,128)S(1)}, f32[10,2,3,1,128]{4,3,2,1,0:T(1,128)S(1)}, u32[]{:S(2)}, u32[]{:S(2)}) collective-permute-start(f32[10,2,3,1,128]{4,3,2,1,0:T(1,128)S(1)} %get-tuple-element.353), channel_id=1, source_target_pairs={{4,0},{8,4},{12,8},{0,12},{5,1},{9,5},{13,9},{1,13},{6,2},{10,6},{... | collective-permute-start | bytes 92168 | tf_op jit(solution)/shard_map/ppermute | solution.py:51
  54.4 1.7 %collective-permute-start.16 = (f32[10,2,3,4,1]{4,3,2,1,0:T(4,128)S(1)}, f32[10,2,3,4,1]{4,3,2,1,0:T(4,128)S(1)}, u32[]{:S(2)}, u32[]{:S(2)}) collective-permute-start(f32[10,2,3,4,1]{4,3,2,1,0:T(4,128)S(1)} %get-tuple-element.308), channel_id=1, source_target_pairs={{0,1},{1,2},{2,3},{3,0},{4,5},{5,6},{6,7},{7,4},{8,9},{9,10},{10,1... | collective-permute-start | bytes 2888 | tf_op jit(solution)/shard_map/ppermute | solution.py:48
  56.1 1.3 %collective-permute-start.17 = (f32[10,2,3,4,1]{4,3,2,1,0:T(4,128)S(1)}, f32[10,2,3,4,1]{4,3,2,1,0:T(4,128)S(1)}, u32[]{:S(2)}, u32[]{:S(2)}) collective-permute-start(f32[10,2,3,4,1]{4,3,2,1,0:T(4,128)S(1)} %get-tuple-element.309), channel_id=1, source_target_pairs={{1,0},{2,1},{3,2},{0,3},{5,4},{6,5},{7,6},{4,7},{9,8},{10,9},{11,1... | collective-permute-start | bytes 2888 | tf_op jit(solution)/shard_map/ppermute | solution.py:51
  57.7 3.8 %collective-permute-done.16 = f32[10,2,3,4,1]{4,3,2,1,0:T(4,128)S(1)} collective-permute-done((f32[10,2,3,4,1]{4,3,2,1,0:T(4,128)S(1)}, f32[10,2,3,4,1]{4,3,2,1,0:T(4,128)S(1)}, u32[]{:S(2)}, u32[]{:S(2)}) %collective-permute-start.16) | collective-permute-done | bytes 992 | tf_op jit(solution)/shard_map/ppermute | solution.py:48
  61.5 1.9 %collective-permute-done.17 = f32[10,2,3,4,1]{4,3,2,1,0:T(4,128)S(1)} collective-permute-done((f32[10,2,3,4,1]{4,3,2,1,0:T(4,128)S(1)}, f32[10,2,3,4,1]{4,3,2,1,0:T(4,128)S(1)}, u32[]{:S(2)}, u32[]{:S(2)}) %collective-permute-start.17) | collective-permute-done | bytes 992 | tf_op jit(solution)/shard_map/ppermute | solution.py:51
  69.3 2.8 %collective-permute-start.9 = (f32[22,4,1,256]{3,2,1,0:T(1,128)S(1)}, f32[22,4,1,256]{3,2,1,0:T(1,128)S(1)}, u32[]{:S(2)}, u32[]{:S(2)}) collective-permute-start(f32[22,4,1,256]{3,2,1,0:T(1,128)S(1)} %get-tuple-element.190), channel_id=1, source_target_pairs={{4,0},{8,4},{12,8},{0,12},{5,1},{9,5},{13,9},{1,13},{6,2},{10,6},{... | collective-permute-start | bytes 270344 | tf_op jit(solution)/shard_map/ppermute | solution.py:51
  72.2 2.1 %collective-permute-done.9 = f32[22,4,1,256]{3,2,1,0:T(1,128)S(1)} collective-permute-done((f32[22,4,1,256]{3,2,1,0:T(1,128)S(1)}, f32[22,4,1,256]{3,2,1,0:T(1,128)S(1)}, u32[]{:S(2)}, u32[]{:S(2)}) %collective-permute-start.9) | collective-permute-done | bytes 90144 | tf_op jit(solution)/shard_map/ppermute | solution.py:51
  74.3 4.2 %collective-permute-done.8 = f32[22,4,1,256]{3,2,1,0:T(1,128)S(1)} collective-permute-done((f32[22,4,1,256]{3,2,1,0:T(1,128)S(1)}, f32[22,4,1,256]{3,2,1,0:T(1,128)S(1)}, u32[]{:S(2)}, u32[]{:S(2)}) %collective-permute-start.8) | collective-permute-done | bytes 90144 | tf_op jit(solution)/shard_map/ppermute | solution.py:48
  78.9 2.4 %collective-permute-start.11 = (f32[22,4,6,1]{3,2,1,0:T(8,128)S(1)}, f32[22,4,6,1]{3,2,1,0:T(8,128)S(1)}, u32[]{:S(2)}, u32[]{:S(2)}) collective-permute-start(f32[22,4,6,1]{3,2,1,0:T(8,128)S(1)} %get-tuple-element.186), channel_id=1, source_target_pairs={{1,0},{2,1},{3,2},{0,3},{5,4},{6,5},{7,6},{4,7},{9,8},{10,9},{11,1... | collective-permute-start | bytes 6344 | tf_op jit(solution)/shard_map/ppermute | solution.py:51
  81.3 9.0 %collective-permute-done.11 = f32[22,4,6,1]{3,2,1,0:T(8,128)S(1)} collective-permute-done((f32[22,4,6,1]{3,2,1,0:T(8,128)S(1)}, f32[22,4,6,1]{3,2,1,0:T(8,128)S(1)}, u32[]{:S(2)}, u32[]{:S(2)}) %collective-permute-start.11) | collective-permute-done | bytes 2144 | tf_op jit(solution)/shard_map/ppermute | solution.py:51
  90.3 5.1 %collective-permute-done.10 = f32[22,4,6,1]{3,2,1,0:T(8,128)S(1)} collective-permute-done((f32[22,4,6,1]{3,2,1,0:T(8,128)S(1)}, f32[22,4,6,1]{3,2,1,0:T(8,128)S(1)}, u32[]{:S(2)}, u32[]{:S(2)}) %collective-permute-start.10) | collective-permute-done | bytes 2144 | tf_op jit(solution)/shard_map/ppermute | solution.py:48
  95.4 0.8 add_add_fusion
  (421 shorter events, 43.6 us)
Async XLA Ops:
  2.8 39.6 %collective-permute-start.13 = (f32[10,2,1,2,128]{4,3,2,1,0:T(2,128)S(1)}, f32[10,2,1,2,128]{4,3,2,1,0:T(2,128)S(1)}, u32[]{:S(2)}, u32[]{:S(2)}) collective-permute-start(f32[10,2,1,2,128]{4,3,2,1,0:T(2,128)S(1)} %pad_maximum_fusion.89), channel_id=1, source_target_pairs={{16,0},{0,16},{17,1},{1,17},{18,2},{2,18},{19,3},{3,19},{20,4},{4,... | collective-permute-start | bytes 61448 | tf_op jit(solution)/shard_map/ppermute | solution.py:51
  3.3 39.1 %collective-permute-start.12 = (f32[10,2,1,2,128]{4,3,2,1,0:T(2,128)S(1)}, f32[10,2,1,2,128]{4,3,2,1,0:T(2,128)S(1)}, u32[]{:S(2)}, u32[]{:S(2)}) collective-permute-start(f32[10,2,1,2,128]{4,3,2,1,0:T(2,128)S(1)} %pad_maximum_fusion.89), channel_id=1, source_target_pairs={{0,16},{16,0},{1,17},{17,1},{2,18},{18,2},{3,19},{19,3},{4,20},{20... | collective-permute-start | bytes 61448 | tf_op jit(solution)/shard_map/ppermute | solution.py:48
  34.2 8.1 %copy-start = (f32[3,2,1,2,128]{4,3,2,1,0:T(2,128)S(1)}, f32[3,2,1,2,128]{4,3,2,1,0:T(2,128)}, u32[]{:S(2)}) copy-start(f32[3,2,1,2,128]{4,3,2,1,0:T(2,128)} %param.11) | copy-start | bytes 18436
  34.2 8.1 %copy-start.1 = (f32[3,2,1,2,128]{4,3,2,1,0:T(2,128)S(1)}, f32[3,2,1,2,128]{4,3,2,1,0:T(2,128)}, u32[]{:S(2)}) copy-start(f32[3,2,1,2,128]{4,3,2,1,0:T(2,128)} %param.12) | copy-start | bytes 18436
  34.2 8.1 %copy-start.2 = (f32[2,1,2,128]{3,2,1,0:T(2,128)S(1)}, f32[2,1,2,128]{3,2,1,0:T(2,128)}, u32[]{:S(2)}) copy-start(f32[2,1,2,128]{3,2,1,0:T(2,128)} %param.10) | copy-start | bytes 6148
  34.5 17.6 %copy-start.7 = (pred[2]{0:T(512)(128)(4,1)S(1)}, pred[2]{0:T(512)(128)(4,1)}, u32[]{:S(2)}) copy-start(pred[2]{0:T(512)(128)(4,1)} %constant.113.clone.1) | copy-start | bytes 10
  35.7 16.6 %copy-start.6 = (pred[4]{0:T(512)(128)(4,1)S(1)}, pred[4]{0:T(512)(128)(4,1)}, u32[]{:S(2)}) copy-start(pred[4]{0:T(512)(128)(4,1)} %constant.114.clone.1) | copy-start | bytes 16
  35.7 1.4 %collective-permute-start = (f32[4,1,6,258]{3,2,1,0:T(8,128)S(1)}, f32[4,1,6,258]{3,2,1,0:T(8,128)S(1)}, u32[]{:S(2)}, u32[]{:S(2)}) collective-permute-start(f32[4,1,6,258]{3,2,1,0:T(8,128)S(1)} %get-tuple-element.302), channel_id=1, source_target_pairs={{0,16},{16,0},{1,17},{17,1},{2,18},{18,2},{3,19},{19,3},{4,20},{20... | collective-permute-start | bytes 74312 | tf_op jit(solution)/shard_map/ppermute | solution.py:48
  36.2 1.2 %collective-permute-start.1 = (f32[4,1,6,258]{3,2,1,0:T(8,128)S(1)}, f32[4,1,6,258]{3,2,1,0:T(8,128)S(1)}, u32[]{:S(2)}, u32[]{:S(2)}) collective-permute-start(f32[4,1,6,258]{3,2,1,0:T(8,128)S(1)} %get-tuple-element.303), channel_id=1, source_target_pairs={{16,0},{0,16},{17,1},{1,17},{18,2},{2,18},{19,3},{3,19},{20,4},{4,... | collective-permute-start | bytes 74312 | tf_op jit(solution)/shard_map/ppermute | solution.py:51
  36.3 16.1 %copy-start.5 = (pred[256]{0:T(512)(128)(4,1)S(1)}, pred[256]{0:T(512)(128)(4,1)}, u32[]{:S(2)}) copy-start(pred[256]{0:T(512)(128)(4,1)} %constant.115.clone.1) | copy-start | bytes 772
  37.5 6.8 %collective-permute-start.2 = (f32[4,6,1,258]{3,2,1,0:T(1,128)S(1)}, f32[4,6,1,258]{3,2,1,0:T(1,128)S(1)}, u32[]{:S(2)}, u32[]{:S(2)}) collective-permute-start(f32[4,6,1,258]{3,2,1,0:T(1,128)S(1)} %get-tuple-element.192), channel_id=1, source_target_pairs={{0,4},{4,8},{8,12},{12,0},{1,5},{5,9},{9,13},{13,1},{2,6},{6,10},{... | collective-permute-start | bytes 74312 | tf_op jit(solution)/shard_map/ppermute | solution.py:48
  40.2 4.4 %collective-permute-start.3 = (f32[4,6,1,258]{3,2,1,0:T(1,128)S(1)}, f32[4,6,1,258]{3,2,1,0:T(1,128)S(1)}, u32[]{:S(2)}, u32[]{:S(2)}) collective-permute-start(f32[4,6,1,258]{3,2,1,0:T(1,128)S(1)} %get-tuple-element.193), channel_id=1, source_target_pairs={{4,0},{8,4},{12,8},{0,12},{5,1},{9,5},{13,9},{1,13},{6,2},{10,6},{... | collective-permute-start | bytes 74312 | tf_op jit(solution)/shard_map/ppermute | solution.py:51
  44.8 6.9 %collective-permute-start.4 = (f32[4,6,8,1]{3,2,1,0:T(8,128)S(1)}, f32[4,6,8,1]{3,2,1,0:T(8,128)S(1)}, u32[]{:S(2)}, u32[]{:S(2)}) collective-permute-start(f32[4,6,8,1]{3,2,1,0:T(8,128)S(1)} %get-tuple-element.188), channel_id=1, source_target_pairs={{0,1},{1,2},{2,3},{3,0},{4,5},{5,6},{6,7},{7,4},{8,9},{9,10},{10,1... | collective-permute-start | bytes 2312 | tf_op jit(solution)/shard_map/ppermute | solution.py:48
  46.4 5.4 %collective-permute-start.5 = (f32[4,6,8,1]{3,2,1,0:T(8,128)S(1)}, f32[4,6,8,1]{3,2,1,0:T(8,128)S(1)}, u32[]{:S(2)}, u32[]{:S(2)}) collective-permute-start(f32[4,6,8,1]{3,2,1,0:T(8,128)S(1)} %get-tuple-element.189), channel_id=1, source_target_pairs={{1,0},{2,1},{3,2},{0,3},{5,4},{6,5},{7,6},{4,7},{9,8},{10,9},{11,1... | collective-permute-start | bytes 2312 | tf_op jit(solution)/shard_map/ppermute | solution.py:51
  47.8 6.3 %collective-permute-start.14 = (f32[10,2,3,1,128]{4,3,2,1,0:T(1,128)S(1)}, f32[10,2,3,1,128]{4,3,2,1,0:T(1,128)S(1)}, u32[]{:S(2)}, u32[]{:S(2)}) collective-permute-start(f32[10,2,3,1,128]{4,3,2,1,0:T(1,128)S(1)} %get-tuple-element.352), channel_id=1, source_target_pairs={{0,4},{4,8},{8,12},{12,0},{1,5},{5,9},{9,13},{13,1},{2,6},{6,10},{... | collective-permute-start | bytes 92168 | tf_op jit(solution)/shard_map/ppermute | solution.py:48
  49.0 5.1 %collective-permute-start.15 = (f32[10,2,3,1,128]{4,3,2,1,0:T(1,128)S(1)}, f32[10,2,3,1,128]{4,3,2,1,0:T(1,128)S(1)}, u32[]{:S(2)}, u32[]{:S(2)}) collective-permute-start(f32[10,2,3,1,128]{4,3,2,1,0:T(1,128)S(1)} %get-tuple-element.353), channel_id=1, source_target_pairs={{4,0},{8,4},{12,8},{0,12},{5,1},{9,5},{13,9},{1,13},{6,2},{10,6},{... | collective-permute-start | bytes 92168 | tf_op jit(solution)/shard_map/ppermute | solution.py:51
  53.6 15.6 %collective-permute-start.7 = (f32[22,1,4,256]{3,2,1,0:T(4,128)S(1)}, f32[22,1,4,256]{3,2,1,0:T(4,128)S(1)}, u32[]{:S(2)}, u32[]{:S(2)}) collective-permute-start(f32[22,1,4,256]{3,2,1,0:T(4,128)S(1)} %get-tuple-element.304), channel_id=1, source_target_pairs={{16,0},{0,16},{17,1},{1,17},{18,2},{2,18},{19,3},{3,19},{20,4},{4,... | collective-permute-start | bytes 270344 | tf_op jit(solution)/shard_map/ppermute | solution.py:51
  53.6 15.5 %collective-permute-start.6 = (f32[22,1,4,256]{3,2,1,0:T(4,128)S(1)}, f32[22,1,4,256]{3,2,1,0:T(4,128)S(1)}, u32[]{:S(2)}, u32[]{:S(2)}) collective-permute-start(f32[22,1,4,256]{3,2,1,0:T(4,128)S(1)} %get-tuple-element.305), channel_id=1, source_target_pairs={{0,16},{16,0},{1,17},{17,1},{2,18},{18,2},{3,19},{19,3},{4,20},{20... | collective-permute-start | bytes 270344 | tf_op jit(solution)/shard_map/ppermute | solution.py:48
  54.4 7.1 %collective-permute-start.16 = (f32[10,2,3,4,1]{4,3,2,1,0:T(4,128)S(1)}, f32[10,2,3,4,1]{4,3,2,1,0:T(4,128)S(1)}, u32[]{:S(2)}, u32[]{:S(2)}) collective-permute-start(f32[10,2,3,4,1]{4,3,2,1,0:T(4,128)S(1)} %get-tuple-element.308), channel_id=1, source_target_pairs={{0,1},{1,2},{2,3},{3,0},{4,5},{5,6},{6,7},{7,4},{8,9},{9,10},{10,1... | collective-permute-start | bytes 2888 | tf_op jit(solution)/shard_map/ppermute | solution.py:48
  56.1 7.3 %collective-permute-start.17 = (f32[10,2,3,4,1]{4,3,2,1,0:T(4,128)S(1)}, f32[10,2,3,4,1]{4,3,2,1,0:T(4,128)S(1)}, u32[]{:S(2)}, u32[]{:S(2)}) collective-permute-start(f32[10,2,3,4,1]{4,3,2,1,0:T(4,128)S(1)} %get-tuple-element.309), channel_id=1, source_target_pairs={{1,0},{2,1},{3,2},{0,3},{5,4},{6,5},{7,6},{4,7},{9,8},{10,9},{11,1... | collective-permute-start | bytes 2888 | tf_op jit(solution)/shard_map/ppermute | solution.py:51
  69.3 5.0 %collective-permute-start.9 = (f32[22,4,1,256]{3,2,1,0:T(1,128)S(1)}, f32[22,4,1,256]{3,2,1,0:T(1,128)S(1)}, u32[]{:S(2)}, u32[]{:S(2)}) collective-permute-start(f32[22,4,1,256]{3,2,1,0:T(1,128)S(1)} %get-tuple-element.190), channel_id=1, source_target_pairs={{4,0},{8,4},{12,8},{0,12},{5,1},{9,5},{13,9},{1,13},{6,2},{10,6},{... | collective-permute-start | bytes 270344 | tf_op jit(solution)/shard_map/ppermute | solution.py:51
  72.1 6.3 %collective-permute-start.8 = (f32[22,4,1,256]{3,2,1,0:T(1,128)S(1)}, f32[22,4,1,256]{3,2,1,0:T(1,128)S(1)}, u32[]{:S(2)}, u32[]{:S(2)}) collective-permute-start(f32[22,4,1,256]{3,2,1,0:T(1,128)S(1)} %get-tuple-element.191), channel_id=1, source_target_pairs={{0,4},{4,8},{8,12},{12,0},{1,5},{5,9},{9,13},{13,1},{2,6},{6,10},{... | collective-permute-start | bytes 270344 | tf_op jit(solution)/shard_map/ppermute | solution.py:48
  78.9 11.4 %collective-permute-start.11 = (f32[22,4,6,1]{3,2,1,0:T(8,128)S(1)}, f32[22,4,6,1]{3,2,1,0:T(8,128)S(1)}, u32[]{:S(2)}, u32[]{:S(2)}) collective-permute-start(f32[22,4,6,1]{3,2,1,0:T(8,128)S(1)} %get-tuple-element.186), channel_id=1, source_target_pairs={{1,0},{2,1},{3,2},{0,3},{5,4},{6,5},{7,6},{4,7},{9,8},{10,9},{11,1... | collective-permute-start | bytes 6344 | tf_op jit(solution)/shard_map/ppermute | solution.py:51
  81.2 14.2 %collective-permute-start.10 = (f32[22,4,6,1]{3,2,1,0:T(8,128)S(1)}, f32[22,4,6,1]{3,2,1,0:T(8,128)S(1)}, u32[]{:S(2)}, u32[]{:S(2)}) collective-permute-start(f32[22,4,6,1]{3,2,1,0:T(8,128)S(1)} %get-tuple-element.187), channel_id=1, source_target_pairs={{0,1},{1,2},{2,3},{3,0},{4,5},{5,6},{6,7},{7,4},{8,9},{9,10},{10,1... | collective-permute-start | bytes 6344 | tf_op jit(solution)/shard_map/ppermute | solution.py:48
  (3 other events, 4.5 us)
where the time goes:
time: 101 us; the launch traced here: 100 us
  local copies, waits for them, and re-layouts  30.3 us (30%)
  waiting for transfers between devices  29.4 us (29%)
  starting transfers between devices  21.7 us (21%)
  other arithmetic  16.1 us (16%)
  between operations  2.67 us (3%)
    ppermute x9, waiting for transfers between devices, padded(): lax.ppermute(lax.slice_in_dim(block, block.shape[dim] - width, None, axis...  15.7 us
    ppermute x9, waiting for transfers between devices, padded(): lax.ppermute(lax.slice_in_dim(block, 0, width, axis=dim), axis, backward)  13.7 us
    ppermute x9, starting transfers between devices, padded(): lax.ppermute(lax.slice_in_dim(block, 0, width, axis=dim), axis, backward)  13.4 us
    ppermute x9, starting transfers between devices, padded(): lax.ppermute(lax.slice_in_dim(block, block.shape[dim] - width, None, axis...  8.27 us
    reshape x27, local copies, waits for them, and re-layouts, place_cells(): return spreading.reshape(channels, 2 * bins_x, 2 * bins_y, 2 * bins_z)  8.06 us
    mul x27, local copies, waits for them, and re-layouts, deposit_term(): return jnp.concatenate([weight_cells, weight_cells * moving])  7.99 us
    transpose x27, local copies, waits for them, and re-layouts, place_cells(): spreading.reshape(channels, 2, 2, 2, bins_x, bins_y, bins_z)  6.03 us
    unnamed x37, other arithmetic  2.11 us
  transfers between devices with their start and end apart: 18, of which 10 were waited for; matrix products, arithmetic and copies ran while one was open for 39% of the time, Pallas kernels for 0%

commit v1 on v0

v1 whole, which is shorter than its diff:
```python
import functools

import jax
import jax.numpy as jnp
from jax import lax
from jax.experimental import pallas as pl
from jax.experimental.pallas import tpu as pltpu
from jax.sharding import PartitionSpec as P

VELOCITIES = [
    (0, 0, 0),
    (1, 0, 0),
    (-1, 0, 0),
    (0, 1, 0),
    (0, -1, 0),
    (0, 0, 1),
    (0, 0, -1),
    (1, 1, 0),
    (-1, -1, 0),
    (1, -1, 0),
    (-1, 1, 0),
    (1, 0, 1),
    (-1, 0, -1),
    (1, 0, -1),
    (-1, 0, 1),
    (0, 1, 1),
    (0, -1, -1),
    (0, 1, -1),
    (0, -1, 1),
]
WEIGHTS = [1.0 / 3.0] + [1.0 / 18.0] * 6 + [1.0 / 36.0] * 12
relax_time = 0.8
fraction_floor = 0.1
distance_floor = 0.5

E0, RADIUS, CODE, PLACE = 9, 36, 37, 38
POPS_LANE, SLOT_LANE = 41, 64
Y_FIELDS = list(range(9)) + [RADIUS, CODE]
Y_GRAIN, Y_CORNER, Y_BLOCKS = 19, 34, 36
F32 = jnp.float32


def iota(shape, dim):
    return lax.broadcasted_iota(jnp.int32, shape, dim)


def pick_lanes(values, index):
    return jnp.take_along_axis(values, index, axis=1, mode="promise_in_bounds")


def roll(values, shift, axis):
    size = values.shape[axis]
    return pltpu.roll(values, shift % size, axis) if shift % size else values


def cross(a, b):
    return [
        a[1] * b[2] - a[2] * b[1],
        a[2] * b[0] - a[0] * b[2],
        a[0] * b[1] - a[1] * b[0],
    ]


class Group:
    def __init__(self, refs):
        self.pops, self.cell, self.off, self.rad, self.vel, self.spin, self.inter = refs

    def slot(self, s, field):
        if field < 3:
            return self.vel[field, s, 0]
        if field < 6:
            return self.spin[field - 3, s, 0]
        if field < 9:
            return self.off[field - 6, s, 0]
        if field < RADIUS:
            return self.inter[field - E0, s, 0]
        if field == RADIUS:
            return self.rad[s, 0]
        return self.cell[s, 0].astype(F32)

    def place(self, s):
        code = self.cell[s, 0]
        corner = [code >> 2, (code >> 1) & 1, code & 1]
        return [corner[c].astype(F32) + self.off[c, s, 0] for c in range(3)]


def split_groups(refs, groups):
    return [Group(refs[7 * g : 7 * g + 7]) for g in range(groups)]


def z_pack_kernel(groups, flags, *refs):
    out = refs[-1]
    high = flags[1] == 1
    lane = iota((4, 128), 1)
    index4 = jnp.where(high, jnp.full((4, 128), 127, jnp.int32), jnp.zeros((4, 128), jnp.int32))
    index2 = jnp.where(high, jnp.full((2, 128), 127, jnp.int32), jnp.zeros((2, 128), jnp.int32))
    lane2 = iota((2, 128), 1)
    for g, group in enumerate(split_groups(refs, groups)):
        grain = jnp.zeros((2, 128), F32)
        for s in range(2):
            values = [group.slot(s, field) for field in range(38)] + group.place(s)
            for field, value in enumerate(values):
                grain = jnp.where(lane2 == SLOT_LANE * s + field, pick_lanes(value, index2), grain)
        both = jnp.concatenate([grain[0:1], grain[0:1], grain[1:2], grain[1:2]], axis=0)
        for i in range(2):
            rows = both
            for member in range(19):
                value = group.pops[member, i]
                last = value.shape[1] - 128
                tile = jnp.where(high, value[:, last:], value[:, :128])
                rows = jnp.where(lane == POPS_LANE + member, pick_lanes(tile, index4), rows)
            out[g, 4 * i : 4 * i + 4, :] = rows


def y_pack_kernel(groups, flags, *refs):
    out = refs[-1]
    high = flags[0] == 1
    for g, group in enumerate(split_groups(refs, groups)):
        for member in range(19):
            for i in range(2):
                row = jnp.where(high, group.pops[member, i, 3:4], group.pops[member, i, 0:1])
                for t in range(2):
                    at = 4 * g + 2 * i + t
                    out[member, at : at + 1, :] = row[:, 128 * t : 128 * t + 128]
        for s in range(2):
            for f in range(29):
                if f < 11:
                    value = group.slot(s, Y_FIELDS[f])
                else:
                    kx, q, kz = (f - 11) // 6, (f - 11) // 3 % 2, (f - 11) % 3
                    value = group.inter[9 * kx + 3 * (q + flags[0]) + kz, s, 0]
                q = 2 * f + s
                at = 4 * g + q % 4
                out[Y_GRAIN + q // 4, at : at + 1, :] = jnp.where(high, value[1:2], value[0:1])
    out[Y_GRAIN + 14, :, :] = jnp.where(
        iota((4 * groups, 128), 0) % 4 >= 2, 0.0, out[Y_GRAIN + 14, :, :]
    )
    out[Y_CORNER:Y_BLOCKS, :, :] = jnp.zeros((2, 4 * groups, 128), F32)


def store_z(groups, paired, flags, first, second, held):
    side = flags[1]
    for g in range(groups):
        held[side, g] = first[g]
        held[1 - side, g] = second[(g + 1) % 2 if paired else g]


def corner_kernel(groups, paired, flags, first, second, rows, out, held):
    store_z(groups, paired, flags, first, second, held)
    high = flags[0] == 1
    for side in range(2):
        for g in range(groups):
            for i in range(2):
                value = held[side, g, 4 * i : 4 * i + 4, :]
                at = 4 * g + 2 * i
                out[side, at : at + 2, :] = jnp.where(high, value[2:4], value[0:2])


def equilibrium_parts(velocity):
    squared = 1.0 - 1.5 * (
        velocity[0] * velocity[0] + velocity[1] * velocity[1] + velocity[2] * velocity[2]
    )
    return squared


def dot_lattice(vector, velocity):
    total = None
    for c in range(3):
        if vector[c]:
            if total is None:
                total = velocity[c] if vector[c] > 0 else -velocity[c]
            else:
                total = total + velocity[c] if vector[c] > 0 else total - velocity[c]
    return total


def main_kernel(groups, paired, flags, *refs):
    layers = 2 * groups
    block = split_groups(refs, groups)
    z_first, z_second, y_first, y_second = refs[7 * groups : 7 * groups + 4]
    out_pops, out_loads = refs[7 * groups + 4 : 7 * groups + 6]
    held_z, held_y, edge, placed, solid, passed, share = refs[7 * groups + 6 :]
    targets = [0, 1, 2, layers - 1]

    store_z(groups, paired, flags, z_first, z_second, held_z)
    side = flags[0]
    held_y[side] = y_first[...]
    for b in range(Y_BLOCKS):
        value = y_second[b]
        held_y[1 - side, b] = roll(value, 4, 0) if paired else value
    for s in range(2):
        for layer in range(layers):
            g, i = layer // 2, layer % 2
            at = 4 * g + 2 * i
            edge[s, layer, 2:6, :] = held_z[s, g, 4 * i : 4 * i + 4, :]
            edge[s, layer, 0:2, :] = held_y[0, Y_CORNER + s, at : at + 2, :]
            edge[s, layer, 6:8, :] = held_y[1, Y_CORNER + s, at : at + 2, :]

    row8 = iota((8, 128), 0)
    lane8 = iota((8, 128), 1)
    half = lane8 // 2

    def y_row(end, g, s, field):
        if field in Y_FIELDS:
            f = Y_FIELDS.index(field)
        else:
            k = field - E0
            q = k // 3 % 3 - (1 - end)
            if q not in (0, 1):
                return jnp.zeros((1, 128), F32)
            f = 11 + 6 * (k // 9) + 3 * q + k % 3
        q = 2 * f + s
        at = 4 * g + q % 4
        return held_y[end, Y_GRAIN + q // 4, at : at + 1, :]

    def column(matrix, at):
        return jnp.broadcast_to(matrix[:, at : at + 1], (8, 128))

    def spread(g, s, field):
        own = block[g].slot(s, field)
        low, high = y_row(0, g, s, field), y_row(1, g, s, field)
        rows = jnp.where(
            row8 < 4,
            jnp.where(row8 < 2, low, own[0:1]),
            jnp.where(row8 < 6, own[1:2], high),
        )
        at = SLOT_LANE * s + field
        return jnp.concatenate(
            [
                pick_lanes(rows, half),
                pick_lanes(rows, half + 64),
                jnp.where(
                    lane8 < 64, column(edge[1, 2 * g], at), column(edge[0, 2 * g], at)
                ),
            ],
            axis=1,
        )

    cell_code = (
        2 * (iota((8, 384), 0) % 2) + iota((8, 384), 1) % 2
    ).astype(F32)
    masks = []
    for g in range(groups):
        codes = [spread(g, s, CODE) for s in range(2)]
        for i in range(2):
            masks.append([codes[s] == cell_code + 4.0 * i for s in range(2)])
    for g in range(groups):
        for field in range(36):
            value0, value1 = spread(g, 0, field), spread(g, 1, field)
            for i in range(2):
                mask0, mask1 = masks[2 * g + i]
                placed[field, 2 * g + i] = jnp.where(
                    mask0, value0, jnp.where(mask1, value1, 0.0)
                )
    motion = []
    for layer in range(layers):
        spin = [placed[3 + c, layer] for c in range(3)]
        arm = [0.5 - placed[6 + c, layer] for c in range(3)]
        turn = cross(spin, arm)
        for c in range(3):
            placed[c, layer] = placed[c, layer] + turn[c]

    for n, target in enumerate(targets):
        total = [None] * 4
        for kz in (-1, 0, 1):
            along_z = [None] * 4
            for ky in (-1, 0, 1):
                along_y = [None] * 4
                for kx in (-1, 0, 1):
                    source = (target - kx) % layers
                    weight = placed[E0 + 9 * (kx + 1) + 3 * (ky + 1) + kz + 1, source]
                    spin = [placed[3 + c, source] for c in range(3)]
                    base = [placed[c, source] for c in range(3)]
                    k = (kx, ky, kz)
                    terms = [weight]
                    for c in range(3):
                        u, v = (c + 1) % 3, (c + 2) % 3
                        speed = base[c]
                        if k[v]:
                            speed = speed + spin[u] if k[v] > 0 else speed - spin[u]
                        if k[u]:
                            speed = speed - spin[v] if k[u] > 0 else speed + spin[v]
                        terms.append(weight * speed)
                    along_y = [t if a is None else a + t for a, t in zip(along_y, terms)]
                moved = [roll(a, ky, 0) for a in along_y]
                along_z = [t if a is None else a + t for a, t in zip(along_z, moved)]
            moved = [roll(a, kz, 1) for a in along_z]
            total = [t if a is None else a + t for a, t in zip(total, moved)]
        for f in range(4):
            solid[f, n] = total[f]

    for n, target in enumerate(targets):
        g, i = target // 2, target % 2
        for t in range(3):
            tile = slice(128 * t, 128 * t + 128)
            f = []
            for member in range(19):
                if t < 2:
                    own = block[g].pops[member, i, :, tile]
                    at = 4 * g + 2 * i + t
                    low = held_y[0, member, at : at + 1, :]
                    high = held_y[1, member, at : at + 1, :]
                    f.append(jnp.concatenate([low, low, own, high, high], axis=0))
                else:
                    at = POPS_LANE + member
                    f.append(
                        jnp.where(
                            lane8 < 64, column(edge[1, target], at), column(edge[0, target], at)
                        )
                    )
            sums = [solid[c, n, :, tile] for c in range(4)]
            fraction = 1.0 - jnp.exp(-sums[0])
            excess = relax_time - 0.5
            weight = fraction * excess / (1.0 - fraction + excess)
            inverse = 1.0 / jnp.maximum(sums[0], fraction_floor)
            solid_velocity = [sums[1 + c] * inverse for c in range(3)]
            density = sum(f[1:], f[0])
            momentum = []
            for c in range(3):
                plus = [f[m] for m in range(19) if VELOCITIES[m][c] > 0]
                minus = [f[m] for m in range(19) if VELOCITIES[m][c] < 0]
                momentum.append(sum(plus[1:], plus[0]) - sum(minus[1:], minus[0]))
            per_density = 1.0 / density
            fluid_velocity = [momentum[c] * per_density for c in range(3)]
            for c in range(3):
                share[c, n, :, tile] = (
                    weight * inverse * (momentum[c] - density * solid_velocity[c])
                )
            relax = (1.0 - weight) * (1.0 / relax_time)
            keep = 1.0 - relax
            fluid_base = equilibrium_parts(fluid_velocity)
            solid_base = equilibrium_parts(solid_velocity)
            if n < 2:
                members = list(range(19))
            else:
                sign = -1 if n == 2 else 1
                members = [m for m in range(19) if VELOCITIES[m][0] == sign]
            done = {}
            for member in [0] + list(range(1, 19, 2)):
                reverse = member + 1 if member else 0
                if member not in members and reverse not in members:
                    continue
                part = WEIGHTS[member] * density
                if member == 0:
                    fluid = [part * fluid_base] * 2
                    settled = [part * solid_base] * 2
                else:
                    vector = VELOCITIES[member]
                    ends = []
                    for base, velocity in (
                        (fluid_base, fluid_velocity),
                        (solid_base, solid_velocity),
                    ):
                        along = dot_lattice(vector, velocity)
                        even = base + 4.5 * along * along
                        odd = 3.0 * along
                        ends.append([part * (even + odd), part * (even - odd)])
                    fluid, settled = ends
                pair = [f[member], f[reverse]]
                for way, m in enumerate((member, reverse)[: 2 if member else 1]):
                    if m not in members:
                        continue
                    exchange = (pair[1 - way] - fluid[1 - way]) - (pair[way] - settled[way])
                    value = keep * pair[way] + relax * fluid[way] + weight * exchange
                    passed[m, n, :, tile] = value

    at_layer = {0: 0, 1: 1, 2: 2, -1: 3}
    for member in range(19):
        vector = VELOCITIES[member]
        for i in range(2):
            value = passed[member, at_layer[i - vector[0]]]
            value = roll(value, vector[2], 1)[:, :256]
            out_pops[member, i] = roll(value, vector[1] - 2, 0)[0:4]

    force = [[None] * 3 for _ in range(2)]
    moment = [[None] * 3 for _ in range(2)]

    def add(store, c, value, sign=1):
        if store[c] is None:
            store[c] = value if sign > 0 else -value
        else:
            store[c] = store[c] + value if sign > 0 else store[c] - value

    for kz in (-1, 0, 1):
        across = [[roll(share[c, n], -kz, 1)[:, :256] for c in range(3)] for n in range(4)]
        for ky in (-1, 0, 1):
            near = [[roll(across[n][c], -ky, 0) for c in range(3)] for n in range(4)]
            for i in range(2):
                together = [None] * 3
                for kx in (-1, 0, 1):
                    weight = placed[E0 + 9 * (kx + 1) + 3 * (ky + 1) + kz + 1, i, :, :256]
                    for c in range(3):
                        value = weight * near[at_layer[i + kx]][c]
                        add(together, c, value)
                        if kx and c == 2:
                            add(moment[i], 1, value, -kx)
                        if kx and c == 1:
                            add(moment[i], 2, value, kx)
                for c in range(3):
                    add(force[i], c, together[c])
                if ky:
                    add(moment[i], 0, together[2], ky)
                    add(moment[i], 2, together[0], -ky)
                if kz:
                    add(moment[i], 0, together[1], -kz)
                    add(moment[i], 1, together[0], kz)
    hydro = []
    for i in range(2):
        arm = [0.5 - placed[6 + c, i, :, :256] for c in range(3)]
        turn = cross(arm, force[i])
        hydro.append(force[i] + [moment[i][c] + turn[c] for c in range(3)])

    own = block[0]

    def rows_own(values):
        return jnp.concatenate([values[0], values[0], values[1], values[1]], axis=0)

    def position(code, offset):
        first = jnp.floor(code * 0.25)
        rest = code - 4.0 * first
        second = jnp.floor(rest * 0.5)
        corner = [first, second, rest - 2.0 * second]
        return [corner[c] + offset[c] for c in range(3)]

    def own_field(field):
        return rows_own([own.slot(s, field) for s in range(2)])

    a_place = position(own_field(CODE), [own_field(6 + c) for c in range(3)])
    a_radius = own_field(RADIUS)
    a_speed = [own_field(c) for c in range(3)]
    a_turn = [a_radius * own_field(3 + c) for c in range(3)]
    push = [jnp.zeros((8, 128), F32)] * 3
    twist = [jnp.zeros((8, 128), F32)] * 3
    fields = [CODE, 6, 7, 8, RADIUS, 0, 1, 2, 3, 4, 5]
    lanes = [PLACE, PLACE + 1, PLACE + 2, RADIUS, 0, 1, 2, 3, 4, 5]
    for oy in (-1, 0, 1):
        for g in range(groups):
            steps = [0] if g == 0 else []
            if g == 1:
                steps = steps + [1]
            if g == groups - 1:
                steps = steps + [-1]
            state = []
            for field in fields:
                values = []
                for s in range(2):
                    value = block[g].slot(s, field)
                    if oy < 0:
                        value = jnp.concatenate([y_row(0, g, s, field), value[0:1]], axis=0)
                    if oy > 0:
                        value = jnp.concatenate([value[1:2], y_row(1, g, s, field)], axis=0)
                    values.append(value)
                state.append(jnp.concatenate(values + values, axis=0))
            state = position(state[0], state[1:4]) + state[4:]
            for oz in (-1, 0, 1):
                other = state
                if oz:
                    matrix = edge[(oz + 1) // 2, 2 * g]
                    at = 2 * (oy + 1)
                    rows = jnp.concatenate([matrix[at : at + 1], matrix[at + 2 : at + 3]], axis=0)
                    turned = roll(rows, -SLOT_LANE, 1)
                    matrix = jnp.concatenate([rows, turned, rows, turned], axis=0)
                    end = lane8 == (0 if oz < 0 else 127)
                    other = [
                        jnp.where(end, column(matrix, lanes[q]), roll(state[q], -oz, 1))
                        for q in range(10)
                    ]
                b_radius = other[3]
                turning = [a_turn[c] + b_radius * other[7 + c] for c in range(3)]
                slip = [a_speed[c] - other[4 + c] for c in range(3)]
                gap = [other[c] - a_place[c] for c in range(3)]
                if oy:
                    gap[1] = gap[1] + 2.0 * oy
                if oz:
                    gap[2] = gap[2] + 2.0 * oz
                for ox in steps:
                    first = gap[0] + 2.0 * ox if ox else gap[0]
                    apart = [first, gap[1], gap[2]]
                    distance = jnp.sqrt(
                        apart[0] * apart[0] + apart[1] * apart[1] + apart[2] * apart[2]
                    )
                    scale = 1.0 / jnp.maximum(distance, distance_floor)
                    normal = [apart[c] * scale for c in range(3)]
                    depth = jnp.maximum(a_radius + b_radius - distance, 0.0)
                    strength = a_radius * b_radius * depth
                    swing = cross(turning, normal)
                    relative = [slip[c] + swing[c] for c in range(3)]
                    along = (
                        relative[0] * normal[0]
                        + relative[1] * normal[1]
                        + relative[2] * normal[2]
                    )
                    factor = 1.0 + along
                    pushed = [strength * (factor * normal[c] + relative[c]) for c in range(3)]
                    twisted = cross(normal, pushed)
                    push = [push[c] - pushed[c] for c in range(3)]
                    twist = [twist[c] - twisted[c] for c in range(3)]
    contact = push + [a_radius * twist[c] for c in range(3)]
    contact = [value + roll(value, -2, 0) for value in contact]

    even = (2 * lane8) % 128
    for f in range(6):
        for s in range(2):
            value = jnp.where(masks[0][s][:, :256], hydro[0][f], 0.0) + jnp.where(
                masks[1][s][:, :256], hydro[1][f], 0.0
            )
            value = value + roll(value, -1, 0)
            value = value + roll(value, -1, 1)
            value = jnp.where(
                lane8 < 64, pick_lanes(value[:, :128], even), pick_lanes(value[:, 128:], even)
            )
            both = jnp.concatenate([value[2:3], value[4:5]], axis=0)
            out_loads[f, s, 0] = both + contact[f][4 * s : 4 * s + 2]


VMEM = pl.BlockSpec(memory_space=pltpu.VMEM)
SMEM = pl.BlockSpec(memory_space=pltpu.SMEM)
PARAMS = pltpu.CompilerParams(vmem_limit_bytes=32 * 2**20)


def call(kernel, flags, operands, shapes, scratch=(), aliases=None):
    return pl.pallas_call(
        kernel,
        out_shape=[jax.ShapeDtypeStruct(shape, F32) for shape in shapes],
        in_specs=[SMEM] + [VMEM] * len(operands),
        out_specs=[VMEM] * len(shapes),
        scratch_shapes=[pltpu.VMEM(shape, F32) for shape in scratch],
        compiler_params=PARAMS,
        input_output_aliases=aliases or {},
    )(flags, *operands)


def step(paired, sizes, *blocks):
    nx, ny, nz = sizes
    axes = ("gx", "gy", "gz")

    def permute(value, target):
        pairs = []
        for x in range(nx):
            for y in range(ny):
                for z in range(nz):
                    tx, ty, tz = target(x, y, z)
                    there = ((tx % nx) * ny + ty % ny) * nz + tz % nz
                    pairs.append(((x * ny + y) * nz + z, there))
        return lax.ppermute(value, axes, pairs)

    def swap(value):
        return permute(value, lambda x, y, z: (1 - x, y, z))

    one, zero = jnp.int32(1), jnp.int32(0)
    if paired:
        groups = 2
        ix, iy, iz = [lax.axis_index(axis) for axis in axes]
        flags = jnp.stack([1 - (ix + iy) % 2, 1 - (ix + iz) % 2]).astype(jnp.int32)
        operands = list(blocks) + [swap(block) for block in blocks]
    else:
        groups = 3
        operands = list(blocks)
        operands += [permute(block, lambda x, y, z: (x - 1, y, z)) for block in blocks]
        operands += [permute(block, lambda x, y, z: (x + 1, y, z)) for block in blocks]
    z_shape = (groups, 8, 128)
    y_shape = (Y_BLOCKS, 4 * groups, 128)
    corner_shape = (2, 4 * groups, 128)

    def pack_z(flags):
        return call(functools.partial(z_pack_kernel, groups), flags, operands, [z_shape])[0]

    def pack_y(flags):
        return call(functools.partial(y_pack_kernel, groups), flags, operands, [y_shape])[0]

    def corners(flags, side, ends, rows):
        return pl.pallas_call(
            functools.partial(corner_kernel, groups, paired),
            out_shape=jax.ShapeDtypeStruct(y_shape, F32),
            in_specs=[SMEM, VMEM, VMEM, pl.BlockSpec(memory_space=pl.ANY)],
            out_specs=pl.BlockSpec(
                corner_shape, lambda i: (Y_CORNER // 2, 0, 0), memory_space=pltpu.VMEM
            ),
            grid=(1,),
            scratch_shapes=[pltpu.VMEM((2,) + z_shape, F32)],
            compiler_params=PARAMS,
            input_output_aliases={3: 0},
        )(flags, ends[0], ends[1], rows)

    if paired:
        first = permute(
            pack_z(flags), lambda x, y, z: (x, y, z + (1 if (x + z) % 2 == 0 else -1))
        )
        ends = [first, swap(first)]
        rows = corners(flags, None, ends, pack_y(flags))
        first = permute(rows, lambda x, y, z: (x, y + (1 if (x + y) % 2 == 0 else -1), z))
        halos = [first, swap(first)]
    else:
        flags = jnp.ones((2,), jnp.int32)
        low = jnp.zeros((2,), jnp.int32)
        ends = [
            permute(pack_z(low), lambda x, y, z: (x, y, z - 1)),
            permute(pack_z(flags), lambda x, y, z: (x, y, z + 1)),
        ]
        down = corners(jnp.array([0, 1], jnp.int32), None, ends, pack_y(low))
        up = corners(flags, None, ends, pack_y(flags))
        halos = [
            permute(down, lambda x, y, z: (x, y - 1, z)),
            permute(up, lambda x, y, z: (x, y + 1, z)),
        ]
    scratch = [
        (2,) + z_shape,
        (2,) + y_shape,
        (2, 2 * groups, 8, 128),
        (36, 2 * groups, 8, 384),
        (4, 4, 8, 384),
        (19, 4, 8, 384),
        (3, 4, 8, 384),
    ]
    populations, offset = blocks[0], blocks[2]
    shapes = [populations.shape, (6,) + offset.shape[1:]]
    return tuple(
        call(
            functools.partial(main_kernel, groups, paired),
            flags,
            operands + ends + halos,
            shapes,
            scratch,
        )
    )


def solution(mesh, paired=None):
    sizes = tuple(mesh.shape[axis] for axis in ("gx", "gy", "gz"))
    if paired is None:
        paired = sizes[0] == 2 and sizes[1] % 2 == 0 and sizes[2] % 2 == 0
    cells, bins = P(None, "gx", "gy", "gz"), P(None, None, "gx", "gy", "gz")
    return jax.shard_map(
        functools.partial(step, paired, sizes),
        mesh=mesh,
        in_specs=(cells, cells, bins, cells, bins, bins, bins),
        out_specs=(cells, bins),
        check_vma=False,
    )
```

time: 101 us -> 27.1 us (0.27)
  local copies, waits for them, and re-layouts: 30.3 us -> 2.64 us
  waiting for transfers between devices: 29.4 us -> 7.16 us
  other arithmetic: 16.1 us -> 0.07 us
  starting transfers between devices: 21.7 us -> 9.33 us
  Pallas kernels: 0 us -> 7 us
  between operations: 2.67 us -> 0.68 us
    ppermute x18 -> x11, waiting for transfers between devices: 29.4 us -> 7.16 us  [permute(): return lax.ppermute(value, axes, pairs)]
    ppermute x18 -> x11, starting transfers between devices: 21.7 us -> 9.33 us  [permute(): return lax.ppermute(value, axes, pairs)]
    mul x29 -> x0, local copies, waits for them, and re-layouts: 9.66 us -> none  [the longest x27 7.99 us: deposit_term(): return jnp.concatenate([weight_cells, weight_cells * moving])]
    reshape x27 -> x0, local copies, waits for them, and re-layouts: 8.06 us -> none  [place_cells(): return spreading.reshape(channels, 2 * bins_x, 2 * bins_y, 2 * bins_z)]
    pallas_call x0 -> x4, Pallas kernels: none -> 7 us  [the longest x3 6.45 us: call(): pl.pallas_call(kernel, out_shape=[jax.ShapeDtypeStruct(shape, F32) for sh...]
    transpose x28 -> x0, local copies, waits for them, and re-layouts: 6.51 us -> none  [the longest x27 6.03 us: place_cells(): spreading.reshape(channels, 2, 2, 2, bins_x, bins_y, bins_z)]
    add x8 -> x0, other arithmetic: 3.12 us -> none  [the longest x1 1.13 us: body(): extended + jnp.pad(deposit, ((0, 0), (1 + offset[0], 1 - offset[0]), (1 +...]
    mul x74 -> x0, other arithmetic: 3.1 us -> none  [the longest x1 0.73 us: place_cells(): spreading = jnp.sum(values[:, :, None] * slot_onehot[None], axis=1)]
  transfers between devices with their start and end apart: 18 -> 11, of which waited for: 10 -> 7; matrix products, arithmetic and copies ran while one was open for 39% -> 0% of each run, Pallas kernels for 0% -> 3%
where the time goes in v1:
time: 27.1 us; the launch traced here: 26.9 us
  starting transfers between devices  9.33 us (34%)
  waiting for transfers between devices  7.16 us (26%)
  Pallas kernels  7 us (26%)
  local copies, waits for them, and re-layouts  2.64 us (10%)
  between operations  0.68 us (3%)
    ppermute x11, starting transfers between devices, permute(): return lax.ppermute(value, axes, pairs)  9.33 us
    ppermute x11, waiting for transfers between devices, permute(): return lax.ppermute(value, axes, pairs)  7.16 us
    pallas_call x3, Pallas kernels, call(): pl.pallas_call(kernel, out_shape=[jax.ShapeDtypeStruct(shape, F32) for sh...  6.45 us
    unnamed x18, local copies, waits for them, and re-layouts  2.64 us
    pallas_call x1, Pallas kernels, corners(): pl.pallas_call(functools.partial(corner_kernel, groups, paired), out_shap...  0.56 us
  transfers between devices with their start and end apart: 11, of which 7 were waited for; matrix products, arithmetic and copies ran while one was open for 0% of the time, Pallas kernels for 3%

profile of v1, /device:TPU:0, one launch (start us, length us, event | category | flops | bytes accessed | tf_op | source)
XLA Modules:
  0.0 26.9 jit_solution(4281159270026627694)
XLA Ops:
  0.6 0.5 %collective-permute-start = (f32[19,2,4,256]{3,2,1,0:T(4,128)}, f32[19,2,4,256]{3,2,1,0:T(4,128)S(1)}, u32[]{:S(2)}, u32[]{:S(2)}) collective-permute-start(f32[19,2,4,256]{3,2,1,0:T(4,128)} %refs_0_.5), channel_id=1, source_target_pairs={{0,16},{1,17},{2,18},{3,19},{4,20},{5,21},{6,22},{7,23},{8,24},{9,... | collective-permute-start | bytes 466952 | tf_op jit(solution)/shard_map/ppermute | solution.py:545
  1.2 0.4 %collective-permute-start.3 = (f32[2,1,2,128]{3,2,1,0:T(2,128)}, f32[2,1,2,128]{3,2,1,0:T(2,128)S(1)}, u32[]{:S(2)}, u32[]{:S(2)}) collective-permute-start(f32[2,1,2,128]{3,2,1,0:T(2,128)} %refs_3_.5), channel_id=1, source_target_pairs={{0,16},{1,17},{2,18},{3,19},{4,20},{5,21},{6,22},{7,23},{8,24},{9,... | collective-permute-start | bytes 6152 | tf_op jit(solution)/shard_map/ppermute | solution.py:545
  1.7 0.1 collective-permute-start.2
  1.8 0.4 %collective-permute-start.4 = (f32[3,2,1,2,128]{4,3,2,1,0:T(2,128)}, f32[3,2,1,2,128]{4,3,2,1,0:T(2,128)S(1)}, u32[]{:S(2)}, u32[]{:S(2)}) collective-permute-start(f32[3,2,1,2,128]{4,3,2,1,0:T(2,128)} %refs_4_.5), channel_id=1, source_target_pairs={{0,16},{1,17},{2,18},{3,19},{4,20},{5,21},{6,22},{7,23},{8,24},{9,... | collective-permute-start | bytes 18440 | tf_op jit(solution)/shard_map/ppermute | solution.py:545
  2.2 0.3 %collective-permute-done.1.refs_8_ = s32[2,1,2,128]{3,2,1,0:T(2,128)S(1)} collective-permute-done((s32[2,1,2,128]{3,2,1,0:T(2,128)}, s32[2,1,2,128]{3,2,1,0:T(2,128)S(1)}, u32[]{:S(2)}, u32[]{:S(2)}) %collective-permute-start.1) | collective-permute-done | bytes 2080 | tf_op jit(solution)/shard_map/ppermute | solution.py:545
  2.5 0.3 %copy-done.5 = f32[3,2,1,2,128]{4,3,2,1,0:T(2,128)S(1)} copy-done((f32[3,2,1,2,128]{4,3,2,1,0:T(2,128)S(1)}, f32[3,2,1,2,128]{4,3,2,1,0:T(2,128)}, u32[]{:S(2)}) %copy-start.5) | copy-done | bytes 6168
  3.0 0.4 %collective-permute-start.6 = (f32[27,2,1,2,128]{4,3,2,1,0:T(2,128)S(1)}, f32[27,2,1,2,128]{4,3,2,1,0:T(2,128)S(1)}, u32[]{:S(2)}, u32[]{:S(2)}) collective-permute-start(f32[27,2,1,2,128]{4,3,2,1,0:T(2,128)S(1)} %copy-done.2), channel_id=1, source_target_pairs={{0,16},{1,17},{2,18},{3,19},{4,20},{5,21},{6,22},{7,23},{8,24},{9,... | collective-permute-start | bytes 165896 | tf_op jit(solution)/shard_map/ppermute | solution.py:545
  3.5 0.6 %collective-permute-done.5.refs_12_ = f32[3,2,1,2,128]{4,3,2,1,0:T(2,128)S(1)} collective-permute-done((f32[3,2,1,2,128]{4,3,2,1,0:T(2,128)S(1)}, f32[3,2,1,2,128]{4,3,2,1,0:T(2,128)S(1)}, u32[]{:S(2)}, u32[]{:S(2)}) %collective-permute-start.5) | collective-permute-done | bytes 6176 | tf_op jit(solution)/shard_map/ppermute | solution.py:545
  4.0 0.2 collective-permute-done.6.refs_13_
  4.3 0.9 %copy-done = f32[19,2,4,256]{3,2,1,0:T(4,128)S(1)} copy-done((f32[19,2,4,256]{3,2,1,0:T(4,128)S(1)}, f32[19,2,4,256]{3,2,1,0:T(4,128)}, u32[]{:S(2)}) %copy-start) | copy-done | bytes 155672
  5.2 0.7 %copy-done.6 = s32[2,1,2,128]{3,2,1,0:T(2,128)S(1)} copy-done((s32[2,1,2,128]{3,2,1,0:T(2,128)S(1)}, s32[2,1,2,128]{3,2,1,0:T(2,128)}, u32[]{:S(2)}) %copy-start.6) | copy-done | bytes 2072
  5.9 0.7 %copy-done.8 = f32[2,1,2,128]{3,2,1,0:T(2,128)S(1)} copy-done((f32[2,1,2,128]{3,2,1,0:T(2,128)S(1)}, f32[2,1,2,128]{3,2,1,0:T(2,128)}, u32[]{:S(2)}) %copy-start.8) | copy-done | bytes 2072
  6.6 0.9 %shard_map.86 = f32[2,8,128]{2,1,0:T(8,128)S(1)} custom-call(s32[2]{0:T(128)S(1)} %pad_add_fusion.flags, f32[19,2,4,256]{3,2,1,0:T(4,128)S(1)} %copy-done, s32[2,1,2,128]{3,2,1,0:T(2,128)S(1)} %copy-done.6, f32[3,2,1,2,128]{4,3,2,1,0:T(2,128)S(1)} %copy-done.3, f32[2,1,2,128]{3,2,1,0:T(2,128)S(1)} %copy-done.8, f32[3,2,1,2,128]{4,3,2,1,0:T(2,128)S(1)} %copy-done.4, ...), custom_call_target="tpu_custom_call" | custom-call | tf_op jit(solution)/shard_map/pallas_call | solution.py:522
  7.4 2.9 %collective-permute-start.7 = (f32[2,8,128]{2,1,0:T(8,128)S(1)}, f32[2,8,128]{2,1,0:T(8,128)S(1)}, u32[]{:S(2)}, u32[]{:S(2)}) collective-permute-start(f32[2,8,128]{2,1,0:T(8,128)S(1)} %shard_map.86), channel_id=1, source_target_pairs={{0,1},{1,0},{2,3},{3,2},{4,5},{5,4},{6,7},{7,6},{8,9},{9,8},{10,11... | collective-permute-start | bytes 24584 | tf_op jit(solution)/shard_map/ppermute | solution.py:545
  10.3 1.6 %collective-permute-done.7.first.refs_14_ = f32[2,8,128]{2,1,0:T(8,128)S(1)} collective-permute-done((f32[2,8,128]{2,1,0:T(8,128)S(1)}, f32[2,8,128]{2,1,0:T(8,128)S(1)}, u32[]{:S(2)}, u32[]{:S(2)}) %collective-permute-start.7) | collective-permute-done | bytes 8224 | tf_op jit(solution)/shard_map/ppermute | solution.py:545
  12.0 0.2 collective-permute-start.8
  12.2 0.7 %shard_map.87.rows = f32[36,8,128]{2,1,0:T(8,128)S(1)} custom-call(s32[2]{0:T(128)S(1)} %pad_add_fusion.flags, f32[19,2,4,256]{3,2,1,0:T(4,128)S(1)} %copy-done, s32[2,1,2,128]{3,2,1,0:T(2,128)S(1)} %copy-done.7, f32[3,2,1,2,128]{4,3,2,1,0:T(2,128)S(1)} %copy-done.3, f32[2,1,2,128]{3,2,1,0:T(2,128)S(1)} %copy-done.8, f32[3,2,1,2,128]{4,3,2,1,0:T(2,128)S(1)} %copy-done.4, ...), custom_call_target="tpu_custom_call" | custom-call | tf_op jit(solution)/shard_map/pallas_call | solution.py:522
  12.9 0.2 collective-permute-done.8.second.refs_15_
  13.2 0.6 %shard_map.88 = f32[36,8,128]{2,1,0:T(8,128)S(1)} custom-call(s32[2]{0:T(128)S(1)} %pad_add_fusion.flags, f32[2,8,128]{2,1,0:T(8,128)S(1)} %collective-permute-done.7.first.refs_14_, f32[2,8,128]{2,1,0:T(8,128)S(1)} %collective-permute-done.8.second.refs_15_, f32[36,8,128]{2,1,0:T(8,128)S(1)} %shard_map.87.rows), custom_call_target="tpu_custom_call", output_to_operand_aliasing={{}: (3, {})} | custom-call | tf_op jit(solution)/shard_map/pallas_call | solution.py:572
  13.7 2.2 %collective-permute-start.9 = (f32[36,8,128]{2,1,0:T(8,128)S(1)}, f32[36,8,128]{2,1,0:T(8,128)S(1)}, u32[]{:S(2)}, u32[]{:S(2)}) collective-permute-start(f32[36,8,128]{2,1,0:T(8,128)S(1)} %shard_map.88), channel_id=1, source_target_pairs={{0,4},{1,5},{2,6},{3,7},{4,0},{5,1},{6,2},{7,3},{8,12},{9,13},{10,... | collective-permute-start | bytes 442376 | tf_op jit(solution)/shard_map/ppermute | solution.py:545
  15.9 3.1 %collective-permute-done.9.refs_16_ = f32[36,8,128]{2,1,0:T(8,128)S(1)} collective-permute-done((f32[36,8,128]{2,1,0:T(8,128)S(1)}, f32[36,8,128]{2,1,0:T(8,128)S(1)}, u32[]{:S(2)}, u32[]{:S(2)}) %collective-permute-start.9) | collective-permute-done | bytes 147488 | tf_op jit(solution)/shard_map/ppermute | solution.py:545
  19.0 2.0 %collective-permute-start.10 = (f32[36,8,128]{2,1,0:T(8,128)S(1)}, f32[36,8,128]{2,1,0:T(8,128)S(1)}, u32[]{:S(2)}, u32[]{:S(2)}) collective-permute-start(f32[36,8,128]{2,1,0:T(8,128)S(1)} %collective-permute-done.9.refs_16_), channel_id=1, source_target_pairs={{0,16},{1,17},{2,18},{3,19},{4,20},{5,21},{6,22},{7,23},{8,24},{9,... | collective-permute-start | bytes 442376 | tf_op jit(solution)/shard_map/ppermute | solution.py:545
  21.0 1.0 %collective-permute-done.10.refs_17_ = f32[36,8,128]{2,1,0:T(8,128)S(1)} collective-permute-done((f32[36,8,128]{2,1,0:T(8,128)S(1)}, f32[36,8,128]{2,1,0:T(8,128)S(1)}, u32[]{:S(2)}, u32[]{:S(2)}) %collective-permute-start.10) | collective-permute-done | bytes 147488 | tf_op jit(solution)/shard_map/ppermute | solution.py:545
  22.0 4.9 %shard_map.89 = (f32[19,2,4,256]{3,2,1,0:T(4,128)}, f32[6,2,1,2,128]{4,3,2,1,0:T(2,128)}) custom-call(s32[2]{0:T(128)S(1)} %pad_add_fusion.flags, f32[19,2,4,256]{3,2,1,0:T(4,128)S(1)} %copy-done.1, s32[2,1,2,128]{3,2,1,0:T(2,128)S(1)} %copy-done.7, f32[3,2,1,2,128]{4,3,2,1,0:T(2,128)S(1)} %copy-done.3, f32[2,1,2,128]{3,2,1,0:T(2,128)S(1)} %copy-done.8, ...), custom_call_target="tpu_custom_call" | custom-call | tf_op jit(solution)/shard_map/pallas_call | solution.py:522
  (21 shorter events, 0.3 us)
Async XLA Ops:
  0.6 2.3 %copy-start.2 = (f32[27,2,1,2,128]{4,3,2,1,0:T(2,128)S(1)}, f32[27,2,1,2,128]{4,3,2,1,0:T(2,128)}, u32[]{:S(2)}) copy-start(f32[27,2,1,2,128]{4,3,2,1,0:T(2,128)} %refs_6_.5) | copy-start | bytes 165892
  0.6 3.6 %collective-permute-start = (f32[19,2,4,256]{3,2,1,0:T(4,128)}, f32[19,2,4,256]{3,2,1,0:T(4,128)S(1)}, u32[]{:S(2)}, u32[]{:S(2)}) collective-permute-start(f32[19,2,4,256]{3,2,1,0:T(4,128)} %refs_0_.5), channel_id=1, source_target_pairs={{0,16},{1,17},{2,18},{3,19},{4,20},{5,21},{6,22},{7,23},{8,24},{9,... | collective-permute-start | bytes 466952 | tf_op jit(solution)/shard_map/ppermute | solution.py:545
  1.2 1.4 %collective-permute-start.1 = (s32[2,1,2,128]{3,2,1,0:T(2,128)}, s32[2,1,2,128]{3,2,1,0:T(2,128)S(1)}, u32[]{:S(2)}, u32[]{:S(2)}) collective-permute-start(s32[2,1,2,128]{3,2,1,0:T(2,128)} %refs_1_.5), channel_id=1, source_target_pairs={{0,16},{1,17},{2,18},{3,19},{4,20},{5,21},{6,22},{7,23},{8,24},{9,... | collective-permute-start | bytes 6152 | tf_op jit(solution)/shard_map/ppermute | solution.py:545
  1.2 1.7 %collective-permute-start.3 = (f32[2,1,2,128]{3,2,1,0:T(2,128)}, f32[2,1,2,128]{3,2,1,0:T(2,128)S(1)}, u32[]{:S(2)}, u32[]{:S(2)}) collective-permute-start(f32[2,1,2,128]{3,2,1,0:T(2,128)} %refs_3_.5), channel_id=1, source_target_pairs={{0,16},{1,17},{2,18},{3,19},{4,20},{5,21},{6,22},{7,23},{8,24},{9,... | collective-permute-start | bytes 6152 | tf_op jit(solution)/shard_map/ppermute | solution.py:545
  1.7 1.8 %collective-permute-start.2 = (f32[3,2,1,2,128]{4,3,2,1,0:T(2,128)}, f32[3,2,1,2,128]{4,3,2,1,0:T(2,128)S(1)}, u32[]{:S(2)}, u32[]{:S(2)}) collective-permute-start(f32[3,2,1,2,128]{4,3,2,1,0:T(2,128)} %refs_2_.5), channel_id=1, source_target_pairs={{0,16},{1,17},{2,18},{3,19},{4,20},{5,21},{6,22},{7,23},{8,24},{9,... | collective-permute-start | bytes 18440 | tf_op jit(solution)/shard_map/ppermute | solution.py:545
  1.8 1.7 %collective-permute-start.4 = (f32[3,2,1,2,128]{4,3,2,1,0:T(2,128)}, f32[3,2,1,2,128]{4,3,2,1,0:T(2,128)S(1)}, u32[]{:S(2)}, u32[]{:S(2)}) collective-permute-start(f32[3,2,1,2,128]{4,3,2,1,0:T(2,128)} %refs_4_.5), channel_id=1, source_target_pairs={{0,16},{1,17},{2,18},{3,19},{4,20},{5,21},{6,22},{7,23},{8,24},{9,... | collective-permute-start | bytes 18440 | tf_op jit(solution)/shard_map/ppermute | solution.py:545
  2.2 0.7 %copy-start.5 = (f32[3,2,1,2,128]{4,3,2,1,0:T(2,128)S(1)}, f32[3,2,1,2,128]{4,3,2,1,0:T(2,128)}, u32[]{:S(2)}) copy-start(f32[3,2,1,2,128]{4,3,2,1,0:T(2,128)} %refs_5_.5) | copy-start | bytes 18436
  2.2 2.1 %copy-start.4 = (f32[3,2,1,2,128]{4,3,2,1,0:T(2,128)S(1)}, f32[3,2,1,2,128]{4,3,2,1,0:T(2,128)}, u32[]{:S(2)}) copy-start(f32[3,2,1,2,128]{4,3,2,1,0:T(2,128)} %refs_4_.5) | copy-start | bytes 18436
  2.2 2.1 %copy-start.3 = (f32[3,2,1,2,128]{4,3,2,1,0:T(2,128)S(1)}, f32[3,2,1,2,128]{4,3,2,1,0:T(2,128)}, u32[]{:S(2)}) copy-start(f32[3,2,1,2,128]{4,3,2,1,0:T(2,128)} %refs_2_.5) | copy-start | bytes 18436
  2.9 1.2 %collective-permute-start.5 = (f32[3,2,1,2,128]{4,3,2,1,0:T(2,128)S(1)}, f32[3,2,1,2,128]{4,3,2,1,0:T(2,128)S(1)}, u32[]{:S(2)}, u32[]{:S(2)}) collective-permute-start(f32[3,2,1,2,128]{4,3,2,1,0:T(2,128)S(1)} %copy-done.5), channel_id=1, source_target_pairs={{0,16},{1,17},{2,18},{3,19},{4,20},{5,21},{6,22},{7,23},{8,24},{9,... | collective-permute-start | bytes 18440 | tf_op jit(solution)/shard_map/ppermute | solution.py:545
  3.0 1.3 %collective-permute-start.6 = (f32[27,2,1,2,128]{4,3,2,1,0:T(2,128)S(1)}, f32[27,2,1,2,128]{4,3,2,1,0:T(2,128)S(1)}, u32[]{:S(2)}, u32[]{:S(2)}) collective-permute-start(f32[27,2,1,2,128]{4,3,2,1,0:T(2,128)S(1)} %copy-done.2), channel_id=1, source_target_pairs={{0,16},{1,17},{2,18},{3,19},{4,20},{5,21},{6,22},{7,23},{8,24},{9,... | collective-permute-start | bytes 165896 | tf_op jit(solution)/shard_map/ppermute | solution.py:545
  4.3 0.9 %copy-start = (f32[19,2,4,256]{3,2,1,0:T(4,128)S(1)}, f32[19,2,4,256]{3,2,1,0:T(4,128)}, u32[]{:S(2)}) copy-start(f32[19,2,4,256]{3,2,1,0:T(4,128)} %refs_0_.5) | copy-start | bytes 466948
  5.2 0.7 %copy-start.6 = (s32[2,1,2,128]{3,2,1,0:T(2,128)S(1)}, s32[2,1,2,128]{3,2,1,0:T(2,128)}, u32[]{:S(2)}) copy-start(s32[2,1,2,128]{3,2,1,0:T(2,128)} %refs_1_.5) | copy-start | bytes 6148
  5.9 0.7 %copy-start.8 = (f32[2,1,2,128]{3,2,1,0:T(2,128)S(1)}, f32[2,1,2,128]{3,2,1,0:T(2,128)}, u32[]{:S(2)}) copy-start(f32[2,1,2,128]{3,2,1,0:T(2,128)} %refs_3_.5) | copy-start | bytes 6148
  6.6 5.7 %copy-start.7 = (s32[2,1,2,128]{3,2,1,0:T(2,128)S(1)}, s32[2,1,2,128]{3,2,1,0:T(2,128)}, u32[]{:S(2)}) copy-start(s32[2,1,2,128]{3,2,1,0:T(2,128)} %refs_1_.5) | copy-start | bytes 6148
  7.4 4.5 %collective-permute-start.7 = (f32[2,8,128]{2,1,0:T(8,128)S(1)}, f32[2,8,128]{2,1,0:T(8,128)S(1)}, u32[]{:S(2)}, u32[]{:S(2)}) collective-permute-start(f32[2,8,128]{2,1,0:T(8,128)S(1)} %shard_map.86), channel_id=1, source_target_pairs={{0,1},{1,0},{2,3},{3,2},{4,5},{5,4},{6,7},{7,6},{8,9},{9,8},{10,11... | collective-permute-start | bytes 24584 | tf_op jit(solution)/shard_map/ppermute | solution.py:545
  12.0 1.2 %collective-permute-start.8 = (f32[2,8,128]{2,1,0:T(8,128)S(1)}, f32[2,8,128]{2,1,0:T(8,128)S(1)}, u32[]{:S(2)}, u32[]{:S(2)}) collective-permute-start(f32[2,8,128]{2,1,0:T(8,128)S(1)} %collective-permute-done.7.first.refs_14_), channel_id=1, source_target_pairs={{0,16},{1,17},{2,18},{3,19},{4,20},{5,21},{6,22},{7,23},{8,24},{9,... | collective-permute-start | bytes 24584 | tf_op jit(solution)/shard_map/ppermute | solution.py:545
  12.9 9.1 %copy-start.1 = (f32[19,2,4,256]{3,2,1,0:T(4,128)S(1)}, f32[19,2,4,256]{3,2,1,0:T(4,128)}, u32[]{:S(2)}) copy-start(f32[19,2,4,256]{3,2,1,0:T(4,128)} %refs_0_.5) | copy-start | bytes 466948
  13.7 5.3 %collective-permute-start.9 = (f32[36,8,128]{2,1,0:T(8,128)S(1)}, f32[36,8,128]{2,1,0:T(8,128)S(1)}, u32[]{:S(2)}, u32[]{:S(2)}) collective-permute-start(f32[36,8,128]{2,1,0:T(8,128)S(1)} %shard_map.88), channel_id=1, source_target_pairs={{0,4},{1,5},{2,6},{3,7},{4,0},{5,1},{6,2},{7,3},{8,12},{9,13},{10,... | collective-permute-start | bytes 442376 | tf_op jit(solution)/shard_map/ppermute | solution.py:545
  19.0 3.0 %collective-permute-start.10 = (f32[36,8,128]{2,1,0:T(8,128)S(1)}, f32[36,8,128]{2,1,0:T(8,128)S(1)}, u32[]{:S(2)}, u32[]{:S(2)}) collective-permute-start(f32[36,8,128]{2,1,0:T(8,128)S(1)} %collective-permute-done.9.refs_16_), channel_id=1, source_target_pairs={{0,16},{1,17},{2,18},{3,19},{4,20},{5,21},{6,22},{7,23},{8,24},{9,... | collective-permute-start | bytes 442376 | tf_op jit(solution)/shard_map/ppermute | solution.py:545

commit v2 on v1

--- a/solution.py
+++ b/solution.py
@@ -36,7 +36,8 @@
 E0, RADIUS, CODE, PLACE = 9, 36, 37, 38
 POPS_LANE, SLOT_LANE = 41, 64
 Y_FIELDS = list(range(9)) + [RADIUS, CODE]
-Y_GRAIN, Y_CORNER, Y_BLOCKS = 19, 34, 36
+Y_GRAIN, Y_BLOCKS = 76, 17
+W_GRAIN, W_BLOCKS = 38, 57
 F32 = jnp.float32
 
 
@@ -61,99 +62,138 @@
     ]
 
 
-class Group:
-    def __init__(self, refs):
-        self.pops, self.cell, self.off, self.rad, self.vel, self.spin, self.inter = refs
-
-    def slot(self, s, field):
+def pack_kernel(flags, *refs):
+    sources, (whole, mine, theirs), held, sems = refs[:7], refs[7:10], refs[10:17], refs[17]
+    copies = [
+        pltpu.make_async_copy(source, target, sems.at[n])
+        for n, (source, target) in enumerate(zip(sources, held))
+    ]
+    for copy in copies[1:] + copies[:1]:
+        copy.start()
+    pops, cell, off, rad, vel, spin, inter = held
+    for copy in copies[1:]:
+        copy.wait()
+
+    def slot(s, field):
         if field < 3:
-            return self.vel[field, s, 0]
+            return vel[field, s, 0]
         if field < 6:
-            return self.spin[field - 3, s, 0]
+            return spin[field - 3, s, 0]
         if field < 9:
-            return self.off[field - 6, s, 0]
+            return off[field - 6, s, 0]
         if field < RADIUS:
-            return self.inter[field - E0, s, 0]
+            return inter[field - E0, s, 0]
         if field == RADIUS:
-            return self.rad[s, 0]
-        return self.cell[s, 0].astype(F32)
-
-    def place(self, s):
-        code = self.cell[s, 0]
-        corner = [code >> 2, (code >> 1) & 1, code & 1]
-        return [corner[c].astype(F32) + self.off[c, s, 0] for c in range(3)]
-
-
-def split_groups(refs, groups):
-    return [Group(refs[7 * g : 7 * g + 7]) for g in range(groups)]
-
-
-def z_pack_kernel(groups, flags, *refs):
-    out = refs[-1]
-    high = flags[1] == 1
-    lane = iota((4, 128), 1)
-    index4 = jnp.where(high, jnp.full((4, 128), 127, jnp.int32), jnp.zeros((4, 128), jnp.int32))
-    index2 = jnp.where(high, jnp.full((2, 128), 127, jnp.int32), jnp.zeros((2, 128), jnp.int32))
-    lane2 = iota((2, 128), 1)
-    for g, group in enumerate(split_groups(refs, groups)):
-        grain = jnp.zeros((2, 128), F32)
+            return rad[s, 0]
+        return cell[s, 0].astype(F32)
+
+    for field in range(38):
         for s in range(2):
-            values = [group.slot(s, field) for field in range(38)] + group.place(s)
-            for field, value in enumerate(values):
-                grain = jnp.where(lane2 == SLOT_LANE * s + field, pick_lanes(value, index2), grain)
-        both = jnp.concatenate([grain[0:1], grain[0:1], grain[1:2], grain[1:2]], axis=0)
-        for i in range(2):
-            rows = both
-            for member in range(19):
-                value = group.pops[member, i]
-                last = value.shape[1] - 128
-                tile = jnp.where(high, value[:, last:], value[:, :128])
-                rows = jnp.where(lane == POPS_LANE + member, pick_lanes(tile, index4), rows)
-            out[g, 4 * i : 4 * i + 4, :] = rows
-
-
-def y_pack_kernel(groups, flags, *refs):
-    out = refs[-1]
-    high = flags[0] == 1
-    for g, group in enumerate(split_groups(refs, groups)):
-        for member in range(19):
-            for i in range(2):
-                row = jnp.where(high, group.pops[member, i, 3:4], group.pops[member, i, 0:1])
-                for t in range(2):
-                    at = 4 * g + 2 * i + t
-                    out[member, at : at + 1, :] = row[:, 128 * t : 128 * t + 128]
+            at = 4 * (field % 2) + 2 * s
+            whole[W_GRAIN + field // 2, at : at + 2, :] = slot(s, field)
+    for out, end in ((mine.at[0], flags[0]), (theirs, 1 - flags[0])):
+        high = end == 1
         for s in range(2):
             for f in range(29):
                 if f < 11:
-                    value = group.slot(s, Y_FIELDS[f])
+                    value = slot(s, Y_FIELDS[f])
                 else:
                     kx, q, kz = (f - 11) // 6, (f - 11) // 3 % 2, (f - 11) % 3
-                    value = group.inter[9 * kx + 3 * (q + flags[0]) + kz, s, 0]
-                q = 2 * f + s
-                at = 4 * g + q % 4
-                out[Y_GRAIN + q // 4, at : at + 1, :] = jnp.where(high, value[1:2], value[0:1])
-    out[Y_GRAIN + 14, :, :] = jnp.where(
-        iota((4 * groups, 128), 0) % 4 >= 2, 0.0, out[Y_GRAIN + 14, :, :]
-    )
-    out[Y_CORNER:Y_BLOCKS, :, :] = jnp.zeros((2, 4 * groups, 128), F32)
-
-
-def store_z(groups, paired, flags, first, second, held):
-    side = flags[1]
+                    value = inter[9 * kx + 3 * (q + end) + kz, s, 0]
+                r = Y_GRAIN + 2 * f + s
+                out[r // 8, r % 8 : r % 8 + 1, :] = jnp.where(high, value[1:2], value[0:1])
+        out[16, 6:8, :] = jnp.zeros((2, 128), F32)
+    copies[0].wait()
+    for member in range(19):
+        for i in range(2):
+            value = pops[member, i]
+            for t in range(2):
+                tile = value[:, 128 * t : 128 * t + 128]
+                whole[2 * member + i, 4 * t : 4 * t + 4, :] = tile
+                r = 4 * member + 2 * i + t
+                first, last = tile[0:1], tile[3:4]
+                high = flags[0] == 1
+                mine[0, r // 8, r % 8 : r % 8 + 1, :] = jnp.where(high, last, first)
+                theirs[r // 8, r % 8 : r % 8 + 1, :] = jnp.where(high, first, last)
+
+
+class Block:
+    def __init__(self, whole, halos, group):
+        self.whole, self.halos, self.group = whole, halos, group
+
+    def slot(self, s, field):
+        at = 4 * (field % 2) + 2 * s
+        return self.whole[W_GRAIN + field // 2, at : at + 2, :]
+
+    def pops(self, member, i, t):
+        return self.whole[2 * member + i, 4 * t : 4 * t + 4, :]
+
+    def halo_pops(self, end, member, i, t):
+        r = 4 * member + 2 * i + t
+        return self.halos[end, self.group, r // 8, r % 8 : r % 8 + 1, :]
+
+    def halo_slot(self, end, s, field):
+        if field in Y_FIELDS:
+            f = Y_FIELDS.index(field)
+        else:
+            k = field - E0
+            q = k // 3 % 3 - (1 - end)
+            if q not in (0, 1):
+                return jnp.zeros((1, 128), F32)
+            f = 11 + 6 * (k // 9) + 3 * q + k % 3
+        r = Y_GRAIN + 2 * f + s
+        return self.halos[end, self.group, r // 8, r % 8 : r % 8 + 1, :]
+
+    def bins(self, s, field):
+        own = self.slot(s, field)
+        row = iota((8, 128), 0)
+        low, high = self.halo_slot(0, s, field), self.halo_slot(1, s, field)
+        return jnp.where(
+            row < 4,
+            jnp.where(row < 2, low, own[0:1]),
+            jnp.where(row < 6, own[1:2], high),
+        )
+
+    def cells(self, member, i, t):
+        own = self.pops(member, i, t)
+        low, high = self.halo_pops(0, member, i, t), self.halo_pops(1, member, i, t)
+        return jnp.concatenate([low, low, own, high, high], axis=0)
+
+
+def position(code, offset):
+    first = jnp.floor(code * 0.25)
+    rest = code - 4.0 * first
+    second = jnp.floor(rest * 0.5)
+    corner = [first, second, rest - 2.0 * second]
+    return [corner[c] + offset[c] for c in range(3)]
+
+
+def store_ends(groups, paired, side, first, second, held):
     for g in range(groups):
         held[side, g] = first[g]
         held[1 - side, g] = second[(g + 1) % 2 if paired else g]
 
 
-def corner_kernel(groups, paired, flags, first, second, rows, out, held):
-    store_z(groups, paired, flags, first, second, held)
-    high = flags[0] == 1
-    for side in range(2):
-        for g in range(groups):
-            for i in range(2):
-                value = held[side, g, 4 * i : 4 * i + 4, :]
-                at = 4 * g + 2 * i
-                out[side, at : at + 2, :] = jnp.where(high, value[2:4], value[0:2])
+def z_pack_kernel(groups, paired, flags, *refs):
+    wholes, (first, second, out, held) = refs[:groups], refs[groups:]
+    store_ends(groups, paired, flags[0], first, second, held)
+    high = flags[1] == 1
+    lane = iota((8, 128), 1)
+    index = jnp.where(high, jnp.full((8, 128), 127, jnp.int32), jnp.zeros((8, 128), jnp.int32))
+    for g in range(groups):
+        block = Block(wholes[g], held, g)
+        grain = jnp.zeros((8, 128), F32)
+        for s in range(2):
+            values = [block.bins(s, field) for field in range(38)]
+            values += position(values[CODE], values[6:9])
+            for field, value in enumerate(values):
+                grain = jnp.where(lane == SLOT_LANE * s + field, pick_lanes(value, index), grain)
+        for i in range(2):
+            rows = grain
+            for member in range(19):
+                tile = jnp.where(high, block.cells(member, i, 1), block.cells(member, i, 0))
+                rows = jnp.where(lane == POPS_LANE + member, pick_lanes(tile, index), rows)
+            out[g, i] = rows
 
 
 def equilibrium_parts(velocity):
@@ -176,61 +216,35 @@
 
 def main_kernel(groups, paired, flags, *refs):
     layers = 2 * groups
-    block = split_groups(refs, groups)
-    z_first, z_second, y_first, y_second = refs[7 * groups : 7 * groups + 4]
-    out_pops, out_loads = refs[7 * groups + 4 : 7 * groups + 6]
-    held_z, held_y, edge, placed, solid, passed, share = refs[7 * groups + 6 :]
+    wholes = refs[:groups]
+    y_first, y_second, z_first, z_second = refs[groups : groups + 4]
+    out_pops, out_loads = refs[groups + 4 : groups + 6]
+    held_z, held_y, placed, solid, passed, share = refs[groups + 6 :]
     targets = [0, 1, 2, layers - 1]
 
-    store_z(groups, paired, flags, z_first, z_second, held_z)
-    side = flags[0]
-    held_y[side] = y_first[...]
-    for b in range(Y_BLOCKS):
-        value = y_second[b]
-        held_y[1 - side, b] = roll(value, 4, 0) if paired else value
-    for s in range(2):
-        for layer in range(layers):
-            g, i = layer // 2, layer % 2
-            at = 4 * g + 2 * i
-            edge[s, layer, 2:6, :] = held_z[s, g, 4 * i : 4 * i + 4, :]
-            edge[s, layer, 0:2, :] = held_y[0, Y_CORNER + s, at : at + 2, :]
-            edge[s, layer, 6:8, :] = held_y[1, Y_CORNER + s, at : at + 2, :]
+    store_ends(groups, paired, flags[0], y_first, y_second, held_y)
+    store_ends(groups, paired, flags[1], z_first, z_second, held_z)
+    block = [Block(wholes[g], held_y, g) for g in range(groups)]
+
+    def edge(end, layer):
+        return held_z[end, layer // 2, layer % 2]
 
     row8 = iota((8, 128), 0)
     lane8 = iota((8, 128), 1)
     half = lane8 // 2
 
-    def y_row(end, g, s, field):
-        if field in Y_FIELDS:
-            f = Y_FIELDS.index(field)
-        else:
-            k = field - E0
-            q = k // 3 % 3 - (1 - end)
-            if q not in (0, 1):
-                return jnp.zeros((1, 128), F32)
-            f = 11 + 6 * (k // 9) + 3 * q + k % 3
-        q = 2 * f + s
-        at = 4 * g + q % 4
-        return held_y[end, Y_GRAIN + q // 4, at : at + 1, :]
-
     def column(matrix, at):
         return jnp.broadcast_to(matrix[:, at : at + 1], (8, 128))
 
     def spread(g, s, field):
-        own = block[g].slot(s, field)
-        low, high = y_row(0, g, s, field), y_row(1, g, s, field)
-        rows = jnp.where(
-            row8 < 4,
-            jnp.where(row8 < 2, low, own[0:1]),
-            jnp.where(row8 < 6, own[1:2], high),
-        )
+        rows = block[g].bins(s, field)
         at = SLOT_LANE * s + field
         return jnp.concatenate(
             [
                 pick_lanes(rows, half),
                 pick_lanes(rows, half + 64),
                 jnp.where(
-                    lane8 < 64, column(edge[1, 2 * g], at), column(edge[0, 2 * g], at)
+                    lane8 < 64, column(edge(1, 2 * g), at), column(edge(0, 2 * g), at)
                 ),
             ],
             axis=1,
@@ -296,16 +310,12 @@
             f = []
             for member in range(19):
                 if t < 2:
-                    own = block[g].pops[member, i, :, tile]
-                    at = 4 * g + 2 * i + t
-                    low = held_y[0, member, at : at + 1, :]
-                    high = held_y[1, member, at : at + 1, :]
-                    f.append(jnp.concatenate([low, low, own, high, high], axis=0))
+                    f.append(block[g].cells(member, i, t))
                 else:
                     at = POPS_LANE + member
                     f.append(
                         jnp.where(
-                            lane8 < 64, column(edge[1, target], at), column(edge[0, target], at)
+                            lane8 < 64, column(edge(1, target), at), column(edge(0, target), at)
                         )
                     )
             sums = [solid[c, n, :, tile] for c in range(4)]
@@ -415,13 +425,6 @@
     def rows_own(values):
         return jnp.concatenate([values[0], values[0], values[1], values[1]], axis=0)
 
-    def position(code, offset):
-        first = jnp.floor(code * 0.25)
-        rest = code - 4.0 * first
-        second = jnp.floor(rest * 0.5)
-        corner = [first, second, rest - 2.0 * second]
-        return [corner[c] + offset[c] for c in range(3)]
-
     def own_field(field):
         return rows_own([own.slot(s, field) for s in range(2)])
 
@@ -446,16 +449,16 @@
                 for s in range(2):
                     value = block[g].slot(s, field)
                     if oy < 0:
-                        value = jnp.concatenate([y_row(0, g, s, field), value[0:1]], axis=0)
+                        value = jnp.concatenate([block[g].halo_slot(0, s, field), value[0:1]], axis=0)
                     if oy > 0:
-                        value = jnp.concatenate([value[1:2], y_row(1, g, s, field)], axis=0)
+                        value = jnp.concatenate([value[1:2], block[g].halo_slot(1, s, field)], axis=0)
                     values.append(value)
                 state.append(jnp.concatenate(values + values, axis=0))
             state = position(state[0], state[1:4]) + state[4:]
             for oz in (-1, 0, 1):
                 other = state
                 if oz:
-                    matrix = edge[(oz + 1) // 2, 2 * g]
+                    matrix = edge((oz + 1) // 2, 2 * g)
                     at = 2 * (oy + 1)
                     rows = jnp.concatenate([matrix[at : at + 1], matrix[at + 2 : at + 3]], axis=0)
                     turned = roll(rows, -SLOT_LANE, 1)
@@ -518,21 +521,21 @@
 PARAMS = pltpu.CompilerParams(vmem_limit_bytes=32 * 2**20)
 
 
-def call(kernel, flags, operands, shapes, scratch=(), aliases=None):
+def call(kernel, flags, operands, shapes, scratch=(), space=pltpu.VMEM):
     return pl.pallas_call(
         kernel,
         out_shape=[jax.ShapeDtypeStruct(shape, F32) for shape in shapes],
-        in_specs=[SMEM] + [VMEM] * len(operands),
+        in_specs=[SMEM] + [pl.BlockSpec(memory_space=space)] * len(operands),
         out_specs=[VMEM] * len(shapes),
-        scratch_shapes=[pltpu.VMEM(shape, F32) for shape in scratch],
+        scratch_shapes=[pltpu.VMEM(x, F32) if isinstance(x, tuple) else x for x in scratch],
         compiler_params=PARAMS,
-        input_output_aliases=aliases or {},
     )(flags, *operands)
 
 
 def step(paired, sizes, *blocks):
     nx, ny, nz = sizes
     axes = ("gx", "gy", "gz")
+    groups = 2 if paired else 3
 
     def permute(value, target):
         pairs = []
@@ -547,66 +550,60 @@
     def swap(value):
         return permute(value, lambda x, y, z: (1 - x, y, z))
 
-    one, zero = jnp.int32(1), jnp.int32(0)
+    def to_low(value):
+        return permute(value, lambda x, y, z: (x - 1, y, z))
+
+    def to_high(value):
+        return permute(value, lambda x, y, z: (x + 1, y, z))
+
+    ends_y = (Y_BLOCKS, 8, 128)
+    shape_z = (groups, 2, 8, 128)
+    shape_y = (groups,) + ends_y
     if paired:
-        groups = 2
         ix, iy, iz = [lax.axis_index(axis) for axis in axes]
         flags = jnp.stack([1 - (ix + iy) % 2, 1 - (ix + iz) % 2]).astype(jnp.int32)
-        operands = list(blocks) + [swap(block) for block in blocks]
     else:
-        groups = 3
-        operands = list(blocks)
-        operands += [permute(block, lambda x, y, z: (x - 1, y, z)) for block in blocks]
-        operands += [permute(block, lambda x, y, z: (x + 1, y, z)) for block in blocks]
-    z_shape = (groups, 8, 128)
-    y_shape = (Y_BLOCKS, 4 * groups, 128)
-    corner_shape = (2, 4 * groups, 128)
-
-    def pack_z(flags):
-        return call(functools.partial(z_pack_kernel, groups), flags, operands, [z_shape])[0]
-
-    def pack_y(flags):
-        return call(functools.partial(y_pack_kernel, groups), flags, operands, [y_shape])[0]
-
-    def corners(flags, side, ends, rows):
-        return pl.pallas_call(
-            functools.partial(corner_kernel, groups, paired),
-            out_shape=jax.ShapeDtypeStruct(y_shape, F32),
-            in_specs=[SMEM, VMEM, VMEM, pl.BlockSpec(memory_space=pl.ANY)],
-            out_specs=pl.BlockSpec(
-                corner_shape, lambda i: (Y_CORNER // 2, 0, 0), memory_space=pltpu.VMEM
-            ),
-            grid=(1,),
-            scratch_shapes=[pltpu.VMEM((2,) + z_shape, F32)],
-            compiler_params=PARAMS,
-            input_output_aliases={3: 0},
-        )(flags, ends[0], ends[1], rows)
+        flags = jnp.ones((2,), jnp.int32)
+    held = [pltpu.VMEM(block.shape, block.dtype) for block in blocks]
+    blocks = [pltpu.with_memory_space_constraint(block, pltpu.HBM) for block in blocks]
+    whole, mine, theirs = call(
+        pack_kernel,
+        flags,
+        blocks,
+        [(W_BLOCKS, 8, 128), shape_y, ends_y],
+        held + [pltpu.SemaphoreType.DMA((7,))],
+        pltpu.HBM,
+    )
+
+    def pack_z(flags, wholes, halos):
+        kernel = functools.partial(z_pack_kernel, groups, paired)
+        return call(kernel, flags, wholes + halos, [shape_z], [(2,) + shape_y])[0]
 
     if paired:
+        rows = mine.at[1].set(swap(theirs))
+        wholes = [whole, swap(whole)]
+        first = permute(rows, lambda x, y, z: (x, y + (1 if (x + y) % 2 == 0 else -1), z))
+        halos = [first, swap(first)]
         first = permute(
-            pack_z(flags), lambda x, y, z: (x, y, z + (1 if (x + z) % 2 == 0 else -1))
+            pack_z(flags, wholes, halos),
+            lambda x, y, z: (x, y, z + (1 if (x + z) % 2 == 0 else -1)),
         )
         ends = [first, swap(first)]
-        rows = corners(flags, None, ends, pack_y(flags))
-        first = permute(rows, lambda x, y, z: (x, y + (1 if (x + y) % 2 == 0 else -1), z))
-        halos = [first, swap(first)]
     else:
-        flags = jnp.ones((2,), jnp.int32)
-        low = jnp.zeros((2,), jnp.int32)
-        ends = [
-            permute(pack_z(low), lambda x, y, z: (x, y, z - 1)),
-            permute(pack_z(flags), lambda x, y, z: (x, y, z + 1)),
-        ]
-        down = corners(jnp.array([0, 1], jnp.int32), None, ends, pack_y(low))
-        up = corners(flags, None, ends, pack_y(flags))
+        wholes = [whole, to_low(whole), to_high(whole)]
+        up, down = [jnp.stack([v, to_low(v), to_high(v)]) for v in (mine[0], theirs)]
         halos = [
             permute(down, lambda x, y, z: (x, y - 1, z)),
             permute(up, lambda x, y, z: (x, y + 1, z)),
         ]
+        low = jnp.array([1, 0], jnp.int32)
+        ends = [
+            permute(pack_z(low, wholes, halos), lambda x, y, z: (x, y, z - 1)),
+            permute(pack_z(flags, wholes, halos), lambda x, y, z: (x, y, z + 1)),
+        ]
     scratch = [
-        (2,) + z_shape,
-        (2,) + y_shape,
-        (2, 2 * groups, 8, 128),
+        (2,) + shape_z,
+        (2,) + shape_y,
         (36, 2 * groups, 8, 384),
         (4, 4, 8, 384),
         (19, 4, 8, 384),
@@ -614,15 +611,8 @@
     ]
     populations, offset = blocks[0], blocks[2]
     shapes = [populations.shape, (6,) + offset.shape[1:]]
-    return tuple(
-        call(
-            functools.partial(main_kernel, groups, paired),
-            flags,
-            operands + ends + halos,
-            shapes,
-            scratch,
-        )
-    )
+    kernel = functools.partial(main_kernel, groups, paired)
+    return tuple(call(kernel, flags, wholes + halos + ends, shapes, scratch))
 
 
 def solution(mesh, paired=None):

time: 27.1 us -> 23.7 us (0.87)
  local copies, waits for them, and re-layouts: 2.64 us -> 0.01 us
  waiting for transfers between devices: 7.16 us -> 6.06 us
  Pallas kernels: 7 us -> 7.57 us
    unnamed x18 -> x0, local copies, waits for them, and re-layouts: 2.64 us -> none
    pallas_call x3, Pallas kernels: 6.45 us -> 7.57 us  [call(): pl.pallas_call(kernel, out_shape=[jax.ShapeDtypeStruct(shape, F32) for sh...]
    ppermute x11 -> x6, waiting for transfers between devices: 7.16 us -> 6.06 us  [permute(): return lax.ppermute(value, axes, pairs)]
    pallas_call x1 -> x0, Pallas kernels: 0.56 us -> none  [corners(): pl.pallas_call(functools.partial(corner_kernel, groups, paired), out_shap...]
    ppermute x11 -> x6, starting transfers between devices: 9.33 us -> 9.18 us  [permute(): return lax.ppermute(value, axes, pairs)]
  transfers between devices with their start and end apart: 11 -> 6, of which waited for: 7 -> 5; matrix products, arithmetic and copies ran while one was open for 0% -> 0% of each run, Pallas kernels for 3% -> 0%
where the time goes in v2:
time: 23.7 us; the launch traced here: 23.6 us
  starting transfers between devices  9.18 us (39%)
  Pallas kernels  7.57 us (32%)
  waiting for transfers between devices  6.06 us (26%)
  between operations  0.67 us (3%)
    ppermute x6, starting transfers between devices, permute(): return lax.ppermute(value, axes, pairs)  9.18 us
    pallas_call x3, Pallas kernels, call(): pl.pallas_call(kernel, out_shape=[jax.ShapeDtypeStruct(shape, F32) for sh...  7.57 us
    ppermute x6, waiting for transfers between devices, permute(): return lax.ppermute(value, axes, pairs)  6.06 us
  transfers between devices with their start and end apart: 6, of which 5 were waited for; matrix products, arithmetic and copies ran while one was open for 0% of the time, Pallas kernels for 0%

profile of v2, /device:TPU:0, one launch (start us, length us, event | category | flops | bytes accessed | tf_op | source)
XLA Modules:
  0.0 23.6 jit_solution(16274822848976996007)
XLA Ops:
  0.6 0.1 pad_add_fusion.flags
  0.7 1.7 %shard_map.86 = (f32[57,8,128]{2,1,0:T(8,128)S(1)}, f32[2,17,8,128]{3,2,1,0:T(8,128)S(1)}, f32[17,8,128]{2,1,0:T(8,128)S(1)}) custom-call(s32[2]{0:T(128)S(1)} %pad_add_fusion.flags, f32[19,2,4,256]{3,2,1,0:T(4,128)} %refs_0_.1, s32[2,1,2,128]{3,2,1,0:T(2,128)} %refs_1_.1, f32[3,2,1,2,128]{4,3,2,1,0:T(2,128)} %refs_2_.1, f32[2,1,2,128]{3,2,1,0:T(2,128)} %refs_3_.1, ...), custom_call_target="tpu_custom_call" | custom-call | tf_op jit(solution)/shard_map/pallas_call | solution.py:525
  2.4 0.5 %collective-permute-start.1 = (f32[17,8,128]{2,1,0:T(8,128)S(1)}, f32[17,8,128]{2,1,0:T(8,128)S(1)}, u32[]{:S(2)}, u32[]{:S(2)}) collective-permute-start(f32[17,8,128]{2,1,0:T(8,128)S(1)} %get-tuple-element.19), channel_id=1, source_target_pairs={{0,16},{1,17},{2,18},{3,19},{4,20},{5,21},{6,22},{7,23},{8,24},{9,... | collective-permute-start | bytes 208904 | tf_op jit(solution)/shard_map/ppermute | solution.py:548
  2.9 0.9 %collective-permute-done.1 = f32[17,8,128]{2,1,0:T(8,128)S(1)} collective-permute-done((f32[17,8,128]{2,1,0:T(8,128)S(1)}, f32[17,8,128]{2,1,0:T(8,128)S(1)}, u32[]{:S(2)}, u32[]{:S(2)}) %collective-permute-start.1) | collective-permute-done | bytes 69664 | tf_op jit(solution)/shard_map/ppermute | solution.py:548
  3.9 2.9 %collective-permute-start.2 = (f32[2,17,8,128]{3,2,1,0:T(8,128)S(1)}, f32[2,17,8,128]{3,2,1,0:T(8,128)S(1)}, u32[]{:S(2)}, u32[]{:S(2)}) collective-permute-start(f32[2,17,8,128]{3,2,1,0:T(8,128)S(1)} %bitcast_dynamic-update-slice_fusion), channel_id=1, source_target_pairs={{0,4},{1,5},{2,6},{3,7},{4,0},{5,1},{6,2},{7,3},{8,12},{9,13},{10,... | collective-permute-start | bytes 417800 | tf_op jit(solution)/shard_map/ppermute | solution.py:548
  6.8 1.9 %collective-permute-start = (f32[57,8,128]{2,1,0:T(8,128)S(1)}, f32[57,8,128]{2,1,0:T(8,128)S(1)}, u32[]{:S(2)}, u32[]{:S(2)}) collective-permute-start(f32[57,8,128]{2,1,0:T(8,128)S(1)} %get-tuple-element.17.refs_0_), channel_id=1, source_target_pairs={{0,16},{1,17},{2,18},{3,19},{4,20},{5,21},{6,22},{7,23},{8,24},{9,... | collective-permute-start | bytes 700424 | tf_op jit(solution)/shard_map/ppermute | solution.py:548
  8.7 1.1 %collective-permute-done.2.refs_2_ = f32[2,17,8,128]{3,2,1,0:T(8,128)S(1)} collective-permute-done((f32[2,17,8,128]{3,2,1,0:T(8,128)S(1)}, f32[2,17,8,128]{3,2,1,0:T(8,128)S(1)}, u32[]{:S(2)}, u32[]{:S(2)}) %collective-permute-start.2) | collective-permute-done | bytes 139296 | tf_op jit(solution)/shard_map/ppermute | solution.py:548
  9.8 1.9 %collective-permute-start.3 = (f32[2,17,8,128]{3,2,1,0:T(8,128)S(1)}, f32[2,17,8,128]{3,2,1,0:T(8,128)S(1)}, u32[]{:S(2)}, u32[]{:S(2)}) collective-permute-start(f32[2,17,8,128]{3,2,1,0:T(8,128)S(1)} %collective-permute-done.2.refs_2_), channel_id=1, source_target_pairs={{0,16},{1,17},{2,18},{3,19},{4,20},{5,21},{6,22},{7,23},{8,24},{9,... | collective-permute-start | bytes 417800 | tf_op jit(solution)/shard_map/ppermute | solution.py:548
  11.7 0.0 collective-permute-done.refs_1_
  11.7 1.0 %collective-permute-done.3.refs_3_ = f32[2,17,8,128]{3,2,1,0:T(8,128)S(1)} collective-permute-done((f32[2,17,8,128]{3,2,1,0:T(8,128)S(1)}, f32[2,17,8,128]{3,2,1,0:T(8,128)S(1)}, u32[]{:S(2)}, u32[]{:S(2)}) %collective-permute-start.3) | collective-permute-done | bytes 139296 | tf_op jit(solution)/shard_map/ppermute | solution.py:548
  12.7 1.0 %shard_map.87 = f32[2,2,8,128]{3,2,1,0:T(8,128)S(1)} custom-call(s32[2]{0:T(128)S(1)} %pad_add_fusion.flags, f32[57,8,128]{2,1,0:T(8,128)S(1)} %get-tuple-element.17.refs_0_, f32[57,8,128]{2,1,0:T(8,128)S(1)} %collective-permute-done.refs_1_, f32[2,17,8,128]{3,2,1,0:T(8,128)S(1)} %collective-permute-done.2.refs_2_, ...), custom_call_target="tpu_custom_call" | custom-call | tf_op jit(solution)/shard_map/pallas_call | solution.py:525
  13.7 1.8 %collective-permute-start.4 = (f32[2,2,8,128]{3,2,1,0:T(8,128)S(1)}, f32[2,2,8,128]{3,2,1,0:T(8,128)S(1)}, u32[]{:S(2)}, u32[]{:S(2)}) collective-permute-start(f32[2,2,8,128]{3,2,1,0:T(8,128)S(1)} %shard_map.87), channel_id=1, source_target_pairs={{0,1},{1,0},{2,3},{3,2},{4,5},{5,4},{6,7},{7,6},{8,9},{9,8},{10,11... | collective-permute-start | bytes 49160 | tf_op jit(solution)/shard_map/ppermute | solution.py:548
  15.5 2.0 %collective-permute-done.4.refs_4_ = f32[2,2,8,128]{3,2,1,0:T(8,128)S(1)} collective-permute-done((f32[2,2,8,128]{3,2,1,0:T(8,128)S(1)}, f32[2,2,8,128]{3,2,1,0:T(8,128)S(1)}, u32[]{:S(2)}, u32[]{:S(2)}) %collective-permute-start.4) | collective-permute-done | bytes 16416 | tf_op jit(solution)/shard_map/ppermute | solution.py:548
  17.5 0.1 collective-permute-start.5
  17.6 1.1 %collective-permute-done.5.refs_5_ = f32[2,2,8,128]{3,2,1,0:T(8,128)S(1)} collective-permute-done((f32[2,2,8,128]{3,2,1,0:T(8,128)S(1)}, f32[2,2,8,128]{3,2,1,0:T(8,128)S(1)}, u32[]{:S(2)}, u32[]{:S(2)}) %collective-permute-start.5) | collective-permute-done | bytes 16416 | tf_op jit(solution)/shard_map/ppermute | solution.py:548
  18.7 4.9 %shard_map.88 = (f32[19,2,4,256]{3,2,1,0:T(4,128)}, f32[6,2,1,2,128]{4,3,2,1,0:T(2,128)}) custom-call(s32[2]{0:T(128)S(1)} %pad_add_fusion.flags, f32[57,8,128]{2,1,0:T(8,128)S(1)} %get-tuple-element.17.refs_0_, f32[57,8,128]{2,1,0:T(8,128)S(1)} %collective-permute-done.refs_1_, f32[2,17,8,128]{3,2,1,0:T(8,128)S(1)} %collective-permute-done.2.refs_2_, ...), custom_call_target="tpu_custom_call" | custom-call | tf_op jit(solution)/shard_map/pallas_call | solution.py:525
  (1 shorter events, 0.0 us)
Async XLA Ops:
  2.4 1.4 %collective-permute-start.1 = (f32[17,8,128]{2,1,0:T(8,128)S(1)}, f32[17,8,128]{2,1,0:T(8,128)S(1)}, u32[]{:S(2)}, u32[]{:S(2)}) collective-permute-start(f32[17,8,128]{2,1,0:T(8,128)S(1)} %get-tuple-element.19), channel_id=1, source_target_pairs={{0,16},{1,17},{2,18},{3,19},{4,20},{5,21},{6,22},{7,23},{8,24},{9,... | collective-permute-start | bytes 208904 | tf_op jit(solution)/shard_map/ppermute | solution.py:548
  3.9 6.0 %collective-permute-start.2 = (f32[2,17,8,128]{3,2,1,0:T(8,128)S(1)}, f32[2,17,8,128]{3,2,1,0:T(8,128)S(1)}, u32[]{:S(2)}, u32[]{:S(2)}) collective-permute-start(f32[2,17,8,128]{3,2,1,0:T(8,128)S(1)} %bitcast_dynamic-update-slice_fusion), channel_id=1, source_target_pairs={{0,4},{1,5},{2,6},{3,7},{4,0},{5,1},{6,2},{7,3},{8,12},{9,13},{10,... | collective-permute-start | bytes 417800 | tf_op jit(solution)/shard_map/ppermute | solution.py:548
  6.8 4.9 %collective-permute-start = (f32[57,8,128]{2,1,0:T(8,128)S(1)}, f32[57,8,128]{2,1,0:T(8,128)S(1)}, u32[]{:S(2)}, u32[]{:S(2)}) collective-permute-start(f32[57,8,128]{2,1,0:T(8,128)S(1)} %get-tuple-element.17.refs_0_), channel_id=1, source_target_pairs={{0,16},{1,17},{2,18},{3,19},{4,20},{5,21},{6,22},{7,23},{8,24},{9,... | collective-permute-start | bytes 700424 | tf_op jit(solution)/shard_map/ppermute | solution.py:548
  9.8 2.9 %collective-permute-start.3 = (f32[2,17,8,128]{3,2,1,0:T(8,128)S(1)}, f32[2,17,8,128]{3,2,1,0:T(8,128)S(1)}, u32[]{:S(2)}, u32[]{:S(2)}) collective-permute-start(f32[2,17,8,128]{3,2,1,0:T(8,128)S(1)} %collective-permute-done.2.refs_2_), channel_id=1, source_target_pairs={{0,16},{1,17},{2,18},{3,19},{4,20},{5,21},{6,22},{7,23},{8,24},{9,... | collective-permute-start | bytes 417800 | tf_op jit(solution)/shard_map/ppermute | solution.py:548
  13.7 3.8 %collective-permute-start.4 = (f32[2,2,8,128]{3,2,1,0:T(8,128)S(1)}, f32[2,2,8,128]{3,2,1,0:T(8,128)S(1)}, u32[]{:S(2)}, u32[]{:S(2)}) collective-permute-start(f32[2,2,8,128]{3,2,1,0:T(8,128)S(1)} %shard_map.87), channel_id=1, source_target_pairs={{0,1},{1,0},{2,3},{3,2},{4,5},{5,4},{6,7},{7,6},{8,9},{9,8},{10,11... | collective-permute-start | bytes 49160 | tf_op jit(solution)/shard_map/ppermute | solution.py:548
  17.5 1.2 %collective-permute-start.5 = (f32[2,2,8,128]{3,2,1,0:T(8,128)S(1)}, f32[2,2,8,128]{3,2,1,0:T(8,128)S(1)}, u32[]{:S(2)}, u32[]{:S(2)}) collective-permute-start(f32[2,2,8,128]{3,2,1,0:T(8,128)S(1)} %collective-permute-done.4.refs_4_), channel_id=1, source_target_pairs={{0,16},{1,17},{2,18},{3,19},{4,20},{5,21},{6,22},{7,23},{8,24},{9,... | collective-permute-start | bytes 49160 | tf_op jit(solution)/shard_map/ppermute | solution.py:548

commit v3 on v2

v3 whole, which is shorter than its diff:
```python
import functools

import jax
import jax.numpy as jnp
from jax import lax
from jax.experimental import pallas as pl
from jax.experimental.pallas import tpu as pltpu
from jax.sharding import PartitionSpec as P

VELOCITIES = [
    (0, 0, 0),
    (1, 0, 0),
    (-1, 0, 0),
    (0, 1, 0),
    (0, -1, 0),
    (0, 0, 1),
    (0, 0, -1),
    (1, 1, 0),
    (-1, -1, 0),
    (1, -1, 0),
    (-1, 1, 0),
    (1, 0, 1),
    (-1, 0, -1),
    (1, 0, -1),
    (-1, 0, 1),
    (0, 1, 1),
    (0, -1, -1),
    (0, 1, -1),
    (0, -1, 1),
]
WEIGHTS = [1.0 / 3.0] + [1.0 / 18.0] * 6 + [1.0 / 36.0] * 12
relax_time = 0.8
fraction_floor = 0.1
distance_floor = 0.5

E0, RADIUS, CODE, PLACE = 9, 36, 37, 38
POPS_AT, CODE_AT, EDGE_VALUES = 36, 55, 57
Z_TILES, CONTACT_TILE = 8, 7
Y_FIELDS = list(range(9)) + [RADIUS, CODE]
Y_GRAIN, Y_BLOCKS = 76, 17
W_GRAIN, W_BLOCKS = 38, 57
F32 = jnp.float32


def iota(shape, dim):
    return lax.broadcasted_iota(jnp.int32, shape, dim)


def pick_lanes(values, index):
    return jnp.take_along_axis(values, index, axis=1, mode="promise_in_bounds")


def roll(values, shift, axis):
    size = values.shape[axis]
    return pltpu.roll(values, shift % size, axis) if shift % size else values


def cross(a, b):
    return [
        a[1] * b[2] - a[2] * b[1],
        a[2] * b[0] - a[0] * b[2],
        a[0] * b[1] - a[1] * b[0],
    ]


def pack_kernel(flags, *refs):
    sources, (whole, mine, theirs), held, sems = refs[:7], refs[7:10], refs[10:17], refs[17]
    copies = [
        pltpu.make_async_copy(source, target, sems.at[n])
        for n, (source, target) in enumerate(zip(sources, held))
    ]
    for copy in copies[1:] + copies[:1]:
        copy.start()
    pops, cell, off, rad, vel, spin, inter = held
    for copy in copies[1:]:
        copy.wait()

    def slot(s, field, rows=slice(None)):
        if field < 3:
            return vel[field, s, 0, rows, :]
        if field < 6:
            return spin[field - 3, s, 0, rows, :]
        if field < 9:
            return off[field - 6, s, 0, rows, :]
        if field < RADIUS:
            return inter[field - E0, s, 0, rows, :]
        if field == RADIUS:
            return rad[s, 0, rows, :]
        return cell[s, 0, rows, :].astype(F32)

    for field in range(38):
        for s in range(2):
            at = 4 * (field % 2) + 2 * s
            whole[W_GRAIN + field // 2, at : at + 2, :] = slot(s, field)
    for out, end in ((mine.at[0], flags[0]), (theirs, 1 - flags[0])):
        for s in range(2):
            for f in range(29):
                if f < 11:
                    value = slot(s, Y_FIELDS[f], pl.ds(end, 1))
                else:
                    kx, q, kz = (f - 11) // 6, (f - 11) // 3 % 2, (f - 11) % 3
                    value = inter[9 * kx + 3 * (q + end) + kz, s, 0, pl.ds(end, 1), :]
                r = Y_GRAIN + 2 * f + s
                out[r // 8, r % 8 : r % 8 + 1, :] = value
        out[16, 6:8, :] = jnp.zeros((2, 128), F32)
    copies[0].wait()
    for out, end in ((mine.at[0], flags[0]), (theirs, 1 - flags[0])):
        for member in range(19):
            for i in range(2):
                row = pops[member, i, pl.ds(3 * end, 1), :]
                for t in range(2):
                    r = 4 * member + 2 * i + t
                    out[r // 8, r % 8 : r % 8 + 1, :] = row[:, 128 * t : 128 * t + 128]
    for member in range(19):
        for i in range(2):
            for t in range(2):
                tile = pops[member, i, :, 128 * t : 128 * t + 128]
                whole[2 * member + i, 4 * t : 4 * t + 4, :] = tile


class Block:
    def __init__(self, whole, halos, group):
        self.whole, self.halos, self.group = whole, halos, group

    def slot(self, s, field):
        at = 4 * (field % 2) + 2 * s
        return self.whole[W_GRAIN + field // 2, at : at + 2, :]

    def pops(self, member, i, t):
        return self.whole[2 * member + i, 4 * t : 4 * t + 4, :]

    def halo_pops(self, end, member, i, t):
        r = 4 * member + 2 * i + t
        return self.halos[end, self.group, r // 8, r % 8 : r % 8 + 1, :]

    def halo_slot(self, end, s, field):
        if field in Y_FIELDS:
            f = Y_FIELDS.index(field)
        else:
            k = field - E0
            q = k // 3 % 3 - (1 - end)
            if q not in (0, 1):
                return jnp.zeros((1, 128), F32)
            f = 11 + 6 * (k // 9) + 3 * q + k % 3
        r = Y_GRAIN + 2 * f + s
        return self.halos[end, self.group, r // 8, r % 8 : r % 8 + 1, :]

    def bins(self, s, field):
        row = iota((8, 128), 0)
        n, at = W_GRAIN + field // 2, 4 * (field % 2) + 2 * s
        rows = [
            self.halo_slot(0, s, field),
            self.whole[n, at : at + 1, :],
            self.whole[n, at + 1 : at + 2, :],
            self.halo_slot(1, s, field),
        ]
        rows = [jnp.broadcast_to(value, (8, 128)) for value in rows]
        return jnp.where(
            row < 4,
            jnp.where(row < 2, rows[0], rows[1]),
            jnp.where(row < 6, rows[2], rows[3]),
        )

    def cells(self, member, i, t):
        row = iota((8, 128), 0)
        own = self.whole[2 * member + i]
        if isinstance(t, int):
            own = roll(own, 2 - 4 * t, 0)
            low, high = [self.halo_pops(end, member, i, t) for end in range(2)]
        else:
            own = jnp.where(t, roll(own, -2, 0), roll(own, 2, 0))
            low, high = [
                jnp.where(
                    t, self.halo_pops(end, member, i, 1), self.halo_pops(end, member, i, 0)
                )
                for end in range(2)
            ]
        low, high = jnp.broadcast_to(low, (8, 128)), jnp.broadcast_to(high, (8, 128))
        return jnp.where(row < 2, low, jnp.where(row > 5, high, own))


def position(code, offset):
    first = jnp.floor(code * 0.25)
    rest = code - 4.0 * first
    second = jnp.floor(rest * 0.5)
    corner = [first, second, rest - 2.0 * second]
    return [corner[c] + offset[c] for c in range(3)]


def store_ends(groups, paired, side, first, second, held):
    for g in range(groups):
        held[side, g] = first[g]
        held[1 - side, g] = second[(g + 1) % 2 if paired else g]


def lane_groups(groups):
    return [0, 1, 0, 1] if groups == 2 else [0, 1, 1, 2]


def by_group(groups, values, lane):
    order = lane_groups(groups)
    result = values[order[3]]
    for q in (2, 1, 0):
        if order[q] != order[q + 1] or q < 2:
            result = jnp.where(lane < 32 * (q + 1), values[order[q]], result)
    return result


def by_layer(groups, values, lane):
    odd = lane // 16 % 2 == 1
    pairs = [jnp.where(odd, values[2 * g + 1], values[2 * g]) for g in range(groups)]
    return by_group(groups, pairs, lane)


def cell_codes(lane, row):
    return (4 * (lane // 16 % 2) + 2 * (row % 2) + lane % 2).astype(F32)


def choose(masks, values):
    return jnp.where(masks[0], values[0], jnp.where(masks[1], values[1], 0.0))


def z_pack_kernel(groups, paired, flags, *refs):
    wholes, (first, second, out, held) = refs[:groups], refs[groups:]
    store_ends(groups, paired, flags[0], first, second, held)
    high = flags[1] == 1
    lane, row = iota((8, 128), 1), iota((8, 128), 0)
    block = [Block(wholes[g], held, g) for g in range(groups)]
    start = jnp.where(high, 127, 0)
    index = jnp.full((8, 128), start, jnp.int32)
    pops_index = jnp.full((8, 128), jnp.where(high, 126, 0), jnp.int32) + lane % 2
    inner = lane % 16 // 2

    def picked(s, field):
        values = [pick_lanes(block[g].bins(s, field), index) for g in range(groups)]
        return by_group(groups, values, lane)

    slots = [[picked(s, field) for field in range(38)] for s in range(2)]
    code = cell_codes(lane, row)
    masks = [slots[s][CODE] == code for s in range(2)]
    values = [choose(masks, [slots[0][f], slots[1][f]]) for f in range(36)]
    for member in range(19):
        tiles = []
        for layer in range(2 * groups):
            g, i = layer // 2, layer % 2
            tile = block[g].cells(member, i, high)
            tiles.append(pick_lanes(tile, pops_index))
        values.append(by_layer(groups, tiles, lane))
    for tile in range(CONTACT_TILE):
        packed = values[8 * tile]
        for q in range(1, 8):
            if 8 * tile + q < len(values):
                packed = jnp.where(inner == q, values[8 * tile + q], packed)
        out[tile] = packed
    packed = jnp.zeros((8, 128), F32)
    for s in range(2):
        state = position(slots[s][CODE], slots[s][6:9]) + [slots[s][RADIUS]] + slots[s][0:6]
        for q, value in enumerate(state):
            packed = jnp.where(lane % 32 == 16 * s + q, value, packed)
    out[CONTACT_TILE] = packed


def dot_lattice(vector, velocity):
    total = None
    for c in range(3):
        if vector[c]:
            if total is None:
                total = velocity[c] if vector[c] > 0 else -velocity[c]
            else:
                total = total + velocity[c] if vector[c] > 0 else total - velocity[c]
    return total


def equilibrium_base(velocity):
    return 1.0 - 1.5 * (
        velocity[0] * velocity[0] + velocity[1] * velocity[1] + velocity[2] * velocity[2]
    )


def collide(f, sums, members):
    fraction = 1.0 - jnp.exp(-sums[0])
    excess = relax_time - 0.5
    weight = fraction * excess / (1.0 - fraction + excess)
    inverse = 1.0 / jnp.maximum(sums[0], fraction_floor)
    solid_velocity = [sums[1 + c] * inverse for c in range(3)]
    density = sum(f[1:], f[0])
    momentum = []
    for c in range(3):
        plus = [f[m] for m in range(19) if VELOCITIES[m][c] > 0]
        minus = [f[m] for m in range(19) if VELOCITIES[m][c] < 0]
        momentum.append(sum(plus[1:], plus[0]) - sum(minus[1:], minus[0]))
    per_density = 1.0 / density
    fluid_velocity = [momentum[c] * per_density for c in range(3)]
    share = [weight * inverse * (momentum[c] - density * solid_velocity[c]) for c in range(3)]
    relax = (1.0 - weight) * (1.0 / relax_time)
    keep = 1.0 - relax
    fluid_base = equilibrium_base(fluid_velocity)
    solid_base = equilibrium_base(solid_velocity)
    done = {}
    for member in [0] + list(range(1, 19, 2)):
        reverse = member + 1 if member else 0
        if member not in members and reverse not in members:
            continue
        part = WEIGHTS[member] * density
        if member == 0:
            fluid = [part * fluid_base] * 2
            settled = [part * solid_base] * 2
        else:
            ends = []
            for base, velocity in (
                (fluid_base, fluid_velocity),
                (solid_base, solid_velocity),
            ):
                along = dot_lattice(VELOCITIES[member], velocity)
                even = base + 4.5 * along * along
                odd = 3.0 * along
                ends.append([part * (even + odd), part * (even - odd)])
            fluid, settled = ends
        pair = [f[member], f[reverse]]
        for way, m in enumerate((member, reverse)[: 2 if member else 1]):
            if m in members:
                exchange = (pair[1 - way] - fluid[1 - way]) - (pair[way] - settled[way])
                done[m] = keep * pair[way] + relax * fluid[way] + weight * exchange
    return done, share


def deposit_terms(weight, base, spin, k):
    terms = [weight]
    for c in range(3):
        u, v = (c + 1) % 3, (c + 2) % 3
        speed = base[c]
        if k[v]:
            speed = speed + spin[u] if k[v] > 0 else speed - spin[u]
        if k[u]:
            speed = speed - spin[v] if k[u] > 0 else speed + spin[v]
        terms.append(weight * speed)
    return terms


def plus(totals, terms):
    return list(terms) if totals is None else [a + b for a, b in zip(totals, terms)]


class Moments:
    def __init__(self):
        self.force, self.moment = [None] * 3, [None] * 3

    def add(self, store, c, value, sign):
        if store[c] is None:
            store[c] = value if sign > 0 else -value
        else:
            store[c] = store[c] + value if sign > 0 else store[c] - value

    def turn(self, axis, forces, sign):
        u, v = (axis + 1) % 3, (axis + 2) % 3
        self.add(self.moment, v, forces[u], sign)
        self.add(self.moment, u, forces[v], -sign)

    def push(self, forces):
        for c in range(3):
            self.add(self.force, c, forces[c], 1)

    def loads(self, offset):
        turned = cross([0.5 - value for value in offset], self.force)
        return self.force + [self.moment[c] + turned[c] for c in range(3)]


def pair_force(gap, a_radius, a_speed, a_turn, other, keep=None):
    b_radius = other[0]
    distance = jnp.sqrt(gap[0] * gap[0] + gap[1] * gap[1] + gap[2] * gap[2])
    scale = 1.0 / jnp.maximum(distance, distance_floor)
    normal = [gap[c] * scale for c in range(3)]
    depth = jnp.maximum(a_radius + b_radius - distance, 0.0)
    strength = a_radius * b_radius * depth
    if keep is not None:
        strength = jnp.where(keep, strength, 0.0)
    turning = [a_turn[c] + b_radius * other[4 + c] for c in range(3)]
    swing = cross(turning, normal)
    relative = [a_speed[c] - other[1 + c] + swing[c] for c in range(3)]
    along = relative[0] * normal[0] + relative[1] * normal[1] + relative[2] * normal[2]
    factor = 1.0 + along
    pushed = [strength * (factor * normal[c] + relative[c]) for c in range(3)]
    return pushed, cross(normal, pushed)


def own_state(block):
    def rows(field):
        values = [block.slot(s, field) for s in range(2)]
        return jnp.concatenate([values[0], values[0], values[1], values[1]], axis=0)

    place = position(rows(CODE), [rows(6 + c) for c in range(3)])
    return place, [rows(RADIUS)] + [rows(c) for c in range(6)]


PARTS = [4, 9, 14, 18]
AT_LAYER = {0: 0, 1: 1, 2: 2, -1: 3}


def bulk_kernel(groups, paired, flags, *refs):
    layers = 2 * groups
    wholes, (y_first, y_second) = refs[:groups], refs[groups : groups + 2]
    out_pops, out_loads = refs[groups + 2 : groups + 4]
    held, placed, solid, passed, share = refs[groups + 4 :]
    targets = [0, 1, 2, layers - 1]
    store_ends(groups, paired, flags[0], y_first, y_second, held)
    block = [Block(wholes[g], held, g) for g in range(groups)]
    lane8 = iota((8, 128), 1)
    half = lane8 // 2

    def spread(rows):
        return jnp.concatenate([pick_lanes(rows, half), pick_lanes(rows, half + 64)], axis=1)

    cell_code = (2 * (iota((8, 256), 0) % 2) + iota((8, 256), 1) % 2).astype(F32)
    masks = []
    codes = [[block[g].bins(s, CODE) for g in range(groups)] for s in range(2)]
    for g in range(groups):
        wide = [spread(codes[s][g]) for s in range(2)]
        for i in range(2):
            masks.append([wide[s] == cell_code + 4.0 * i for s in range(2)])
    for field in range(36):
        rows = [[block[g].bins(s, field) for g in range(groups)] for s in range(2)]
        for g in range(groups):
            values = [spread(rows[s][g]) for s in range(2)]
            for i in range(2):
                placed[field, 2 * g + i] = choose(masks[2 * g + i], values)
    for layer in range(layers):
        spin = [placed[3 + c, layer] for c in range(3)]
        turned = cross(spin, [0.5 - placed[6 + c, layer] for c in range(3)])
        for c in range(3):
            placed[c, layer] = placed[c, layer] + turned[c]

    for n, target in enumerate(targets):
        total = None
        for kz in (-1, 0, 1):
            along_z = None
            for ky in (-1, 0, 1):
                along_y = None
                for kx in (-1, 0, 1):
                    source = (target - kx) % layers
                    weight = placed[E0 + 9 * (kx + 1) + 3 * (ky + 1) + kz + 1, source]
                    spin = [placed[3 + c, source] for c in range(3)]
                    base = [placed[c, source] for c in range(3)]
                    along_y = plus(along_y, deposit_terms(weight, base, spin, (kx, ky, kz)))
                along_z = plus(along_z, [roll(a, ky, 0) for a in along_y])
            total = plus(total, [roll(a, kz, 1) for a in along_z])
        for f in range(4):
            solid[f, n] = total[f]

    for n, target in enumerate(targets):
        g, i = target // 2, target % 2
        if n < 2:
            members = list(range(19))
        else:
            members = [m for m in range(19) if VELOCITIES[m][0] == (-1 if n == 2 else 1)]
        for t in range(2):
            tile = slice(128 * t, 128 * t + 128)
            f = [block[g].cells(member, i, t) for member in range(19)]
            done, forces = collide(f, [solid[c, n, :, tile] for c in range(4)], members)
            for c in range(3):
                share[c, n, :, tile] = forces[c]
            for m, value in done.items():
                passed[m, n, :, tile] = value
    for member in range(19):
        vector = VELOCITIES[member]
        for i in range(2):
            value = roll(passed[member, AT_LAYER[i - vector[0]]], vector[2], 1)
            value = roll(value, vector[1] - 2, 0)
            for t in range(2):
                out_pops[2 * member + i, 4 * t : 4 * t + 4, :] = value[
                    0:4, 128 * t : 128 * t + 128
                ]

    moments = [Moments() for _ in range(2)]
    for kz in (-1, 0, 1):
        across = [[roll(share[c, n], -kz, 1) for c in range(3)] for n in range(4)]
        for ky in (-1, 0, 1):
            near = [[roll(across[n][c], -ky, 0) for c in range(3)] for n in range(4)]
            for i in range(2):
                together = None
                for kx in (-1, 0, 1):
                    weight = placed[E0 + 9 * (kx + 1) + 3 * (ky + 1) + kz + 1, i]
                    forces = [weight * near[AT_LAYER[i + kx]][c] for c in range(3)]
                    together = plus(together, forces)
                    if kx:
                        moments[i].turn(0, forces, kx)
                moments[i].push(together)
                if ky:
                    moments[i].turn(1, together, ky)
                if kz:
                    moments[i].turn(2, together, kz)
    hydro = [moments[i].loads([placed[6 + c, i] for c in range(3)]) for i in range(2)]

    even = (2 * lane8) % 128
    inside = (lane8 > 0) & (lane8 < 127)
    for f in range(6):
        for s in range(2):
            value = jnp.where(masks[0][s], hydro[0][f], 0.0) + jnp.where(
                masks[1][s], hydro[1][f], 0.0
            )
            value = value + roll(value, -1, 0)
            value = value + roll(value, -1, 1)
            value = jnp.where(
                lane8 < 64, pick_lanes(value[:, :128], even), pick_lanes(value[:, 128:], even)
            )
            value = jnp.where(inside, value, 0.0)
            both = jnp.concatenate([value[2:3], value[4:5]], axis=0)
            out_loads[f, 2 * s : 2 * s + 2, :] = both


def side_kernel(groups, paired, flags, *refs):
    layers = 2 * groups
    wholes, (y_first, y_second) = refs[:groups], refs[groups : groups + 2]
    out_contact, out_edge, held = refs[groups + 2 :]
    store_ends(groups, paired, flags[0], y_first, y_second, held)
    block = [Block(wholes[g], held, g) for g in range(groups)]
    lane8, row8 = iota((8, 128), 1), iota((8, 128), 0)
    inner = lane8 % 16
    z_near = jnp.where(inner < 8, jnp.maximum(inner - 4, 0), jnp.minimum(inner + 116, 127))
    z_bin = jnp.where(inner < 8, z_near // 2, jnp.minimum(inner + 244, 255) // 2)

    def at_edge(s, field):
        rows = [pick_lanes(block[g].bins(s, field), z_bin) for g in range(groups)]
        return by_group(groups, rows, lane8)

    edge_code = cell_codes(lane8, row8)
    codes = [at_edge(s, CODE) for s in range(2)]
    for s in range(2):
        out_edge[CODE_AT + s] = codes[s]
    edge_masks = [value == edge_code for value in codes]
    for field in range(36):
        out_edge[field] = choose(edge_masks, [at_edge(s, field) for s in range(2)])
    for member in range(19):
        tiles = []
        for layer in range(layers):
            near = [block[layer // 2].cells(member, layer % 2, t) for t in range(2)]
            tiles.append(
                jnp.where(inner < 8, pick_lanes(near[0], z_near), pick_lanes(near[1], z_near))
            )
        out_edge[POPS_AT + member] = by_layer(groups, tiles, lane8)

    place, state = own_state(block[0])
    a_radius, a_speed = state[0], state[1:4]
    a_turn = [a_radius * value for value in state[4:7]]
    push, twist = None, None
    for oy in (-1, 0, 1):
        for g in range(groups):
            steps = [0] if g == 0 else []
            if g == 1:
                steps = steps + [1]
            if g == groups - 1:
                steps = steps + [-1]
            states = []
            for field in [CODE, 6, 7, 8, RADIUS, 0, 1, 2, 3, 4, 5]:
                values = []
                for s in range(2):
                    value = block[g].slot(s, field)
                    if oy < 0:
                        value = jnp.concatenate(
                            [block[g].halo_slot(0, s, field), value[0:1]], axis=0
                        )
                    if oy > 0:
                        value = jnp.concatenate(
                            [value[1:2], block[g].halo_slot(1, s, field)], axis=0
                        )
                    values.append(value)
                states.append(jnp.concatenate(values + values, axis=0))
            states = position(states[0], states[1:4]) + states[4:]
            for oz in (-1, 0, 1):
                other = [roll(value, -oz, 1) for value in states]
                keep = lane8 != (0 if oz < 0 else 127) if oz else None
                gap = [other[c] - place[c] for c in range(3)]
                gap[1], gap[2] = gap[1] + 2.0 * oy, gap[2] + 2.0 * oz
                for ox in steps:
                    apart = [gap[0] + 2.0 * ox, gap[1], gap[2]]
                    pushed, twisted = pair_force(
                        apart, a_radius, a_speed, a_turn, other[3:], keep
                    )
                    push, twist = plus(push, pushed), plus(twist, twisted)
    contact = [-value for value in push] + [-a_radius * value for value in twist]
    contact = [value + roll(value, -2, 0) for value in contact]

    for f in range(6):
        out_contact[f] = contact[f]


def edge_kernel(
    groups, paired, flags, whole, bulk_pops, bulk_loads, bulk_contact, edge, first, second, *refs
):
    final_pops, final_loads, held, out_pops, out_loads, sems = refs
    side = flags[1]
    for tile in range(Z_TILES):
        held[side, tile] = first[tile]
        value = second[tile]
        held[1 - side, tile] = roll(value, 32, 1) if paired else value
    lane, row = iota((8, 128), 1), iota((8, 128), 0)
    inner = lane % 16
    at_low = (inner == 2) | (inner == 3)
    at_high = (inner == 12) | (inner == 13)

    def value_of(field):
        q = 2 * (field % 8)
        low = roll(held[0, field // 8], 2 - q, 1)
        high = roll(held[1, field // 8], 12 - q, 1)
        return jnp.where(at_low, low, jnp.where(at_high, high, edge[field]))

    speed, spin, offset = [[value_of(3 * n + c) for c in range(3)] for n in range(3)]
    weights = [value_of(E0 + k) for k in range(27)]
    turned = cross(spin, [0.5 - value for value in offset])
    base = [speed[c] + turned[c] for c in range(3)]
    sums = None
    for kx in (-1, 0, 1):
        for kz in (-1, 0, 1):
            along = None
            for ky in (-1, 0, 1):
                weight = weights[9 * (kx + 1) + 3 * (ky + 1) + kz + 1]
                terms = deposit_terms(weight, base, spin, (kx, ky, kz))
                along = plus(along, [roll(a, ky, 0) for a in terms])
            sums = plus(sums, [roll(a, 16 * kx + kz, 1) for a in along])
    f = [value_of(POPS_AT + member) for member in range(19)]
    done, share = collide(f, sums, list(range(19)))

    lane4 = iota((4, 128), 1)
    copies = []
    for member in range(19):
        vector = VELOCITIES[member]
        value = roll(done[member], vector[1] - 2, 0)
        shift = 16 * vector[0] + vector[2]
        for i in range(2):
            for t in range(2):
                home = shift - 16 * i + (116 if t else -4)
                moved = roll(value, home, 1)[0:4]
                bulk = bulk_pops[2 * member + i, 4 * t : 4 * t + 4, :]
                mask = lane4 >= 126 if t else lane4 < 2
                out_pops[member, i, :, 128 * t : 128 * t + 128] = jnp.where(mask, moved, bulk)
        if member in PARTS:
            n = PARTS.index(member)
            part = pl.ds(PARTS[n - 1] + 1 if n else 0, member - (PARTS[n - 1] if n else -1))
            copy = pltpu.make_async_copy(out_pops.at[part], final_pops.at[part], sems.at[n])
            copy.start()
            copies.append(copy)

    moments = Moments()
    for kx in (-1, 0, 1):
        for kz in (-1, 0, 1):
            near = [roll(share[c], -16 * kx - kz, 1) for c in range(3)]
            together = None
            for ky in (-1, 0, 1):
                weight = weights[9 * (kx + 1) + 3 * (ky + 1) + kz + 1]
                forces = [weight * roll(near[c], -ky, 0) for c in range(3)]
                together = plus(together, forces)
                if ky:
                    moments.turn(1, forces, ky)
            moments.push(together)
            if kx:
                moments.turn(0, together, kx)
            if kz:
                moments.turn(2, together, kz)
    hydro = moments.loads(offset)

    place, state = own_state(Block(whole, None, 0))
    own_index = jnp.where(lane < 64, 0, 127)
    place = [pick_lanes(value, own_index) for value in place]
    state = [pick_lanes(value, own_index) for value in state]
    a_radius, a_speed = state[0], state[1:4]
    a_turn = [a_radius * value for value in state[4:7]]
    step_x, step_y = inner - 1, lane % 64 // 16 - 1
    order = lane_groups(groups)
    runs = [order.index(groups - 1), 0, 1]
    run = 32 * jnp.where(step_x < 0, runs[0], jnp.where(step_x == 0, 0, runs[2]))
    other = [None] * 10
    for end in range(2):
        tile = held[end, CONTACT_TILE]
        for oy in (-1, 0, 1):
            at = 2 * (oy + 1)
            rows = jnp.concatenate([tile[at : at + 1], tile[at + 2 : at + 3]], axis=0)
            moved = roll(rows, -16, 1)
            rows = jnp.concatenate([rows, moved, rows, moved], axis=0)
            mask = (lane // 64 == end) & (step_y == oy)
            for q in range(10):
                value = pick_lanes(rows, run + q)
                other[q] = value if other[q] is None else jnp.where(mask, value, other[q])
    keep = (step_x < 2) & (step_y < 2)
    gap = [
        other[0] - place[0] + (2 * step_x).astype(F32),
        other[1] - place[1] + (2 * step_y).astype(F32),
        other[2] - place[2] + jnp.where(lane < 64, -2.0, 2.0),
    ]
    pushed, twisted = pair_force(gap, a_radius, a_speed, a_turn, other[3:], keep)
    contact = [-value for value in pushed] + [-a_radius * value for value in twisted]
    ends = lane == 0, lane == 127
    masks = [edge[CODE_AT + s] == cell_codes(lane, row) for s in range(2)]
    for f in range(6):
        value = contact[f] + roll(contact[f], -2, 0)
        value = value + roll(value, -1, 1) + roll(value, -2, 1)
        value = value + roll(value, -16, 1) + roll(value, -32, 1)
        touch = jnp.where(ends[0], value, jnp.where(ends[1], roll(value, 63, 1), 0.0))
        for s in range(2):
            value = jnp.where(masks[s], hydro[f], 0.0)
            value = value + roll(value, -16, 1)
            value = value + roll(value, -1, 0)
            value = value + roll(value, -1, 1)
            value = jnp.where(
                ends[0], roll(value, -4, 1), jnp.where(ends[1], roll(value, 117, 1), 0.0)
            )
            both = jnp.concatenate([value[2:3], value[4:5]], axis=0)
            both = both + touch[4 * s : 4 * s + 2]
            both = both + bulk_contact[f, 4 * s : 4 * s + 2, :]
            out_loads[f, s, 0] = bulk_loads[f, 2 * s : 2 * s + 2, :] + both
    copy = pltpu.make_async_copy(out_loads, final_loads, sems.at[len(PARTS)])
    copy.start()
    for copy in copies + [copy]:
        copy.wait()


SMEM = pl.BlockSpec(memory_space=pltpu.SMEM)
PARAMS = pltpu.CompilerParams(vmem_limit_bytes=32 * 2**20)


def call(kernel, flags, operands, shapes, scratch=(), spaces=(pltpu.VMEM, pltpu.VMEM)):
    return pl.pallas_call(
        kernel,
        out_shape=[jax.ShapeDtypeStruct(shape, F32) for shape in shapes],
        in_specs=[SMEM] + [pl.BlockSpec(memory_space=spaces[0])] * len(operands),
        out_specs=[pl.BlockSpec(memory_space=spaces[1])] * len(shapes),
        scratch_shapes=[pltpu.VMEM(x, F32) if isinstance(x, tuple) else x for x in scratch],
        compiler_params=PARAMS,
    )(flags, *operands)


def step(paired, sizes, *blocks):
    nx, ny, nz = sizes
    axes = ("gx", "gy", "gz")
    groups = 2 if paired else 3

    def permute(value, target):
        pairs = []
        for x in range(nx):
            for y in range(ny):
                for z in range(nz):
                    tx, ty, tz = target(x, y, z)
                    there = ((tx % nx) * ny + ty % ny) * nz + tz % nz
                    pairs.append(((x * ny + y) * nz + z, there))
        return lax.ppermute(value, axes, pairs)

    def swap(value):
        return permute(value, lambda x, y, z: (1 - x, y, z))

    def to_low(value):
        return permute(value, lambda x, y, z: (x - 1, y, z))

    def to_high(value):
        return permute(value, lambda x, y, z: (x + 1, y, z))

    ends_y = (Y_BLOCKS, 8, 128)
    shape_z = (Z_TILES, 8, 128)
    shape_y = (groups,) + ends_y
    if paired:
        ix, iy, iz = [lax.axis_index(axis) for axis in axes]
        flags = jnp.stack([1 - (ix + iy) % 2, 1 - (ix + iz) % 2]).astype(jnp.int32)
    else:
        flags = jnp.ones((2,), jnp.int32)
    held = [pltpu.VMEM(block.shape, block.dtype) for block in blocks]
    blocks = [pltpu.with_memory_space_constraint(block, pltpu.HBM) for block in blocks]
    whole, mine, theirs = call(
        pack_kernel,
        flags,
        blocks,
        [(W_BLOCKS, 8, 128), shape_y, ends_y],
        held + [pltpu.SemaphoreType.DMA((7,))],
        (pltpu.HBM, pltpu.VMEM),
    )

    def pack_z(flags, wholes, halos):
        kernel = functools.partial(z_pack_kernel, groups, paired)
        return call(kernel, flags, wholes + halos, [shape_z], [(2,) + shape_y])[0]

    def pack_bulk(wholes, halos):
        scratch = [
            (2,) + shape_y,
            (36, 2 * groups, 8, 256),
            (4, 4, 8, 256),
            (19, 4, 8, 256),
            (3, 4, 8, 256),
        ]
        return call(
            functools.partial(bulk_kernel, groups, paired),
            flags,
            wholes + halos,
            [(W_GRAIN, 8, 128), (6, 4, 128)],
            scratch,
        )

    if paired:
        rows = mine.at[1].set(swap(theirs))
        wholes = [whole, swap(whole)]
        first = permute(rows, lambda x, y, z: (x, y + (1 if (x + y) % 2 == 0 else -1), z))
        halos = [first, swap(first)]
        first = permute(
            pack_z(flags, wholes, halos),
            lambda x, y, z: (x, y, z + (1 if (x + z) % 2 == 0 else -1)),
        )
        bulk = pack_bulk(wholes, halos)
        first, bulk = lax.optimization_barrier((first, bulk))
        ends = [first, swap(first)]
    else:
        wholes = [whole, to_low(whole), to_high(whole)]
        up, down = [jnp.stack([v, to_low(v), to_high(v)]) for v in (mine[0], theirs)]
        halos = [
            permute(down, lambda x, y, z: (x, y - 1, z)),
            permute(up, lambda x, y, z: (x, y + 1, z)),
        ]
        low = jnp.array([1, 0], jnp.int32)
        ends = [
            permute(pack_z(low, wholes, halos), lambda x, y, z: (x, y, z - 1)),
            permute(pack_z(flags, wholes, halos), lambda x, y, z: (x, y, z + 1)),
        ]
        bulk = pack_bulk(wholes, halos)
    side = call(
        functools.partial(side_kernel, groups, paired),
        flags,
        wholes + halos,
        [(6, 8, 128), (EDGE_VALUES, 8, 128)],
        [(2,) + shape_y],
    )
    populations, offset = blocks[0], blocks[2]
    shapes = [populations.shape, (6,) + offset.shape[1:]]
    return tuple(
        call(
            functools.partial(edge_kernel, groups, paired),
            flags,
            [whole] + list(bulk) + list(side) + ends,
            shapes,
            [(2,) + shape_z] + shapes + [pltpu.SemaphoreType.DMA((len(PARTS) + 1,))],
            (pltpu.VMEM, pltpu.HBM),
        )
    )


def solution(mesh, paired=None):
    sizes = tuple(mesh.shape[axis] for axis in ("gx", "gy", "gz"))
    if paired is None:
        paired = sizes[0] == 2 and sizes[1] % 2 == 0 and sizes[2] % 2 == 0
    cells, bins = P(None, "gx", "gy", "gz"), P(None, None, "gx", "gy", "gz")
    return jax.shard_map(
        functools.partial(step, paired, sizes),
        mesh=mesh,
        in_specs=(cells, cells, bins, cells, bins, bins, bins),
        out_specs=(cells, bins),
        check_vma=False,
    )
```

time: 23.7 us -> 22 us (0.928)
  waiting for transfers between devices: 6.06 us -> 3.18 us
  starting transfers between devices: 9.18 us -> 9.82 us
  Pallas kernels: 7.57 us -> 8.07 us
    ppermute x6, waiting for transfers between devices: 6.06 us -> 3.18 us  [permute(): return lax.ppermute(value, axes, pairs)]
    ppermute x6, starting transfers between devices: 9.18 us -> 9.82 us  [permute(): return lax.ppermute(value, axes, pairs)]
    pallas_call x3 -> x5, Pallas kernels: 7.57 us -> 8.07 us  [call(): pl.pallas_call(kernel, out_shape=[jax.ShapeDtypeStruct(shape, F32) for sh...]
  transfers between devices with their start and end apart: 6 -> 6, of which waited for: 5 -> 4; matrix products, arithmetic and copies ran while one was open for 0% -> 0% of each run, Pallas kernels for 0% -> 15%
where the time goes in v3:
time: 22 us; the launch traced here: 21.9 us
  starting transfers between devices  9.82 us (45%)
  Pallas kernels  8.07 us (37%)
  waiting for transfers between devices  3.18 us (14%)
  between operations  0.7 us (3%)
    ppermute x6, starting transfers between devices, permute(): return lax.ppermute(value, axes, pairs)  9.82 us
    pallas_call x5, Pallas kernels, call(): pl.pallas_call(kernel, out_shape=[jax.ShapeDtypeStruct(shape, F32) for sh...  8.07 us
    ppermute x6, waiting for transfers between devices, permute(): return lax.ppermute(value, axes, pairs)  3.18 us
  transfers between devices with their start and end apart: 6, of which 4 were waited for; matrix products, arithmetic and copies ran while one was open for 0% of the time, Pallas kernels for 15%

profile of v3, /device:TPU:0, one launch (start us, length us, event | category | flops | bytes accessed | tf_op | source)
XLA Modules:
  0.0 21.9 jit_solution(2768910672479500367)
XLA Ops:
  0.6 0.1 pad_add_fusion.flags
  0.7 1.7 %shard_map.86 = (f32[57,8,128]{2,1,0:T(8,128)S(1)}, f32[2,17,8,128]{3,2,1,0:T(8,128)S(1)}, f32[17,8,128]{2,1,0:T(8,128)S(1)}) custom-call(s32[2]{0:T(128)S(1)} %pad_add_fusion.flags, f32[19,2,4,256]{3,2,1,0:T(4,128)} %refs_0_.1, s32[2,1,2,128]{3,2,1,0:T(2,128)} %refs_1_.1, f32[3,2,1,2,128]{4,3,2,1,0:T(2,128)} %refs_2_.1, f32[2,1,2,128]{3,2,1,0:T(2,128)} %refs_3_.1, ...), custom_call_target="tpu_custom_call" | custom-call | tf_op jit(solution)/shard_map/pallas_call | solution.py:720
  2.4 0.5 %collective-permute-start.1 = (f32[17,8,128]{2,1,0:T(8,128)S(1)}, f32[17,8,128]{2,1,0:T(8,128)S(1)}, u32[]{:S(2)}, u32[]{:S(2)}) collective-permute-start(f32[17,8,128]{2,1,0:T(8,128)S(1)} %get-tuple-element.26), channel_id=1, source_target_pairs={{0,16},{1,17},{2,18},{3,19},{4,20},{5,21},{6,22},{7,23},{8,24},{9,... | collective-permute-start | bytes 208904 | tf_op jit(solution)/shard_map/ppermute | solution.py:743
  2.9 0.9 %collective-permute-done.1 = f32[17,8,128]{2,1,0:T(8,128)S(1)} collective-permute-done((f32[17,8,128]{2,1,0:T(8,128)S(1)}, f32[17,8,128]{2,1,0:T(8,128)S(1)}, u32[]{:S(2)}, u32[]{:S(2)}) %collective-permute-start.1) | collective-permute-done | bytes 69664 | tf_op jit(solution)/shard_map/ppermute | solution.py:743
  3.9 2.9 %collective-permute-start.2 = (f32[2,17,8,128]{3,2,1,0:T(8,128)S(1)}, f32[2,17,8,128]{3,2,1,0:T(8,128)S(1)}, u32[]{:S(2)}, u32[]{:S(2)}) collective-permute-start(f32[2,17,8,128]{3,2,1,0:T(8,128)S(1)} %bitcast_dynamic-update-slice_fusion), channel_id=1, source_target_pairs={{0,4},{1,5},{2,6},{3,7},{4,0},{5,1},{6,2},{7,3},{8,12},{9,13},{10,... | collective-permute-start | bytes 417800 | tf_op jit(solution)/shard_map/ppermute | solution.py:743
  6.8 1.9 %collective-permute-start = (f32[57,8,128]{2,1,0:T(8,128)S(1)}, f32[57,8,128]{2,1,0:T(8,128)S(1)}, u32[]{:S(2)}, u32[]{:S(2)}) collective-permute-start(f32[57,8,128]{2,1,0:T(8,128)S(1)} %get-tuple-element.24.refs_0_.whole), channel_id=1, source_target_pairs={{0,16},{1,17},{2,18},{3,19},{4,20},{5,21},{6,22},{7,23},{8,24},{9,... | collective-permute-start | bytes 700424 | tf_op jit(solution)/shard_map/ppermute | solution.py:743
  8.7 1.1 %collective-permute-done.2.refs_2_ = f32[2,17,8,128]{3,2,1,0:T(8,128)S(1)} collective-permute-done((f32[2,17,8,128]{3,2,1,0:T(8,128)S(1)}, f32[2,17,8,128]{3,2,1,0:T(8,128)S(1)}, u32[]{:S(2)}, u32[]{:S(2)}) %collective-permute-start.2) | collective-permute-done | bytes 139296 | tf_op jit(solution)/shard_map/ppermute | solution.py:743
  9.8 1.9 %collective-permute-start.3 = (f32[2,17,8,128]{3,2,1,0:T(8,128)S(1)}, f32[2,17,8,128]{3,2,1,0:T(8,128)S(1)}, u32[]{:S(2)}, u32[]{:S(2)}) collective-permute-start(f32[2,17,8,128]{3,2,1,0:T(8,128)S(1)} %collective-permute-done.2.refs_2_), channel_id=1, source_target_pairs={{0,16},{1,17},{2,18},{3,19},{4,20},{5,21},{6,22},{7,23},{8,24},{9,... | collective-permute-start | bytes 417800 | tf_op jit(solution)/shard_map/ppermute | solution.py:743
  11.7 0.0 collective-permute-done.refs_1_
  11.7 1.0 %collective-permute-done.3.refs_3_ = f32[2,17,8,128]{3,2,1,0:T(8,128)S(1)} collective-permute-done((f32[2,17,8,128]{3,2,1,0:T(8,128)S(1)}, f32[2,17,8,128]{3,2,1,0:T(8,128)S(1)}, u32[]{:S(2)}, u32[]{:S(2)}) %collective-permute-start.3) | collective-permute-done | bytes 139296 | tf_op jit(solution)/shard_map/ppermute | solution.py:743
  12.7 0.9 %shard_map.87 = f32[8,8,128]{2,1,0:T(8,128)S(1)} custom-call(s32[2]{0:T(128)S(1)} %pad_add_fusion.flags, f32[57,8,128]{2,1,0:T(8,128)S(1)} %get-tuple-element.24.refs_0_.whole, f32[57,8,128]{2,1,0:T(8,128)S(1)} %collective-permute-done.refs_1_, f32[2,17,8,128]{3,2,1,0:T(8,128)S(1)} %collective-permute-done.2.refs_2_, ...), custom_call_target="tpu_custom_call" | custom-call | tf_op jit(solution)/shard_map/pallas_call | solution.py:720
  13.7 1.8 %collective-permute-start.4 = (f32[8,8,128]{2,1,0:T(8,128)S(1)}, f32[8,8,128]{2,1,0:T(8,128)S(1)}, u32[]{:S(2)}, u32[]{:S(2)}) collective-permute-start(f32[8,8,128]{2,1,0:T(8,128)S(1)} %shard_map.87), channel_id=1, source_target_pairs={{0,1},{1,0},{2,3},{3,2},{4,5},{5,4},{6,7},{7,6},{8,9},{9,8},{10,11... | collective-permute-start | bytes 98312 | tf_op jit(solution)/shard_map/ppermute | solution.py:743
  15.5 2.0 %shard_map.88 = (f32[38,8,128]{2,1,0:T(8,128)S(1)}, f32[6,4,128]{2,1,0:T(4,128)S(1)}) custom-call(s32[2]{0:T(128)S(1)} %pad_add_fusion.flags, f32[57,8,128]{2,1,0:T(8,128)S(1)} %get-tuple-element.24.refs_0_.whole, f32[57,8,128]{2,1,0:T(8,128)S(1)} %collective-permute-done.refs_1_, f32[2,17,8,128]{3,2,1,0:T(8,128)S(1)} %collective-permute-done.2.refs_2_, ...), custom_call_target="tpu_custom_call" | custom-call | tf_op jit(solution)/shard_map/pallas_call | solution.py:720
  17.5 0.1 collective-permute-done.4.first
  17.6 0.8 %collective-permute-start.5 = (f32[8,8,128]{2,1,0:T(8,128)S(1)}, f32[8,8,128]{2,1,0:T(8,128)S(1)}, u32[]{:S(2)}, u32[]{:S(2)}) collective-permute-start(f32[8,8,128]{2,1,0:T(8,128)S(1)} %collective-permute-done.4.first), channel_id=1, source_target_pairs={{0,16},{1,17},{2,18},{3,19},{4,20},{5,21},{6,22},{7,23},{8,24},{9,... | collective-permute-start | bytes 98312 | tf_op jit(solution)/shard_map/ppermute | solution.py:743
  18.4 1.3 %shard_map.89 = (f32[6,8,128]{2,1,0:T(8,128)S(1)}, f32[57,8,128]{2,1,0:T(8,128)S(1)}) custom-call(s32[2]{0:T(128)S(1)} %pad_add_fusion.flags, f32[57,8,128]{2,1,0:T(8,128)S(1)} %get-tuple-element.24.refs_0_.whole, f32[57,8,128]{2,1,0:T(8,128)S(1)} %collective-permute-done.refs_1_, f32[2,17,8,128]{3,2,1,0:T(8,128)S(1)} %collective-permute-done.2.refs_2_, ...), custom_call_target="tpu_custom_call" | custom-call | tf_op jit(solution)/shard_map/pallas_call | solution.py:720
  19.7 0.0 collective-permute-done.5.second
  19.7 2.2 %shard_map.90 = (f32[19,2,4,256]{3,2,1,0:T(4,128)}, f32[6,2,1,2,128]{4,3,2,1,0:T(2,128)}) custom-call(s32[2]{0:T(128)S(1)} %pad_add_fusion.flags, f32[57,8,128]{2,1,0:T(8,128)S(1)} %get-tuple-element.24.refs_0_.whole, f32[38,8,128]{2,1,0:T(8,128)S(1)} %get-tuple-element.29.bulk_pops, f32[6,4,128]{2,1,0:T(4,128)S(1)} %get-tuple-element.30.bulk_loads, ...), custom_call_target="tpu_custom_call" | custom-call | tf_op jit(solution)/shard_map/pallas_call | solution.py:720
  (1 shorter events, 0.0 us)
Async XLA Ops:
  2.4 1.4 %collective-permute-start.1 = (f32[17,8,128]{2,1,0:T(8,128)S(1)}, f32[17,8,128]{2,1,0:T(8,128)S(1)}, u32[]{:S(2)}, u32[]{:S(2)}) collective-permute-start(f32[17,8,128]{2,1,0:T(8,128)S(1)} %get-tuple-element.26), channel_id=1, source_target_pairs={{0,16},{1,17},{2,18},{3,19},{4,20},{5,21},{6,22},{7,23},{8,24},{9,... | collective-permute-start | bytes 208904 | tf_op jit(solution)/shard_map/ppermute | solution.py:743
  3.9 6.0 %collective-permute-start.2 = (f32[2,17,8,128]{3,2,1,0:T(8,128)S(1)}, f32[2,17,8,128]{3,2,1,0:T(8,128)S(1)}, u32[]{:S(2)}, u32[]{:S(2)}) collective-permute-start(f32[2,17,8,128]{3,2,1,0:T(8,128)S(1)} %bitcast_dynamic-update-slice_fusion), channel_id=1, source_target_pairs={{0,4},{1,5},{2,6},{3,7},{4,0},{5,1},{6,2},{7,3},{8,12},{9,13},{10,... | collective-permute-start | bytes 417800 | tf_op jit(solution)/shard_map/ppermute | solution.py:743
  6.8 4.9 %collective-permute-start = (f32[57,8,128]{2,1,0:T(8,128)S(1)}, f32[57,8,128]{2,1,0:T(8,128)S(1)}, u32[]{:S(2)}, u32[]{:S(2)}) collective-permute-start(f32[57,8,128]{2,1,0:T(8,128)S(1)} %get-tuple-element.24.refs_0_.whole), channel_id=1, source_target_pairs={{0,16},{1,17},{2,18},{3,19},{4,20},{5,21},{6,22},{7,23},{8,24},{9,... | collective-permute-start | bytes 700424 | tf_op jit(solution)/shard_map/ppermute | solution.py:743
  9.8 2.9 %collective-permute-start.3 = (f32[2,17,8,128]{3,2,1,0:T(8,128)S(1)}, f32[2,17,8,128]{3,2,1,0:T(8,128)S(1)}, u32[]{:S(2)}, u32[]{:S(2)}) collective-permute-start(f32[2,17,8,128]{3,2,1,0:T(8,128)S(1)} %collective-permute-done.2.refs_2_), channel_id=1, source_target_pairs={{0,16},{1,17},{2,18},{3,19},{4,20},{5,21},{6,22},{7,23},{8,24},{9,... | collective-permute-start | bytes 417800 | tf_op jit(solution)/shard_map/ppermute | solution.py:743
  13.7 4.0 %collective-permute-start.4 = (f32[8,8,128]{2,1,0:T(8,128)S(1)}, f32[8,8,128]{2,1,0:T(8,128)S(1)}, u32[]{:S(2)}, u32[]{:S(2)}) collective-permute-start(f32[8,8,128]{2,1,0:T(8,128)S(1)} %shard_map.87), channel_id=1, source_target_pairs={{0,1},{1,0},{2,3},{3,2},{4,5},{5,4},{6,7},{7,6},{8,9},{9,8},{10,11... | collective-permute-start | bytes 98312 | tf_op jit(solution)/shard_map/ppermute | solution.py:743
  17.6 2.0 %collective-permute-start.5 = (f32[8,8,128]{2,1,0:T(8,128)S(1)}, f32[8,8,128]{2,1,0:T(8,128)S(1)}, u32[]{:S(2)}, u32[]{:S(2)}) collective-permute-start(f32[8,8,128]{2,1,0:T(8,128)S(1)} %collective-permute-done.4.first), channel_id=1, source_target_pairs={{0,16},{1,17},{2,18},{3,19},{4,20},{5,21},{6,22},{7,23},{8,24},{9,... | collective-permute-start | bytes 98312 | tf_op jit(solution)/shard_map/ppermute | solution.py:743

commit v4 on v3

--- a/solution.py
+++ b/solution.py
@@ -42,6 +42,13 @@
 F32 = jnp.float32
 
 
+def end_flags(sides):
+    if sides is not None:
+        return sides
+    ix, iy, iz = [lax.axis_index(axis) for axis in ("gx", "gy", "gz")]
+    return 1 - lax.rem(ix + iy, 2), 1 - lax.rem(ix + iz, 2)
+
+
 def iota(shape, dim):
     return lax.broadcasted_iota(jnp.int32, shape, dim)
 
@@ -63,7 +70,8 @@
     ]
 
 
-def pack_kernel(flags, *refs):
+def pack_kernel(sides, *refs):
+    flags = end_flags(sides)
     sources, (whole, mine, theirs), held, sems = refs[:7], refs[7:10], refs[10:17], refs[17]
     copies = [
         pltpu.make_async_copy(source, target, sems.at[n])
@@ -220,7 +228,8 @@
     return jnp.where(masks[0], values[0], jnp.where(masks[1], values[1], 0.0))
 
 
-def z_pack_kernel(groups, paired, flags, *refs):
+def z_pack_kernel(groups, paired, sides, *refs):
+    flags = end_flags(sides)
     wholes, (first, second, out, held) = refs[:groups], refs[groups:]
     store_ends(groups, paired, flags[0], first, second, held)
     high = flags[1] == 1
@@ -396,7 +405,8 @@
 AT_LAYER = {0: 0, 1: 1, 2: 2, -1: 3}
 
 
-def bulk_kernel(groups, paired, flags, *refs):
+def bulk_kernel(groups, paired, sides, *refs):
+    flags = end_flags(sides)
     layers = 2 * groups
     wholes, (y_first, y_second) = refs[:groups], refs[groups : groups + 2]
     out_pops, out_loads = refs[groups + 2 : groups + 4]
@@ -507,7 +517,8 @@
             out_loads[f, 2 * s : 2 * s + 2, :] = both
 
 
-def side_kernel(groups, paired, flags, *refs):
+def side_kernel(groups, paired, sides, *refs):
+    flags = end_flags(sides)
     layers = 2 * groups
     wholes, (y_first, y_second) = refs[:groups], refs[groups : groups + 2]
     out_contact, out_edge, held = refs[groups + 2 :]
@@ -584,10 +595,10 @@
 
 
 def edge_kernel(
-    groups, paired, flags, whole, bulk_pops, bulk_loads, bulk_contact, edge, first, second, *refs
+    groups, paired, sides, whole, bulk_pops, bulk_loads, bulk_contact, edge, first, second, *refs
 ):
     final_pops, final_loads, held, out_pops, out_loads, sems = refs
-    side = flags[1]
+    side = end_flags(sides)[1]
     for tile in range(Z_TILES):
         held[side, tile] = first[tile]
         value = second[tile]
@@ -712,19 +723,18 @@
         copy.wait()
 
 
-SMEM = pl.BlockSpec(memory_space=pltpu.SMEM)
 PARAMS = pltpu.CompilerParams(vmem_limit_bytes=32 * 2**20)
 
 
-def call(kernel, flags, operands, shapes, scratch=(), spaces=(pltpu.VMEM, pltpu.VMEM)):
+def call(kernel, operands, shapes, scratch=(), spaces=(pltpu.VMEM, pltpu.VMEM)):
     return pl.pallas_call(
         kernel,
         out_shape=[jax.ShapeDtypeStruct(shape, F32) for shape in shapes],
-        in_specs=[SMEM] + [pl.BlockSpec(memory_space=spaces[0])] * len(operands),
+        in_specs=[pl.BlockSpec(memory_space=spaces[0])] * len(operands),
         out_specs=[pl.BlockSpec(memory_space=spaces[1])] * len(shapes),
         scratch_shapes=[pltpu.VMEM(x, F32) if isinstance(x, tuple) else x for x in scratch],
         compiler_params=PARAMS,
-    )(flags, *operands)
+    )(*operands)
 
 
 def step(paired, sizes, *blocks):
@@ -754,25 +764,20 @@
     ends_y = (Y_BLOCKS, 8, 128)
     shape_z = (Z_TILES, 8, 128)
     shape_y = (groups,) + ends_y
-    if paired:
-        ix, iy, iz = [lax.axis_index(axis) for axis in axes]
-        flags = jnp.stack([1 - (ix + iy) % 2, 1 - (ix + iz) % 2]).astype(jnp.int32)
-    else:
-        flags = jnp.ones((2,), jnp.int32)
+    sides = None if paired else (1, 1)
     held = [pltpu.VMEM(block.shape, block.dtype) for block in blocks]
     blocks = [pltpu.with_memory_space_constraint(block, pltpu.HBM) for block in blocks]
     whole, mine, theirs = call(
-        pack_kernel,
-        flags,
+        functools.partial(pack_kernel, sides),
         blocks,
         [(W_BLOCKS, 8, 128), shape_y, ends_y],
         held + [pltpu.SemaphoreType.DMA((7,))],
         (pltpu.HBM, pltpu.VMEM),
     )
 
-    def pack_z(flags, wholes, halos):
-        kernel = functools.partial(z_pack_kernel, groups, paired)
-        return call(kernel, flags, wholes + halos, [shape_z], [(2,) + shape_y])[0]
+    def pack_z(sides, wholes, halos):
+        kernel = functools.partial(z_pack_kernel, groups, paired, sides)
+        return call(kernel, wholes + halos, [shape_z], [(2,) + shape_y])[0]
 
     def pack_bulk(wholes, halos):
         scratch = [
@@ -783,8 +788,7 @@
             (3, 4, 8, 256),
         ]
         return call(
-            functools.partial(bulk_kernel, groups, paired),
-            flags,
+            functools.partial(bulk_kernel, groups, paired, sides),
             wholes + halos,
             [(W_GRAIN, 8, 128), (6, 4, 128)],
             scratch,
@@ -796,7 +800,7 @@
         first = permute(rows, lambda x, y, z: (x, y + (1 if (x + y) % 2 == 0 else -1), z))
         halos = [first, swap(first)]
         first = permute(
-            pack_z(flags, wholes, halos),
+            pack_z(sides, wholes, halos),
             lambda x, y, z: (x, y, z + (1 if (x + z) % 2 == 0 else -1)),
         )
         bulk = pack_bulk(wholes, halos)
@@ -809,15 +813,14 @@
             permute(down, lambda x, y, z: (x, y - 1, z)),
             permute(up, lambda x, y, z: (x, y + 1, z)),
         ]
-        low = jnp.array([1, 0], jnp.int32)
+        low = (1, 0)
         ends = [
             permute(pack_z(low, wholes, halos), lambda x, y, z: (x, y, z - 1)),
-            permute(pack_z(flags, wholes, halos), lambda x, y, z: (x, y, z + 1)),
+            permute(pack_z(sides, wholes, halos), lambda x, y, z: (x, y, z + 1)),
         ]
         bulk = pack_bulk(wholes, halos)
     side = call(
-        functools.partial(side_kernel, groups, paired),
-        flags,
+        functools.partial(side_kernel, groups, paired, sides),
         wholes + halos,
         [(6, 8, 128), (EDGE_VALUES, 8, 128)],
         [(2,) + shape_y],
@@ -826,8 +829,7 @@
     shapes = [populations.shape, (6,) + offset.shape[1:]]
     return tuple(
         call(
-            functools.partial(edge_kernel, groups, paired),
-            flags,
+            functools.partial(edge_kernel, groups, paired, sides),
             [whole] + list(bulk) + list(side) + ends,
             shapes,
             [(2,) + shape_z] + shapes + [pltpu.SemaphoreType.DMA((len(PARTS) + 1,))],

time: 22 us -> 19.5 us (0.89)
  Pallas kernels: 8.07 us -> 5.44 us
  waiting for transfers between devices: 3.18 us -> 3.94 us
  starting transfers between devices: 9.82 us -> 9.28 us
    pallas_call x5, Pallas kernels: 8.07 us -> 5.44 us  [call(): pl.pallas_call(kernel, out_shape=[jax.ShapeDtypeStruct(shape, F32) for sh...]
    ppermute x6, waiting for transfers between devices: 3.18 us -> 3.94 us  [permute(): return lax.ppermute(value, axes, pairs)]
    ppermute x6, starting transfers between devices: 9.82 us -> 9.28 us  [permute(): return lax.ppermute(value, axes, pairs)]
  transfers between devices with their start and end apart: 6 -> 6, of which waited for: 4 -> 5; matrix products, arithmetic and copies ran while one was open for 0% -> 0% of each run, Pallas kernels for 15% -> 11%
where the time goes in v4:
time: 19.5 us; the launch traced here: 19.3 us
  starting transfers between devices  9.28 us (48%)
  Pallas kernels  5.44 us (28%)
  waiting for transfers between devices  3.94 us (20%)
  between operations  0.67 us (3%)
    ppermute x6, starting transfers between devices, permute(): return lax.ppermute(value, axes, pairs)  9.28 us
    pallas_call x5, Pallas kernels, call(): pl.pallas_call(kernel, out_shape=[jax.ShapeDtypeStruct(shape, F32) for sh...  5.44 us
    ppermute x6, waiting for transfers between devices, permute(): return lax.ppermute(value, axes, pairs)  3.94 us
  transfers between devices with their start and end apart: 6, of which 5 were waited for; matrix products, arithmetic and copies ran while one was open for 0% of the time, Pallas kernels for 11%

profile of v4, /device:TPU:0, one launch (start us, length us, event | category | flops | bytes accessed | tf_op | source)
XLA Modules:
  0.0 19.3 jit_solution(1568321748615531878)
XLA Ops:
  0.6 1.1 %shard_map.86 = (f32[57,8,128]{2,1,0:T(8,128)S(1)}, f32[2,17,8,128]{3,2,1,0:T(8,128)S(1)}, f32[17,8,128]{2,1,0:T(8,128)S(1)}) custom-call(f32[19,2,4,256]{3,2,1,0:T(4,128)} %refs_0_.1, s32[2,1,2,128]{3,2,1,0:T(2,128)} %refs_1_.1, f32[3,2,1,2,128]{4,3,2,1,0:T(2,128)} %refs_2_.1, f32[2,1,2,128]{3,2,1,0:T(2,128)} %refs_3_.1, f32[3,2,1,2,128]{4,3,2,1,0:T(2,128)} %refs_4_.1, ...), custom_call_target="tpu_custom_call" | custom-call | tf_op jit(solution)/shard_map/pallas_call | solution.py:730
  1.8 0.5 %collective-permute-start.1 = (f32[17,8,128]{2,1,0:T(8,128)S(1)}, f32[17,8,128]{2,1,0:T(8,128)S(1)}, u32[]{:S(2)}, u32[]{:S(2)}) collective-permute-start(f32[17,8,128]{2,1,0:T(8,128)S(1)} %get-tuple-element.26), channel_id=1, source_target_pairs={{0,16},{1,17},{2,18},{3,19},{4,20},{5,21},{6,22},{7,23},{8,24},{9,... | collective-permute-start | bytes 208904 | tf_op jit(solution)/shard_map/ppermute | solution.py:753
  2.3 0.9 %collective-permute-done.1 = f32[17,8,128]{2,1,0:T(8,128)S(1)} collective-permute-done((f32[17,8,128]{2,1,0:T(8,128)S(1)}, f32[17,8,128]{2,1,0:T(8,128)S(1)}, u32[]{:S(2)}, u32[]{:S(2)}) %collective-permute-start.1) | collective-permute-done | bytes 69664 | tf_op jit(solution)/shard_map/ppermute | solution.py:753
  3.2 2.9 %collective-permute-start.2 = (f32[2,17,8,128]{3,2,1,0:T(8,128)S(1)}, f32[2,17,8,128]{3,2,1,0:T(8,128)S(1)}, u32[]{:S(2)}, u32[]{:S(2)}) collective-permute-start(f32[2,17,8,128]{3,2,1,0:T(8,128)S(1)} %bitcast_dynamic-update-slice_fusion), channel_id=1, source_target_pairs={{0,4},{1,5},{2,6},{3,7},{4,0},{5,1},{6,2},{7,3},{8,12},{9,13},{10,... | collective-permute-start | bytes 417800 | tf_op jit(solution)/shard_map/ppermute | solution.py:753
  6.1 1.9 %collective-permute-start = (f32[57,8,128]{2,1,0:T(8,128)S(1)}, f32[57,8,128]{2,1,0:T(8,128)S(1)}, u32[]{:S(2)}, u32[]{:S(2)}) collective-permute-start(f32[57,8,128]{2,1,0:T(8,128)S(1)} %get-tuple-element.24.refs_0_.whole), channel_id=1, source_target_pairs={{0,16},{1,17},{2,18},{3,19},{4,20},{5,21},{6,22},{7,23},{8,24},{9,... | collective-permute-start | bytes 700424 | tf_op jit(solution)/shard_map/ppermute | solution.py:753
  8.0 1.1 %collective-permute-done.2.refs_2_ = f32[2,17,8,128]{3,2,1,0:T(8,128)S(1)} collective-permute-done((f32[2,17,8,128]{3,2,1,0:T(8,128)S(1)}, f32[2,17,8,128]{3,2,1,0:T(8,128)S(1)}, u32[]{:S(2)}, u32[]{:S(2)}) %collective-permute-start.2) | collective-permute-done | bytes 139296 | tf_op jit(solution)/shard_map/ppermute | solution.py:753
  9.2 1.9 %collective-permute-start.3 = (f32[2,17,8,128]{3,2,1,0:T(8,128)S(1)}, f32[2,17,8,128]{3,2,1,0:T(8,128)S(1)}, u32[]{:S(2)}, u32[]{:S(2)}) collective-permute-start(f32[2,17,8,128]{3,2,1,0:T(8,128)S(1)} %collective-permute-done.2.refs_2_), channel_id=1, source_target_pairs={{0,16},{1,17},{2,18},{3,19},{4,20},{5,21},{6,22},{7,23},{8,24},{9,... | collective-permute-start | bytes 417800 | tf_op jit(solution)/shard_map/ppermute | solution.py:753
  11.1 0.0 collective-permute-done.refs_1_
  11.1 1.0 %collective-permute-done.3.refs_3_ = f32[2,17,8,128]{3,2,1,0:T(8,128)S(1)} collective-permute-done((f32[2,17,8,128]{3,2,1,0:T(8,128)S(1)}, f32[2,17,8,128]{3,2,1,0:T(8,128)S(1)}, u32[]{:S(2)}, u32[]{:S(2)}) %collective-permute-start.3) | collective-permute-done | bytes 139296 | tf_op jit(solution)/shard_map/ppermute | solution.py:753
  12.1 0.5 %shard_map.87 = f32[8,8,128]{2,1,0:T(8,128)S(1)} custom-call(f32[57,8,128]{2,1,0:T(8,128)S(1)} %get-tuple-element.24.refs_0_.whole, f32[57,8,128]{2,1,0:T(8,128)S(1)} %collective-permute-done.refs_1_, f32[2,17,8,128]{3,2,1,0:T(8,128)S(1)} %collective-permute-done.2.refs_2_, f32[2,17,8,128]{3,2,1,0:T(8,128)S(1)} %collective-permute-done.3.refs_3_), custom_call_target="tpu_custom_call" | custom-call | tf_op jit(solution)/shard_map/pallas_call | solution.py:730
  12.5 1.8 %collective-permute-start.4 = (f32[8,8,128]{2,1,0:T(8,128)S(1)}, f32[8,8,128]{2,1,0:T(8,128)S(1)}, u32[]{:S(2)}, u32[]{:S(2)}) collective-permute-start(f32[8,8,128]{2,1,0:T(8,128)S(1)} %shard_map.87), channel_id=1, source_target_pairs={{0,1},{1,0},{2,3},{3,2},{4,5},{5,4},{6,7},{7,6},{8,9},{9,8},{10,11... | collective-permute-start | bytes 98312 | tf_op jit(solution)/shard_map/ppermute | solution.py:753
  14.4 1.4 %shard_map.88 = (f32[38,8,128]{2,1,0:T(8,128)S(1)}, f32[6,4,128]{2,1,0:T(4,128)S(1)}) custom-call(f32[57,8,128]{2,1,0:T(8,128)S(1)} %get-tuple-element.24.refs_0_.whole, f32[57,8,128]{2,1,0:T(8,128)S(1)} %collective-permute-done.refs_1_, f32[2,17,8,128]{3,2,1,0:T(8,128)S(1)} %collective-permute-done.2.refs_2_, ...), custom_call_target="tpu_custom_call" | custom-call | tf_op jit(solution)/shard_map/pallas_call | solution.py:730
  15.8 0.7 %collective-permute-done.4.first = f32[8,8,128]{2,1,0:T(8,128)S(1)} collective-permute-done((f32[8,8,128]{2,1,0:T(8,128)S(1)}, f32[8,8,128]{2,1,0:T(8,128)S(1)}, u32[]{:S(2)}, u32[]{:S(2)}) %collective-permute-start.4) | collective-permute-done | bytes 32800 | tf_op jit(solution)/shard_map/ppermute | solution.py:753
  16.5 0.2 %collective-permute-start.5 = (f32[8,8,128]{2,1,0:T(8,128)S(1)}, f32[8,8,128]{2,1,0:T(8,128)S(1)}, u32[]{:S(2)}, u32[]{:S(2)}) collective-permute-start(f32[8,8,128]{2,1,0:T(8,128)S(1)} %collective-permute-done.4.first), channel_id=1, source_target_pairs={{0,16},{1,17},{2,18},{3,19},{4,20},{5,21},{6,22},{7,23},{8,24},{9,... | collective-permute-start | bytes 98312 | tf_op jit(solution)/shard_map/ppermute | solution.py:753
  16.7 0.8 %shard_map.89 = (f32[6,8,128]{2,1,0:T(8,128)S(1)}, f32[57,8,128]{2,1,0:T(8,128)S(1)}) custom-call(f32[57,8,128]{2,1,0:T(8,128)S(1)} %get-tuple-element.24.refs_0_.whole, f32[57,8,128]{2,1,0:T(8,128)S(1)} %collective-permute-done.refs_1_, f32[2,17,8,128]{3,2,1,0:T(8,128)S(1)} %collective-permute-done.2.refs_2_, ...), custom_call_target="tpu_custom_call" | custom-call | tf_op jit(solution)/shard_map/pallas_call | solution.py:730
  17.5 0.2 %collective-permute-done.5.second = f32[8,8,128]{2,1,0:T(8,128)S(1)} collective-permute-done((f32[8,8,128]{2,1,0:T(8,128)S(1)}, f32[8,8,128]{2,1,0:T(8,128)S(1)}, u32[]{:S(2)}, u32[]{:S(2)}) %collective-permute-start.5) | collective-permute-done | bytes 32800 | tf_op jit(solution)/shard_map/ppermute | solution.py:753
  17.7 1.6 %shard_map.90 = (f32[19,2,4,256]{3,2,1,0:T(4,128)}, f32[6,2,1,2,128]{4,3,2,1,0:T(2,128)}) custom-call(f32[57,8,128]{2,1,0:T(8,128)S(1)} %get-tuple-element.24.refs_0_.whole, f32[38,8,128]{2,1,0:T(8,128)S(1)} %get-tuple-element.29.bulk_pops, f32[6,4,128]{2,1,0:T(4,128)S(1)} %get-tuple-element.30.bulk_loads, f32[6,8,128]{2,1,0:T(8,128)S(1)} %get-tuple-element.31.bulk_contact, ...), custom_call_target="tpu_custom_call" | custom-call | tf_op jit(solution)/shard_map/pallas_call | solution.py:730
  (1 shorter events, 0.0 us)
Async XLA Ops:
  1.8 1.4 %collective-permute-start.1 = (f32[17,8,128]{2,1,0:T(8,128)S(1)}, f32[17,8,128]{2,1,0:T(8,128)S(1)}, u32[]{:S(2)}, u32[]{:S(2)}) collective-permute-start(f32[17,8,128]{2,1,0:T(8,128)S(1)} %get-tuple-element.26), channel_id=1, source_target_pairs={{0,16},{1,17},{2,18},{3,19},{4,20},{5,21},{6,22},{7,23},{8,24},{9,... | collective-permute-start | bytes 208904 | tf_op jit(solution)/shard_map/ppermute | solution.py:753
  3.2 6.0 %collective-permute-start.2 = (f32[2,17,8,128]{3,2,1,0:T(8,128)S(1)}, f32[2,17,8,128]{3,2,1,0:T(8,128)S(1)}, u32[]{:S(2)}, u32[]{:S(2)}) collective-permute-start(f32[2,17,8,128]{3,2,1,0:T(8,128)S(1)} %bitcast_dynamic-update-slice_fusion), channel_id=1, source_target_pairs={{0,4},{1,5},{2,6},{3,7},{4,0},{5,1},{6,2},{7,3},{8,12},{9,13},{10,... | collective-permute-start | bytes 417800 | tf_op jit(solution)/shard_map/ppermute | solution.py:753
  6.1 4.9 %collective-permute-start = (f32[57,8,128]{2,1,0:T(8,128)S(1)}, f32[57,8,128]{2,1,0:T(8,128)S(1)}, u32[]{:S(2)}, u32[]{:S(2)}) collective-permute-start(f32[57,8,128]{2,1,0:T(8,128)S(1)} %get-tuple-element.24.refs_0_.whole), channel_id=1, source_target_pairs={{0,16},{1,17},{2,18},{3,19},{4,20},{5,21},{6,22},{7,23},{8,24},{9,... | collective-permute-start | bytes 700424 | tf_op jit(solution)/shard_map/ppermute | solution.py:753
  9.2 2.9 %collective-permute-start.3 = (f32[2,17,8,128]{3,2,1,0:T(8,128)S(1)}, f32[2,17,8,128]{3,2,1,0:T(8,128)S(1)}, u32[]{:S(2)}, u32[]{:S(2)}) collective-permute-start(f32[2,17,8,128]{3,2,1,0:T(8,128)S(1)} %collective-permute-done.2.refs_2_), channel_id=1, source_target_pairs={{0,16},{1,17},{2,18},{3,19},{4,20},{5,21},{6,22},{7,23},{8,24},{9,... | collective-permute-start | bytes 417800 | tf_op jit(solution)/shard_map/ppermute | solution.py:753
  12.5 4.0 %collective-permute-start.4 = (f32[8,8,128]{2,1,0:T(8,128)S(1)}, f32[8,8,128]{2,1,0:T(8,128)S(1)}, u32[]{:S(2)}, u32[]{:S(2)}) collective-permute-start(f32[8,8,128]{2,1,0:T(8,128)S(1)} %shard_map.87), channel_id=1, source_target_pairs={{0,1},{1,0},{2,3},{3,2},{4,5},{5,4},{6,7},{7,6},{8,9},{9,8},{10,11... | collective-permute-start | bytes 98312 | tf_op jit(solution)/shard_map/ppermute | solution.py:753
  16.5 1.2 %collective-permute-start.5 = (f32[8,8,128]{2,1,0:T(8,128)S(1)}, f32[8,8,128]{2,1,0:T(8,128)S(1)}, u32[]{:S(2)}, u32[]{:S(2)}) collective-permute-start(f32[8,8,128]{2,1,0:T(8,128)S(1)} %collective-permute-done.4.first), channel_id=1, source_target_pairs={{0,16},{1,17},{2,18},{3,19},{4,20},{5,21},{6,22},{7,23},{8,24},{9,... | collective-permute-start | bytes 98312 | tf_op jit(solution)/shard_map/ppermute | solution.py:753

commit v5 on v4

--- a/solution.py
+++ b/solution.py
@@ -37,7 +37,9 @@
 POPS_AT, CODE_AT, EDGE_VALUES = 36, 55, 57
 Z_TILES, CONTACT_TILE = 8, 7
 Y_FIELDS = list(range(9)) + [RADIUS, CODE]
-Y_GRAIN, Y_BLOCKS = 76, 17
+Y_MEMBERS = [m for m in range(19) if VELOCITIES[m][1]] + [19, 20, 21]
+Y_STANDS = {0: 10, 1: 11, 5: 12}
+Y_GRAIN, Y_BLOCKS = 52, 14
 W_GRAIN, W_BLOCKS = 38, 57
 F32 = jnp.float32
 
@@ -75,12 +77,15 @@
     sources, (whole, mine, theirs), held, sems = refs[:7], refs[7:10], refs[10:17], refs[17]
     copies = [
         pltpu.make_async_copy(source, target, sems.at[n])
-        for n, (source, target) in enumerate(zip(sources, held))
+        for n, (source, target) in enumerate(zip(sources[1:], held[1:]))
     ]
-    for copy in copies[1:] + copies[:1]:
+    for n, part in enumerate(POPS_PARTS):
+        part = pl.ds(*part)
+        copies.append(pltpu.make_async_copy(sources[0].at[part], held[0].at[part], sems.at[6 + n]))
+    for copy in copies:
         copy.start()
     pops, cell, off, rad, vel, spin, inter = held
-    for copy in copies[1:]:
+    for copy in copies[:6]:
         copy.wait()
 
     def slot(s, field, rows=slice(None)):
@@ -110,14 +115,26 @@
                     value = inter[9 * kx + 3 * (q + end) + kz, s, 0, pl.ds(end, 1), :]
                 r = Y_GRAIN + 2 * f + s
                 out[r // 8, r % 8 : r % 8 + 1, :] = value
-        out[16, 6:8, :] = jnp.zeros((2, 128), F32)
-    copies[0].wait()
+        out[Y_BLOCKS - 1, 6:8, :] = jnp.zeros((2, 128), F32)
+    for copy in copies[6:]:
+        copy.wait()
+    still = [m for m in range(19) if not VELOCITIES[m][1]]
+    for i in range(2):
+        sums = []
+        for c in (0, 2):
+            rising = [pops[m, i] for m in still if VELOCITIES[m][c] > 0]
+            falling = [pops[m, i] for m in still if VELOCITIES[m][c] < 0]
+            sums.append(sum(rising[1:], rising[0]) - sum(falling[1:], falling[0]))
+        total = sum([pops[m, i] for m in still[1:]], pops[0, i])
+        pops[19, i] = total - sums[0] - sums[1]
+        pops[20, i] = sums[0]
+        pops[21, i] = sums[1]
     for out, end in ((mine.at[0], flags[0]), (theirs, 1 - flags[0])):
-        for member in range(19):
+        for n, member in enumerate(Y_MEMBERS):
             for i in range(2):
                 row = pops[member, i, pl.ds(3 * end, 1), :]
                 for t in range(2):
-                    r = 4 * member + 2 * i + t
+                    r = 4 * n + 2 * i + t
                     out[r // 8, r % 8 : r % 8 + 1, :] = row[:, 128 * t : 128 * t + 128]
     for member in range(19):
         for i in range(2):
@@ -138,7 +155,13 @@
         return self.whole[2 * member + i, 4 * t : 4 * t + 4, :]
 
     def halo_pops(self, end, member, i, t):
-        r = 4 * member + 2 * i + t
+        if VELOCITIES[member][1]:
+            n = Y_MEMBERS.index(member)
+        elif member in Y_STANDS:
+            n = Y_STANDS[member]
+        else:
+            return jnp.zeros((1, 128), F32)
+        r = 4 * n + 2 * i + t
         return self.halos[end, self.group, r // 8, r % 8 : r % 8 + 1, :]
 
     def halo_slot(self, end, s, field):
@@ -401,6 +424,7 @@
     return place, [rows(RADIUS)] + [rows(c) for c in range(6)]
 
 
+POPS_PARTS = [(0, 5), (5, 5), (10, 5), (15, 4)]
 PARTS = [4, 9, 14, 18]
 AT_LAYER = {0: 0, 1: 1, 2: 2, -1: 3}
 
@@ -766,12 +790,13 @@
     shape_y = (groups,) + ends_y
     sides = None if paired else (1, 1)
     held = [pltpu.VMEM(block.shape, block.dtype) for block in blocks]
+    held[0] = pltpu.VMEM((22,) + blocks[0].shape[1:], F32)
     blocks = [pltpu.with_memory_space_constraint(block, pltpu.HBM) for block in blocks]
     whole, mine, theirs = call(
         functools.partial(pack_kernel, sides),
         blocks,
         [(W_BLOCKS, 8, 128), shape_y, ends_y],
-        held + [pltpu.SemaphoreType.DMA((7,))],
+        held + [pltpu.SemaphoreType.DMA((6 + len(POPS_PARTS),))],
         (pltpu.HBM, pltpu.VMEM),
     )
 

time: 19.5 us -> 18.8 us (0.964)
  starting transfers between devices: 9.28 us -> 7.18 us
  waiting for transfers between devices: 3.94 us -> 5.51 us
    ppermute x6, starting transfers between devices: 9.28 us -> 7.18 us  [permute(): return lax.ppermute(value, axes, pairs)]
    ppermute x6, waiting for transfers between devices: 3.94 us -> 5.51 us  [permute(): return lax.ppermute(value, axes, pairs)]
  transfers between devices with their start and end apart: 6 -> 6, of which waited for: 5 -> 5; matrix products, arithmetic and copies ran while one was open for 0% -> 0% of each run, Pallas kernels for 11% -> 12%
where the time goes in v5:
time: 18.8 us; the launch traced here: 18.7 us
  starting transfers between devices  7.18 us (38%)
  waiting for transfers between devices  5.51 us (29%)
  Pallas kernels  5.31 us (28%)
  between operations  0.67 us (4%)
    ppermute x6, starting transfers between devices, permute(): return lax.ppermute(value, axes, pairs)  7.18 us
    ppermute x6, waiting for transfers between devices, permute(): return lax.ppermute(value, axes, pairs)  5.51 us
    pallas_call x5, Pallas kernels, call(): pl.pallas_call(kernel, out_shape=[jax.ShapeDtypeStruct(shape, F32) for sh...  5.31 us
  transfers between devices with their start and end apart: 6, of which 5 were waited for; matrix products, arithmetic and copies ran while one was open for 0% of the time, Pallas kernels for 12%

profile of v5, /device:TPU:0, one launch (start us, length us, event | category | flops | bytes accessed | tf_op | source)
XLA Modules:
  0.0 18.7 jit_solution(1933333490789663087)
XLA Ops:
  0.6 1.1 %shard_map.86 = (f32[57,8,128]{2,1,0:T(8,128)S(1)}, f32[2,14,8,128]{3,2,1,0:T(8,128)S(1)}, f32[14,8,128]{2,1,0:T(8,128)S(1)}) custom-call(f32[19,2,4,256]{3,2,1,0:T(4,128)} %refs_0_.1, s32[2,1,2,128]{3,2,1,0:T(2,128)} %refs_1_.1, f32[3,2,1,2,128]{4,3,2,1,0:T(2,128)} %refs_2_.1, f32[2,1,2,128]{3,2,1,0:T(2,128)} %refs_3_.1, f32[3,2,1,2,128]{4,3,2,1,0:T(2,128)} %refs_4_.1, ...), custom_call_target="tpu_custom_call" | custom-call | tf_op jit(solution)/shard_map/pallas_call | solution.py:754
  1.7 0.5 %collective-permute-start.1 = (f32[14,8,128]{2,1,0:T(8,128)S(1)}, f32[14,8,128]{2,1,0:T(8,128)S(1)}, u32[]{:S(2)}, u32[]{:S(2)}) collective-permute-start(f32[14,8,128]{2,1,0:T(8,128)S(1)} %get-tuple-element.26), channel_id=1, source_target_pairs={{0,16},{1,17},{2,18},{3,19},{4,20},{5,21},{6,22},{7,23},{8,24},{9,... | collective-permute-start | bytes 172040 | tf_op jit(solution)/shard_map/ppermute | solution.py:777
  2.3 0.1 collective-permute-start
  2.3 0.8 %collective-permute-done.1 = f32[14,8,128]{2,1,0:T(8,128)S(1)} collective-permute-done((f32[14,8,128]{2,1,0:T(8,128)S(1)}, f32[14,8,128]{2,1,0:T(8,128)S(1)}, u32[]{:S(2)}, u32[]{:S(2)}) %collective-permute-start.1) | collective-permute-done | bytes 57376 | tf_op jit(solution)/shard_map/ppermute | solution.py:777
  3.2 2.9 %collective-permute-start.2 = (f32[2,14,8,128]{3,2,1,0:T(8,128)S(1)}, f32[2,14,8,128]{3,2,1,0:T(8,128)S(1)}, u32[]{:S(2)}, u32[]{:S(2)}) collective-permute-start(f32[2,14,8,128]{3,2,1,0:T(8,128)S(1)} %bitcast_dynamic-update-slice_fusion), channel_id=1, source_target_pairs={{0,4},{1,5},{2,6},{3,7},{4,0},{5,1},{6,2},{7,3},{8,12},{9,13},{10,... | collective-permute-start | bytes 344072 | tf_op jit(solution)/shard_map/ppermute | solution.py:777
  6.1 2.8 %collective-permute-done.2.refs_2_ = f32[2,14,8,128]{3,2,1,0:T(8,128)S(1)} collective-permute-done((f32[2,14,8,128]{3,2,1,0:T(8,128)S(1)}, f32[2,14,8,128]{3,2,1,0:T(8,128)S(1)}, u32[]{:S(2)}, u32[]{:S(2)}) %collective-permute-start.2) | collective-permute-done | bytes 114720 | tf_op jit(solution)/shard_map/ppermute | solution.py:777
  8.8 1.6 %collective-permute-start.3 = (f32[2,14,8,128]{3,2,1,0:T(8,128)S(1)}, f32[2,14,8,128]{3,2,1,0:T(8,128)S(1)}, u32[]{:S(2)}, u32[]{:S(2)}) collective-permute-start(f32[2,14,8,128]{3,2,1,0:T(8,128)S(1)} %collective-permute-done.2.refs_2_), channel_id=1, source_target_pairs={{0,16},{1,17},{2,18},{3,19},{4,20},{5,21},{6,22},{7,23},{8,24},{9,... | collective-permute-start | bytes 344072 | tf_op jit(solution)/shard_map/ppermute | solution.py:777
  10.5 0.0 collective-permute-done.refs_1_
  10.5 1.0 %collective-permute-done.3.refs_3_ = f32[2,14,8,128]{3,2,1,0:T(8,128)S(1)} collective-permute-done((f32[2,14,8,128]{3,2,1,0:T(8,128)S(1)}, f32[2,14,8,128]{3,2,1,0:T(8,128)S(1)}, u32[]{:S(2)}, u32[]{:S(2)}) %collective-permute-start.3) | collective-permute-done | bytes 114720 | tf_op jit(solution)/shard_map/ppermute | solution.py:777
  11.4 0.4 %shard_map.87 = f32[8,8,128]{2,1,0:T(8,128)S(1)} custom-call(f32[57,8,128]{2,1,0:T(8,128)S(1)} %get-tuple-element.24.refs_0_.whole, f32[57,8,128]{2,1,0:T(8,128)S(1)} %collective-permute-done.refs_1_, f32[2,14,8,128]{3,2,1,0:T(8,128)S(1)} %collective-permute-done.2.refs_2_, f32[2,14,8,128]{3,2,1,0:T(8,128)S(1)} %collective-permute-done.3.refs_3_), custom_call_target="tpu_custom_call" | custom-call | tf_op jit(solution)/shard_map/pallas_call | solution.py:754
  11.8 1.8 %collective-permute-start.4 = (f32[8,8,128]{2,1,0:T(8,128)S(1)}, f32[8,8,128]{2,1,0:T(8,128)S(1)}, u32[]{:S(2)}, u32[]{:S(2)}) collective-permute-start(f32[8,8,128]{2,1,0:T(8,128)S(1)} %shard_map.87), channel_id=1, source_target_pairs={{0,1},{1,0},{2,3},{3,2},{4,5},{5,4},{6,7},{7,6},{8,9},{9,8},{10,11... | collective-permute-start | bytes 98312 | tf_op jit(solution)/shard_map/ppermute | solution.py:777
  13.7 1.4 %shard_map.88 = (f32[38,8,128]{2,1,0:T(8,128)S(1)}, f32[6,4,128]{2,1,0:T(4,128)S(1)}) custom-call(f32[57,8,128]{2,1,0:T(8,128)S(1)} %get-tuple-element.24.refs_0_.whole, f32[57,8,128]{2,1,0:T(8,128)S(1)} %collective-permute-done.refs_1_, f32[2,14,8,128]{3,2,1,0:T(8,128)S(1)} %collective-permute-done.2.refs_2_, ...), custom_call_target="tpu_custom_call" | custom-call | tf_op jit(solution)/shard_map/pallas_call | solution.py:754
  15.1 0.7 %collective-permute-done.4.first = f32[8,8,128]{2,1,0:T(8,128)S(1)} collective-permute-done((f32[8,8,128]{2,1,0:T(8,128)S(1)}, f32[8,8,128]{2,1,0:T(8,128)S(1)}, u32[]{:S(2)}, u32[]{:S(2)}) %collective-permute-start.4) | collective-permute-done | bytes 32800 | tf_op jit(solution)/shard_map/ppermute | solution.py:777
  15.8 0.2 %collective-permute-start.5 = (f32[8,8,128]{2,1,0:T(8,128)S(1)}, f32[8,8,128]{2,1,0:T(8,128)S(1)}, u32[]{:S(2)}, u32[]{:S(2)}) collective-permute-start(f32[8,8,128]{2,1,0:T(8,128)S(1)} %collective-permute-done.4.first), channel_id=1, source_target_pairs={{0,16},{1,17},{2,18},{3,19},{4,20},{5,21},{6,22},{7,23},{8,24},{9,... | collective-permute-start | bytes 98312 | tf_op jit(solution)/shard_map/ppermute | solution.py:777
  16.0 0.7 %shard_map.89 = (f32[6,8,128]{2,1,0:T(8,128)S(1)}, f32[57,8,128]{2,1,0:T(8,128)S(1)}) custom-call(f32[57,8,128]{2,1,0:T(8,128)S(1)} %get-tuple-element.24.refs_0_.whole, f32[57,8,128]{2,1,0:T(8,128)S(1)} %collective-permute-done.refs_1_, f32[2,14,8,128]{3,2,1,0:T(8,128)S(1)} %collective-permute-done.2.refs_2_, ...), custom_call_target="tpu_custom_call" | custom-call | tf_op jit(solution)/shard_map/pallas_call | solution.py:754
  16.8 0.3 %collective-permute-done.5.second = f32[8,8,128]{2,1,0:T(8,128)S(1)} collective-permute-done((f32[8,8,128]{2,1,0:T(8,128)S(1)}, f32[8,8,128]{2,1,0:T(8,128)S(1)}, u32[]{:S(2)}, u32[]{:S(2)}) %collective-permute-start.5) | collective-permute-done | bytes 32800 | tf_op jit(solution)/shard_map/ppermute | solution.py:777
  17.0 1.6 %shard_map.90 = (f32[19,2,4,256]{3,2,1,0:T(4,128)}, f32[6,2,1,2,128]{4,3,2,1,0:T(2,128)}) custom-call(f32[57,8,128]{2,1,0:T(8,128)S(1)} %get-tuple-element.24.refs_0_.whole, f32[38,8,128]{2,1,0:T(8,128)S(1)} %get-tuple-element.29.bulk_pops, f32[6,4,128]{2,1,0:T(4,128)S(1)} %get-tuple-element.30.bulk_loads, f32[6,8,128]{2,1,0:T(8,128)S(1)} %get-tuple-element.31.bulk_contact, ...), custom_call_target="tpu_custom_call" | custom-call | tf_op jit(solution)/shard_map/pallas_call | solution.py:754
  (1 shorter events, 0.0 us)
Async XLA Ops:
  1.7 1.4 %collective-permute-start.1 = (f32[14,8,128]{2,1,0:T(8,128)S(1)}, f32[14,8,128]{2,1,0:T(8,128)S(1)}, u32[]{:S(2)}, u32[]{:S(2)}) collective-permute-start(f32[14,8,128]{2,1,0:T(8,128)S(1)} %get-tuple-element.26), channel_id=1, source_target_pairs={{0,16},{1,17},{2,18},{3,19},{4,20},{5,21},{6,22},{7,23},{8,24},{9,... | collective-permute-start | bytes 172040 | tf_op jit(solution)/shard_map/ppermute | solution.py:777
  2.3 8.2 %collective-permute-start = (f32[57,8,128]{2,1,0:T(8,128)S(1)}, f32[57,8,128]{2,1,0:T(8,128)S(1)}, u32[]{:S(2)}, u32[]{:S(2)}) collective-permute-start(f32[57,8,128]{2,1,0:T(8,128)S(1)} %get-tuple-element.24.refs_0_.whole), channel_id=1, source_target_pairs={{0,16},{1,17},{2,18},{3,19},{4,20},{5,21},{6,22},{7,23},{8,24},{9,... | collective-permute-start | bytes 700424 | tf_op jit(solution)/shard_map/ppermute | solution.py:777
  3.2 5.7 %collective-permute-start.2 = (f32[2,14,8,128]{3,2,1,0:T(8,128)S(1)}, f32[2,14,8,128]{3,2,1,0:T(8,128)S(1)}, u32[]{:S(2)}, u32[]{:S(2)}) collective-permute-start(f32[2,14,8,128]{3,2,1,0:T(8,128)S(1)} %bitcast_dynamic-update-slice_fusion), channel_id=1, source_target_pairs={{0,4},{1,5},{2,6},{3,7},{4,0},{5,1},{6,2},{7,3},{8,12},{9,13},{10,... | collective-permute-start | bytes 344072 | tf_op jit(solution)/shard_map/ppermute | solution.py:777
  8.8 2.6 %collective-permute-start.3 = (f32[2,14,8,128]{3,2,1,0:T(8,128)S(1)}, f32[2,14,8,128]{3,2,1,0:T(8,128)S(1)}, u32[]{:S(2)}, u32[]{:S(2)}) collective-permute-start(f32[2,14,8,128]{3,2,1,0:T(8,128)S(1)} %collective-permute-done.2.refs_2_), channel_id=1, source_target_pairs={{0,16},{1,17},{2,18},{3,19},{4,20},{5,21},{6,22},{7,23},{8,24},{9,... | collective-permute-start | bytes 344072 | tf_op jit(solution)/shard_map/ppermute | solution.py:777
  11.8 4.0 %collective-permute-start.4 = (f32[8,8,128]{2,1,0:T(8,128)S(1)}, f32[8,8,128]{2,1,0:T(8,128)S(1)}, u32[]{:S(2)}, u32[]{:S(2)}) collective-permute-start(f32[8,8,128]{2,1,0:T(8,128)S(1)} %shard_map.87), channel_id=1, source_target_pairs={{0,1},{1,0},{2,3},{3,2},{4,5},{5,4},{6,7},{7,6},{8,9},{9,8},{10,11... | collective-permute-start | bytes 98312 | tf_op jit(solution)/shard_map/ppermute | solution.py:777
  15.8 1.2 %collective-permute-start.5 = (f32[8,8,128]{2,1,0:T(8,128)S(1)}, f32[8,8,128]{2,1,0:T(8,128)S(1)}, u32[]{:S(2)}, u32[]{:S(2)}) collective-permute-start(f32[8,8,128]{2,1,0:T(8,128)S(1)} %collective-permute-done.4.first), channel_id=1, source_target_pairs={{0,16},{1,17},{2,18},{3,19},{4,20},{5,21},{6,22},{7,23},{8,24},{9,... | collective-permute-start | bytes 98312 | tf_op jit(solution)/shard_map/ppermute | solution.py:777

commit v6 on v5

--- a/solution.py
+++ b/solution.py
@@ -424,6 +424,45 @@
     return place, [rows(RADIUS)] + [rows(c) for c in range(6)]
 
 
+def end_lanes(high, inner):
+    start = jnp.where(high, 12, 2)
+    return (inner == start) | (inner == start + 1)
+
+
+def end_contact(groups, tile, high, state):
+    lane = iota((8, 128), 1)
+    step_x, step_y = lane % 16 - 1, lane // 16 - 1
+    place, a_radius, a_speed, a_spin = state[0:3], state[3], state[4:7], state[7:10]
+    a_turn = [a_radius * value for value in a_spin]
+    before = lane_groups(groups).index(groups - 1)
+    run = 32 * jnp.where(step_x < 0, before, jnp.where(step_x == 0, 0, 1))
+    other = [None] * 10
+    for oy in (-1, 0, 1):
+        at = 2 * (oy + 1)
+        rows = jnp.concatenate([tile[at : at + 1], tile[at + 2 : at + 3]], axis=0)
+        moved = roll(rows, -16, 1)
+        rows = jnp.concatenate([rows, moved, rows, moved], axis=0)
+        for q in range(10):
+            value = pick_lanes(rows, run + q)
+            other[q] = value if oy < 0 else jnp.where(step_y == oy, value, other[q])
+    keep = (step_x < 2) & (step_y < 2)
+    gap = [
+        other[0] - place[0] + (2 * step_x).astype(F32),
+        other[1] - place[1] + (2 * step_y).astype(F32),
+        other[2] - place[2] + jnp.where(high, 2.0, -2.0),
+    ]
+    pushed, twisted = pair_force(gap, a_radius, a_speed, a_turn, other[3:], keep)
+    contact = [-value for value in pushed] + [-a_radius * value for value in twisted]
+    end = lane == jnp.where(high, 127, 0)
+    result = []
+    for value in contact:
+        value = value + roll(value, -2, 0)
+        value = value + roll(value, -1, 1) + roll(value, -2, 1)
+        value = value + roll(value, -16, 1) + roll(value, -32, 1)
+        result.append(jnp.where(end, jnp.where(high, roll(value, 127, 1), value), 0.0))
+    return result
+
+
 POPS_PARTS = [(0, 5), (5, 5), (10, 5), (15, 4)]
 PARTS = [4, 9, 14, 18]
 AT_LAYER = {0: 0, 1: 1, 2: 2, -1: 3}
@@ -544,8 +583,9 @@
 def side_kernel(groups, paired, sides, *refs):
     flags = end_flags(sides)
     layers = 2 * groups
-    wholes, (y_first, y_second) = refs[:groups], refs[groups : groups + 2]
-    out_contact, out_edge, held = refs[groups + 2 :]
+    wholes, (y_first, y_second, z_first) = refs[:groups], refs[groups : groups + 3]
+    out_contact, out_edge, out_state, held = refs[groups + 3 :]
+    high = flags[1] == 1
     store_ends(groups, paired, flags[0], y_first, y_second, held)
     block = [Block(wholes[g], held, g) for g in range(groups)]
     lane8, row8 = iota((8, 128), 1), iota((8, 128), 0)
@@ -557,21 +597,30 @@
         rows = [pick_lanes(block[g].bins(s, field), z_bin) for g in range(groups)]
         return by_group(groups, rows, lane8)
 
+    tiles = [
+        jnp.where(high, roll(z_first[tile], 10, 1), z_first[tile]) for tile in range(CONTACT_TILE)
+    ]
+    filled = end_lanes(high, inner)
+
+    def store(field, value):
+        halo = roll(tiles[field // 8], 2 - 2 * (field % 8), 1)
+        out_edge[field] = jnp.where(filled, halo, value)
+
     edge_code = cell_codes(lane8, row8)
     codes = [at_edge(s, CODE) for s in range(2)]
     for s in range(2):
         out_edge[CODE_AT + s] = codes[s]
     edge_masks = [value == edge_code for value in codes]
     for field in range(36):
-        out_edge[field] = choose(edge_masks, [at_edge(s, field) for s in range(2)])
+        store(field, choose(edge_masks, [at_edge(s, field) for s in range(2)]))
     for member in range(19):
-        tiles = []
+        near_tiles = []
         for layer in range(layers):
             near = [block[layer // 2].cells(member, layer % 2, t) for t in range(2)]
-            tiles.append(
+            near_tiles.append(
                 jnp.where(inner < 8, pick_lanes(near[0], z_near), pick_lanes(near[1], z_near))
             )
-        out_edge[POPS_AT + member] = by_layer(groups, tiles, lane8)
+        store(POPS_AT + member, by_layer(groups, near_tiles, lane8))
 
     place, state = own_state(block[0])
     a_radius, a_speed = state[0], state[1:4]
@@ -614,29 +663,29 @@
     contact = [-value for value in push] + [-a_radius * value for value in twist]
     contact = [value + roll(value, -2, 0) for value in contact]
 
+    ends = [jnp.where(high, 127, 0), jnp.where(high, 0, 127)]
+    ends = [jnp.full((8, 128), end, jnp.int32) for end in ends]
+    picked = [pick_lanes(value, ends[0]) for value in place + state]
+    touch = end_contact(groups, z_first[CONTACT_TILE], high, picked)
     for f in range(6):
-        out_contact[f] = contact[f]
+        out_contact[f] = contact[f] + touch[f]
+    for q, value in enumerate(place + state):
+        out_state[q] = pick_lanes(value, ends[1])
 
 
 def edge_kernel(
-    groups, paired, sides, whole, bulk_pops, bulk_loads, bulk_contact, edge, first, second, *refs
+    groups, paired, sides, bulk_pops, bulk_loads, bulk_contact, edge, state, second, *refs
 ):
-    final_pops, final_loads, held, out_pops, out_loads, sems = refs
-    side = end_flags(sides)[1]
-    for tile in range(Z_TILES):
-        held[side, tile] = first[tile]
-        value = second[tile]
-        held[1 - side, tile] = roll(value, 32, 1) if paired else value
+    final_pops, final_loads, out_pops, out_loads, sems = refs
+    high = end_flags(sides)[1] == 0
     lane, row = iota((8, 128), 1), iota((8, 128), 0)
-    inner = lane % 16
-    at_low = (inner == 2) | (inner == 3)
-    at_high = (inner == 12) | (inner == 13)
+    tiles = [roll(second[tile], 32, 1) if paired else second[tile] for tile in range(Z_TILES)]
+    moved = [jnp.where(high, roll(tiles[tile], 10, 1), tiles[tile]) for tile in range(CONTACT_TILE)]
+    filled = end_lanes(high, lane % 16)
 
     def value_of(field):
-        q = 2 * (field % 8)
-        low = roll(held[0, field // 8], 2 - q, 1)
-        high = roll(held[1, field // 8], 12 - q, 1)
-        return jnp.where(at_low, low, jnp.where(at_high, high, edge[field]))
+        halo = roll(moved[field // 8], 2 - 2 * (field % 8), 1)
+        return jnp.where(filled, halo, edge[field])
 
     speed, spin, offset = [[value_of(3 * n + c) for c in range(3)] for n in range(3)]
     weights = [value_of(E0 + k) for k in range(27)]
@@ -692,43 +741,10 @@
                 moments.turn(2, together, kz)
     hydro = moments.loads(offset)
 
-    place, state = own_state(Block(whole, None, 0))
-    own_index = jnp.where(lane < 64, 0, 127)
-    place = [pick_lanes(value, own_index) for value in place]
-    state = [pick_lanes(value, own_index) for value in state]
-    a_radius, a_speed = state[0], state[1:4]
-    a_turn = [a_radius * value for value in state[4:7]]
-    step_x, step_y = inner - 1, lane % 64 // 16 - 1
-    order = lane_groups(groups)
-    runs = [order.index(groups - 1), 0, 1]
-    run = 32 * jnp.where(step_x < 0, runs[0], jnp.where(step_x == 0, 0, runs[2]))
-    other = [None] * 10
-    for end in range(2):
-        tile = held[end, CONTACT_TILE]
-        for oy in (-1, 0, 1):
-            at = 2 * (oy + 1)
-            rows = jnp.concatenate([tile[at : at + 1], tile[at + 2 : at + 3]], axis=0)
-            moved = roll(rows, -16, 1)
-            rows = jnp.concatenate([rows, moved, rows, moved], axis=0)
-            mask = (lane // 64 == end) & (step_y == oy)
-            for q in range(10):
-                value = pick_lanes(rows, run + q)
-                other[q] = value if other[q] is None else jnp.where(mask, value, other[q])
-    keep = (step_x < 2) & (step_y < 2)
-    gap = [
-        other[0] - place[0] + (2 * step_x).astype(F32),
-        other[1] - place[1] + (2 * step_y).astype(F32),
-        other[2] - place[2] + jnp.where(lane < 64, -2.0, 2.0),
-    ]
-    pushed, twisted = pair_force(gap, a_radius, a_speed, a_turn, other[3:], keep)
-    contact = [-value for value in pushed] + [-a_radius * value for value in twisted]
+    touch = end_contact(groups, tiles[CONTACT_TILE], high, [state[q] for q in range(10)])
     ends = lane == 0, lane == 127
     masks = [edge[CODE_AT + s] == cell_codes(lane, row) for s in range(2)]
     for f in range(6):
-        value = contact[f] + roll(contact[f], -2, 0)
-        value = value + roll(value, -1, 1) + roll(value, -2, 1)
-        value = value + roll(value, -16, 1) + roll(value, -32, 1)
-        touch = jnp.where(ends[0], value, jnp.where(ends[1], roll(value, 63, 1), 0.0))
         for s in range(2):
             value = jnp.where(masks[s], hydro[f], 0.0)
             value = value + roll(value, -16, 1)
@@ -738,8 +754,7 @@
                 ends[0], roll(value, -4, 1), jnp.where(ends[1], roll(value, 117, 1), 0.0)
             )
             both = jnp.concatenate([value[2:3], value[4:5]], axis=0)
-            both = both + touch[4 * s : 4 * s + 2]
-            both = both + bulk_contact[f, 4 * s : 4 * s + 2, :]
+            both = both + touch[f][4 * s : 4 * s + 2] + bulk_contact[f, 4 * s : 4 * s + 2, :]
             out_loads[f, s, 0] = bulk_loads[f, 2 * s : 2 * s + 2, :] + both
     copy = pltpu.make_async_copy(out_loads, final_loads, sems.at[len(PARTS)])
     copy.start()
@@ -846,8 +861,8 @@
         bulk = pack_bulk(wholes, halos)
     side = call(
         functools.partial(side_kernel, groups, paired, sides),
-        wholes + halos,
-        [(6, 8, 128), (EDGE_VALUES, 8, 128)],
+        wholes + halos + ends[:1],
+        [(6, 8, 128), (EDGE_VALUES, 8, 128), (10, 8, 128)],
         [(2,) + shape_y],
     )
     populations, offset = blocks[0], blocks[2]
@@ -855,9 +870,9 @@
     return tuple(
         call(
             functools.partial(edge_kernel, groups, paired, sides),
-            [whole] + list(bulk) + list(side) + ends,
+            list(bulk) + list(side) + ends[1:],
             shapes,
-            [(2,) + shape_z] + shapes + [pltpu.SemaphoreType.DMA((len(PARTS) + 1,))],
+            shapes + [pltpu.SemaphoreType.DMA((len(PARTS) + 1,))],
             (pltpu.VMEM, pltpu.HBM),
         )
     )

time: 18.8 us -> 18.6 us (0.989)
  waiting for transfers between devices: 5.51 us -> 5.28 us
    ppermute x6, waiting for transfers between devices: 5.51 us -> 5.28 us  [permute(): return lax.ppermute(value, axes, pairs)]
  transfers between devices with their start and end apart: 6 -> 6, of which waited for: 5 -> 4; matrix products, arithmetic and copies ran while one was open for 0% -> 0% of each run, Pallas kernels for 12% -> 13%
where the time goes in v6:
time: 18.6 us; the launch traced here: 18.4 us
  starting transfers between devices  7.18 us (39%)
  Pallas kernels  5.29 us (28%)
  waiting for transfers between devices  5.28 us (28%)
  between operations  0.67 us (4%)
    ppermute x6, starting transfers between devices, permute(): return lax.ppermute(value, axes, pairs)  7.18 us
    pallas_call x5, Pallas kernels, call(): pl.pallas_call(kernel, out_shape=[jax.ShapeDtypeStruct(shape, F32) for sh...  5.29 us
    ppermute x6, waiting for transfers between devices, permute(): return lax.ppermute(value, axes, pairs)  5.28 us
  transfers between devices with their start and end apart: 6, of which 4 were waited for; matrix products, arithmetic and copies ran while one was open for 0% of the time, Pallas kernels for 13%

profile of v6, /device:TPU:0, one launch (start us, length us, event | category | flops | bytes accessed | tf_op | source)
XLA Modules:
  0.0 18.4 jit_solution(9911248970673825436)
XLA Ops:
  0.6 1.1 %shard_map.86 = (f32[57,8,128]{2,1,0:T(8,128)S(1)}, f32[2,14,8,128]{3,2,1,0:T(8,128)S(1)}, f32[14,8,128]{2,1,0:T(8,128)S(1)}) custom-call(f32[19,2,4,256]{3,2,1,0:T(4,128)} %refs_0_.1, s32[2,1,2,128]{3,2,1,0:T(2,128)} %refs_1_.1, f32[3,2,1,2,128]{4,3,2,1,0:T(2,128)} %refs_2_.1, f32[2,1,2,128]{3,2,1,0:T(2,128)} %refs_3_.1, f32[3,2,1,2,128]{4,3,2,1,0:T(2,128)} %refs_4_.1, ...), custom_call_target="tpu_custom_call" | custom-call | tf_op jit(solution)/shard_map/pallas_call | solution.py:769
  1.7 0.5 %collective-permute-start.1 = (f32[14,8,128]{2,1,0:T(8,128)S(1)}, f32[14,8,128]{2,1,0:T(8,128)S(1)}, u32[]{:S(2)}, u32[]{:S(2)}) collective-permute-start(f32[14,8,128]{2,1,0:T(8,128)S(1)} %get-tuple-element.27), channel_id=1, source_target_pairs={{0,16},{1,17},{2,18},{3,19},{4,20},{5,21},{6,22},{7,23},{8,24},{9,... | collective-permute-start | bytes 172040 | tf_op jit(solution)/shard_map/ppermute | solution.py:792
  2.3 0.1 collective-permute-start
  2.3 0.8 %collective-permute-done.1 = f32[14,8,128]{2,1,0:T(8,128)S(1)} collective-permute-done((f32[14,8,128]{2,1,0:T(8,128)S(1)}, f32[14,8,128]{2,1,0:T(8,128)S(1)}, u32[]{:S(2)}, u32[]{:S(2)}) %collective-permute-start.1) | collective-permute-done | bytes 57376 | tf_op jit(solution)/shard_map/ppermute | solution.py:792
  3.2 2.9 %collective-permute-start.2 = (f32[2,14,8,128]{3,2,1,0:T(8,128)S(1)}, f32[2,14,8,128]{3,2,1,0:T(8,128)S(1)}, u32[]{:S(2)}, u32[]{:S(2)}) collective-permute-start(f32[2,14,8,128]{3,2,1,0:T(8,128)S(1)} %bitcast_dynamic-update-slice_fusion), channel_id=1, source_target_pairs={{0,4},{1,5},{2,6},{3,7},{4,0},{5,1},{6,2},{7,3},{8,12},{9,13},{10,... | collective-permute-start | bytes 344072 | tf_op jit(solution)/shard_map/ppermute | solution.py:792
  6.1 2.8 %collective-permute-done.2.refs_2_ = f32[2,14,8,128]{3,2,1,0:T(8,128)S(1)} collective-permute-done((f32[2,14,8,128]{3,2,1,0:T(8,128)S(1)}, f32[2,14,8,128]{3,2,1,0:T(8,128)S(1)}, u32[]{:S(2)}, u32[]{:S(2)}) %collective-permute-start.2) | collective-permute-done | bytes 114720 | tf_op jit(solution)/shard_map/ppermute | solution.py:792
  8.8 1.6 %collective-permute-start.3 = (f32[2,14,8,128]{3,2,1,0:T(8,128)S(1)}, f32[2,14,8,128]{3,2,1,0:T(8,128)S(1)}, u32[]{:S(2)}, u32[]{:S(2)}) collective-permute-start(f32[2,14,8,128]{3,2,1,0:T(8,128)S(1)} %collective-permute-done.2.refs_2_), channel_id=1, source_target_pairs={{0,16},{1,17},{2,18},{3,19},{4,20},{5,21},{6,22},{7,23},{8,24},{9,... | collective-permute-start | bytes 344072 | tf_op jit(solution)/shard_map/ppermute | solution.py:792
  10.5 0.0 collective-permute-done.refs_1_
  10.5 1.0 %collective-permute-done.3.refs_3_ = f32[2,14,8,128]{3,2,1,0:T(8,128)S(1)} collective-permute-done((f32[2,14,8,128]{3,2,1,0:T(8,128)S(1)}, f32[2,14,8,128]{3,2,1,0:T(8,128)S(1)}, u32[]{:S(2)}, u32[]{:S(2)}) %collective-permute-start.3) | collective-permute-done | bytes 114720 | tf_op jit(solution)/shard_map/ppermute | solution.py:792
  11.4 0.4 %shard_map.87 = f32[8,8,128]{2,1,0:T(8,128)S(1)} custom-call(f32[57,8,128]{2,1,0:T(8,128)S(1)} %get-tuple-element.25.refs_0_, f32[57,8,128]{2,1,0:T(8,128)S(1)} %collective-permute-done.refs_1_, f32[2,14,8,128]{3,2,1,0:T(8,128)S(1)} %collective-permute-done.2.refs_2_, f32[2,14,8,128]{3,2,1,0:T(8,128)S(1)} %collective-permute-done.3.refs_3_), custom_call_target="tpu_custom_call" | custom-call | tf_op jit(solution)/shard_map/pallas_call | solution.py:769
  11.8 1.8 %collective-permute-start.4 = (f32[8,8,128]{2,1,0:T(8,128)S(1)}, f32[8,8,128]{2,1,0:T(8,128)S(1)}, u32[]{:S(2)}, u32[]{:S(2)}) collective-permute-start(f32[8,8,128]{2,1,0:T(8,128)S(1)} %shard_map.87), channel_id=1, source_target_pairs={{0,1},{1,0},{2,3},{3,2},{4,5},{5,4},{6,7},{7,6},{8,9},{9,8},{10,11... | collective-permute-start | bytes 98312 | tf_op jit(solution)/shard_map/ppermute | solution.py:792
  13.7 1.4 %shard_map.88 = (f32[38,8,128]{2,1,0:T(8,128)S(1)}, f32[6,4,128]{2,1,0:T(4,128)S(1)}) custom-call(f32[57,8,128]{2,1,0:T(8,128)S(1)} %get-tuple-element.25.refs_0_, f32[57,8,128]{2,1,0:T(8,128)S(1)} %collective-permute-done.refs_1_, f32[2,14,8,128]{3,2,1,0:T(8,128)S(1)} %collective-permute-done.2.refs_2_, f32[2,14,8,128]{3,2,1,0:T(8,128)S(1)} %collective-permute-done.3.refs_3_), custom_call_target="tpu_custom_call" | custom-call | tf_op jit(solution)/shard_map/pallas_call | solution.py:769
  15.1 0.7 %collective-permute-done.4.refs_4_ = f32[8,8,128]{2,1,0:T(8,128)S(1)} collective-permute-done((f32[8,8,128]{2,1,0:T(8,128)S(1)}, f32[8,8,128]{2,1,0:T(8,128)S(1)}, u32[]{:S(2)}, u32[]{:S(2)}) %collective-permute-start.4) | collective-permute-done | bytes 32800 | tf_op jit(solution)/shard_map/ppermute | solution.py:792
  15.8 0.2 %collective-permute-start.5 = (f32[8,8,128]{2,1,0:T(8,128)S(1)}, f32[8,8,128]{2,1,0:T(8,128)S(1)}, u32[]{:S(2)}, u32[]{:S(2)}) collective-permute-start(f32[8,8,128]{2,1,0:T(8,128)S(1)} %collective-permute-done.4.refs_4_), channel_id=1, source_target_pairs={{0,16},{1,17},{2,18},{3,19},{4,20},{5,21},{6,22},{7,23},{8,24},{9,... | collective-permute-start | bytes 98312 | tf_op jit(solution)/shard_map/ppermute | solution.py:792
  16.0 1.0 %shard_map.89 = (f32[6,8,128]{2,1,0:T(8,128)S(1)}, f32[57,8,128]{2,1,0:T(8,128)S(1)}, f32[10,8,128]{2,1,0:T(8,128)S(1)}) custom-call(f32[57,8,128]{2,1,0:T(8,128)S(1)} %get-tuple-element.25.refs_0_, f32[57,8,128]{2,1,0:T(8,128)S(1)} %collective-permute-done.refs_1_, f32[2,14,8,128]{3,2,1,0:T(8,128)S(1)} %collective-permute-done.2.refs_2_, ...), custom_call_target="tpu_custom_call" | custom-call | tf_op jit(solution)/shard_map/pallas_call | solution.py:769
  17.0 0.0 collective-permute-done.5.second
  17.0 1.4 %shard_map.90 = (f32[19,2,4,256]{3,2,1,0:T(4,128)}, f32[6,2,1,2,128]{4,3,2,1,0:T(2,128)}) custom-call(f32[38,8,128]{2,1,0:T(8,128)S(1)} %get-tuple-element.30.bulk_pops, f32[6,4,128]{2,1,0:T(4,128)S(1)} %get-tuple-element.31.bulk_loads, f32[6,8,128]{2,1,0:T(8,128)S(1)} %get-tuple-element.33.bulk_contact, f32[57,8,128]{2,1,0:T(8,128)S(1)} %get-tuple-element.34.edge, ...), custom_call_target="tpu_custom_call" | custom-call | tf_op jit(solution)/shard_map/pallas_call | solution.py:769
  (1 shorter events, 0.0 us)
Async XLA Ops:
  1.7 1.4 %collective-permute-start.1 = (f32[14,8,128]{2,1,0:T(8,128)S(1)}, f32[14,8,128]{2,1,0:T(8,128)S(1)}, u32[]{:S(2)}, u32[]{:S(2)}) collective-permute-start(f32[14,8,128]{2,1,0:T(8,128)S(1)} %get-tuple-element.27), channel_id=1, source_target_pairs={{0,16},{1,17},{2,18},{3,19},{4,20},{5,21},{6,22},{7,23},{8,24},{9,... | collective-permute-start | bytes 172040 | tf_op jit(solution)/shard_map/ppermute | solution.py:792
  2.3 8.2 %collective-permute-start = (f32[57,8,128]{2,1,0:T(8,128)S(1)}, f32[57,8,128]{2,1,0:T(8,128)S(1)}, u32[]{:S(2)}, u32[]{:S(2)}) collective-permute-start(f32[57,8,128]{2,1,0:T(8,128)S(1)} %get-tuple-element.25.refs_0_), channel_id=1, source_target_pairs={{0,16},{1,17},{2,18},{3,19},{4,20},{5,21},{6,22},{7,23},{8,24},{9,... | collective-permute-start | bytes 700424 | tf_op jit(solution)/shard_map/ppermute | solution.py:792
  3.2 5.7 %collective-permute-start.2 = (f32[2,14,8,128]{3,2,1,0:T(8,128)S(1)}, f32[2,14,8,128]{3,2,1,0:T(8,128)S(1)}, u32[]{:S(2)}, u32[]{:S(2)}) collective-permute-start(f32[2,14,8,128]{3,2,1,0:T(8,128)S(1)} %bitcast_dynamic-update-slice_fusion), channel_id=1, source_target_pairs={{0,4},{1,5},{2,6},{3,7},{4,0},{5,1},{6,2},{7,3},{8,12},{9,13},{10,... | collective-permute-start | bytes 344072 | tf_op jit(solution)/shard_map/ppermute | solution.py:792
  8.8 2.6 %collective-permute-start.3 = (f32[2,14,8,128]{3,2,1,0:T(8,128)S(1)}, f32[2,14,8,128]{3,2,1,0:T(8,128)S(1)}, u32[]{:S(2)}, u32[]{:S(2)}) collective-permute-start(f32[2,14,8,128]{3,2,1,0:T(8,128)S(1)} %collective-permute-done.2.refs_2_), channel_id=1, source_target_pairs={{0,16},{1,17},{2,18},{3,19},{4,20},{5,21},{6,22},{7,23},{8,24},{9,... | collective-permute-start | bytes 344072 | tf_op jit(solution)/shard_map/ppermute | solution.py:792
  11.8 4.0 %collective-permute-start.4 = (f32[8,8,128]{2,1,0:T(8,128)S(1)}, f32[8,8,128]{2,1,0:T(8,128)S(1)}, u32[]{:S(2)}, u32[]{:S(2)}) collective-permute-start(f32[8,8,128]{2,1,0:T(8,128)S(1)} %shard_map.87), channel_id=1, source_target_pairs={{0,1},{1,0},{2,3},{3,2},{4,5},{5,4},{6,7},{7,6},{8,9},{9,8},{10,11... | collective-permute-start | bytes 98312 | tf_op jit(solution)/shard_map/ppermute | solution.py:792
  15.8 1.2 %collective-permute-start.5 = (f32[8,8,128]{2,1,0:T(8,128)S(1)}, f32[8,8,128]{2,1,0:T(8,128)S(1)}, u32[]{:S(2)}, u32[]{:S(2)}) collective-permute-start(f32[8,8,128]{2,1,0:T(8,128)S(1)} %collective-permute-done.4.refs_4_), channel_id=1, source_target_pairs={{0,16},{1,17},{2,18},{3,19},{4,20},{5,21},{6,22},{7,23},{8,24},{9,... | collective-permute-start | bytes 98312 | tf_op jit(solution)/shard_map/ppermute | solution.py:792

commit v7 on v6

--- a/solution.py
+++ b/solution.py
@@ -278,18 +278,26 @@
             tile = block[g].cells(member, i, high)
             tiles.append(pick_lanes(tile, pops_index))
         values.append(by_layer(groups, tiles, lane))
+    tiles_out = []
     for tile in range(CONTACT_TILE):
         packed = values[8 * tile]
         for q in range(1, 8):
             if 8 * tile + q < len(values):
                 packed = jnp.where(inner == q, values[8 * tile + q], packed)
-        out[tile] = packed
+        tiles_out.append(packed)
     packed = jnp.zeros((8, 128), F32)
     for s in range(2):
         state = position(slots[s][CODE], slots[s][6:9]) + [slots[s][RADIUS]] + slots[s][0:6]
         for q, value in enumerate(state):
             packed = jnp.where(lane % 32 == 16 * s + q, value, packed)
-    out[CONTACT_TILE] = packed
+    tiles_out.append(packed)
+    if paired:
+        tiles_out = [
+            jnp.where(lane < 64, tiles_out[2 * n], tiles_out[2 * n + 1])
+            for n in range(Z_TILES // 2)
+        ]
+    for n, value in enumerate(tiles_out):
+        out[n] = value
 
 
 def dot_lattice(vector, velocity):
@@ -424,6 +432,17 @@
     return place, [rows(RADIUS)] + [rows(c) for c in range(6)]
 
 
+def z_tiles(paired, sent):
+    if not paired:
+        return [sent[tile] for tile in range(Z_TILES)]
+    left = iota((8, 128), 1) < 64
+    tiles = []
+    for n in range(Z_TILES // 2):
+        turned = roll(sent[n], 64, 1)
+        tiles += [jnp.where(left, sent[n], turned), jnp.where(left, turned, sent[n])]
+    return tiles
+
+
 def end_lanes(high, inner):
     start = jnp.where(high, 12, 2)
     return (inner == start) | (inner == start + 1)
@@ -597,8 +616,10 @@
         rows = [pick_lanes(block[g].bins(s, field), z_bin) for g in range(groups)]
         return by_group(groups, rows, lane8)
 
+    halo_tiles = z_tiles(paired, z_first)
     tiles = [
-        jnp.where(high, roll(z_first[tile], 10, 1), z_first[tile]) for tile in range(CONTACT_TILE)
+        jnp.where(high, roll(halo_tiles[tile], 10, 1), halo_tiles[tile])
+        for tile in range(CONTACT_TILE)
     ]
     filled = end_lanes(high, inner)
 
@@ -666,7 +687,7 @@
     ends = [jnp.where(high, 127, 0), jnp.where(high, 0, 127)]
     ends = [jnp.full((8, 128), end, jnp.int32) for end in ends]
     picked = [pick_lanes(value, ends[0]) for value in place + state]
-    touch = end_contact(groups, z_first[CONTACT_TILE], high, picked)
+    touch = end_contact(groups, halo_tiles[CONTACT_TILE], high, picked)
     for f in range(6):
         out_contact[f] = contact[f] + touch[f]
     for q, value in enumerate(place + state):
@@ -679,7 +700,7 @@
     final_pops, final_loads, out_pops, out_loads, sems = refs
     high = end_flags(sides)[1] == 0
     lane, row = iota((8, 128), 1), iota((8, 128), 0)
-    tiles = [roll(second[tile], 32, 1) if paired else second[tile] for tile in range(Z_TILES)]
+    tiles = [roll(value, 32, 1) if paired else value for value in z_tiles(paired, second)]
     moved = [jnp.where(high, roll(tiles[tile], 10, 1), tiles[tile]) for tile in range(CONTACT_TILE)]
     filled = end_lanes(high, lane % 16)
 
@@ -801,7 +822,7 @@
         return permute(value, lambda x, y, z: (x + 1, y, z))
 
     ends_y = (Y_BLOCKS, 8, 128)
-    shape_z = (Z_TILES, 8, 128)
+    shape_z = (Z_TILES // 2 if paired else Z_TILES, 8, 128)
     shape_y = (groups,) + ends_y
     sides = None if paired else (1, 1)
     held = [pltpu.VMEM(block.shape, block.dtype) for block in blocks]

time: 18.6 us -> 18.6 us (level)
  waiting for transfers between devices: 5.28 us -> 5.07 us
    ppermute x6, waiting for transfers between devices: 5.28 us -> 5.07 us  [permute(): return lax.ppermute(value, axes, pairs)]
where the time goes in v7:
time: 18.6 us; the launch traced here: 18.5 us
  starting transfers between devices  7.36 us (40%)
  Pallas kernels  5.36 us (29%)
  waiting for transfers between devices  5.07 us (27%)
  between operations  0.67 us (4%)
    ppermute x6, starting transfers between devices, permute(): return lax.ppermute(value, axes, pairs)  7.36 us
    pallas_call x5, Pallas kernels, call(): pl.pallas_call(kernel, out_shape=[jax.ShapeDtypeStruct(shape, F32) for sh...  5.36 us
    ppermute x6, waiting for transfers between devices, permute(): return lax.ppermute(value, axes, pairs)  5.07 us
  transfers between devices with their start and end apart: 6, of which 4 were waited for; matrix products, arithmetic and copies ran while one was open for 0% of the time, Pallas kernels for 13%

profile of v7, /device:TPU:0, one launch (start us, length us, event | category | flops | bytes accessed | tf_op | source)
XLA Modules:
  0.0 18.5 jit_solution(14287310184350921639)
XLA Ops:
  0.6 1.1 %shard_map.86 = (f32[57,8,128]{2,1,0:T(8,128)S(1)}, f32[2,14,8,128]{3,2,1,0:T(8,128)S(1)}, f32[14,8,128]{2,1,0:T(8,128)S(1)}) custom-call(f32[19,2,4,256]{3,2,1,0:T(4,128)} %refs_0_.1, s32[2,1,2,128]{3,2,1,0:T(2,128)} %refs_1_.1, f32[3,2,1,2,128]{4,3,2,1,0:T(2,128)} %refs_2_.1, f32[2,1,2,128]{3,2,1,0:T(2,128)} %refs_3_.1, f32[3,2,1,2,128]{4,3,2,1,0:T(2,128)} %refs_4_.1, ...), custom_call_target="tpu_custom_call" | custom-call | tf_op jit(solution)/shard_map/pallas_call | solution.py:790
  1.7 0.5 %collective-permute-start.1 = (f32[14,8,128]{2,1,0:T(8,128)S(1)}, f32[14,8,128]{2,1,0:T(8,128)S(1)}, u32[]{:S(2)}, u32[]{:S(2)}) collective-permute-start(f32[14,8,128]{2,1,0:T(8,128)S(1)} %get-tuple-element.27), channel_id=1, source_target_pairs={{0,16},{1,17},{2,18},{3,19},{4,20},{5,21},{6,22},{7,23},{8,24},{9,... | collective-permute-start | bytes 172040 | tf_op jit(solution)/shard_map/ppermute | solution.py:813
  2.3 0.1 collective-permute-start
  2.3 0.8 %collective-permute-done.1 = f32[14,8,128]{2,1,0:T(8,128)S(1)} collective-permute-done((f32[14,8,128]{2,1,0:T(8,128)S(1)}, f32[14,8,128]{2,1,0:T(8,128)S(1)}, u32[]{:S(2)}, u32[]{:S(2)}) %collective-permute-start.1) | collective-permute-done | bytes 57376 | tf_op jit(solution)/shard_map/ppermute | solution.py:813
  3.2 2.9 %collective-permute-start.2 = (f32[2,14,8,128]{3,2,1,0:T(8,128)S(1)}, f32[2,14,8,128]{3,2,1,0:T(8,128)S(1)}, u32[]{:S(2)}, u32[]{:S(2)}) collective-permute-start(f32[2,14,8,128]{3,2,1,0:T(8,128)S(1)} %bitcast_dynamic-update-slice_fusion), channel_id=1, source_target_pairs={{0,4},{1,5},{2,6},{3,7},{4,0},{5,1},{6,2},{7,3},{8,12},{9,13},{10,... | collective-permute-start | bytes 344072 | tf_op jit(solution)/shard_map/ppermute | solution.py:813
  6.1 2.8 %collective-permute-done.2.refs_2_ = f32[2,14,8,128]{3,2,1,0:T(8,128)S(1)} collective-permute-done((f32[2,14,8,128]{3,2,1,0:T(8,128)S(1)}, f32[2,14,8,128]{3,2,1,0:T(8,128)S(1)}, u32[]{:S(2)}, u32[]{:S(2)}) %collective-permute-start.2) | collective-permute-done | bytes 114720 | tf_op jit(solution)/shard_map/ppermute | solution.py:813
  8.8 1.6 %collective-permute-start.3 = (f32[2,14,8,128]{3,2,1,0:T(8,128)S(1)}, f32[2,14,8,128]{3,2,1,0:T(8,128)S(1)}, u32[]{:S(2)}, u32[]{:S(2)}) collective-permute-start(f32[2,14,8,128]{3,2,1,0:T(8,128)S(1)} %collective-permute-done.2.refs_2_), channel_id=1, source_target_pairs={{0,16},{1,17},{2,18},{3,19},{4,20},{5,21},{6,22},{7,23},{8,24},{9,... | collective-permute-start | bytes 344072 | tf_op jit(solution)/shard_map/ppermute | solution.py:813
  10.5 0.0 collective-permute-done.refs_1_
  10.5 1.0 %collective-permute-done.3.refs_3_ = f32[2,14,8,128]{3,2,1,0:T(8,128)S(1)} collective-permute-done((f32[2,14,8,128]{3,2,1,0:T(8,128)S(1)}, f32[2,14,8,128]{3,2,1,0:T(8,128)S(1)}, u32[]{:S(2)}, u32[]{:S(2)}) %collective-permute-start.3) | collective-permute-done | bytes 114720 | tf_op jit(solution)/shard_map/ppermute | solution.py:813
  11.4 0.4 %shard_map.87 = f32[4,8,128]{2,1,0:T(8,128)S(1)} custom-call(f32[57,8,128]{2,1,0:T(8,128)S(1)} %get-tuple-element.25.refs_0_, f32[57,8,128]{2,1,0:T(8,128)S(1)} %collective-permute-done.refs_1_, f32[2,14,8,128]{3,2,1,0:T(8,128)S(1)} %collective-permute-done.2.refs_2_, f32[2,14,8,128]{3,2,1,0:T(8,128)S(1)} %collective-permute-done.3.refs_3_), custom_call_target="tpu_custom_call" | custom-call | tf_op jit(solution)/shard_map/pallas_call | solution.py:790
  11.8 1.8 %collective-permute-start.4 = (f32[4,8,128]{2,1,0:T(8,128)S(1)}, f32[4,8,128]{2,1,0:T(8,128)S(1)}, u32[]{:S(2)}, u32[]{:S(2)}) collective-permute-start(f32[4,8,128]{2,1,0:T(8,128)S(1)} %shard_map.87), channel_id=1, source_target_pairs={{0,1},{1,0},{2,3},{3,2},{4,5},{5,4},{6,7},{7,6},{8,9},{9,8},{10,11... | collective-permute-start | bytes 49160 | tf_op jit(solution)/shard_map/ppermute | solution.py:813
  13.7 1.4 %shard_map.88 = (f32[38,8,128]{2,1,0:T(8,128)S(1)}, f32[6,4,128]{2,1,0:T(4,128)S(1)}) custom-call(f32[57,8,128]{2,1,0:T(8,128)S(1)} %get-tuple-element.25.refs_0_, f32[57,8,128]{2,1,0:T(8,128)S(1)} %collective-permute-done.refs_1_, f32[2,14,8,128]{3,2,1,0:T(8,128)S(1)} %collective-permute-done.2.refs_2_, f32[2,14,8,128]{3,2,1,0:T(8,128)S(1)} %collective-permute-done.3.refs_3_), custom_call_target="tpu_custom_call" | custom-call | tf_op jit(solution)/shard_map/pallas_call | solution.py:790
  15.1 0.5 %collective-permute-done.4.refs_4_ = f32[4,8,128]{2,1,0:T(8,128)S(1)} collective-permute-done((f32[4,8,128]{2,1,0:T(8,128)S(1)}, f32[4,8,128]{2,1,0:T(8,128)S(1)}, u32[]{:S(2)}, u32[]{:S(2)}) %collective-permute-start.4) | collective-permute-done | bytes 16416 | tf_op jit(solution)/shard_map/ppermute | solution.py:813
  15.6 0.4 %collective-permute-start.5 = (f32[4,8,128]{2,1,0:T(8,128)S(1)}, f32[4,8,128]{2,1,0:T(8,128)S(1)}, u32[]{:S(2)}, u32[]{:S(2)}) collective-permute-start(f32[4,8,128]{2,1,0:T(8,128)S(1)} %collective-permute-done.4.refs_4_), channel_id=1, source_target_pairs={{0,16},{1,17},{2,18},{3,19},{4,20},{5,21},{6,22},{7,23},{8,24},{9,... | collective-permute-start | bytes 49160 | tf_op jit(solution)/shard_map/ppermute | solution.py:813
  16.0 1.0 %shard_map.89 = (f32[6,8,128]{2,1,0:T(8,128)S(1)}, f32[57,8,128]{2,1,0:T(8,128)S(1)}, f32[10,8,128]{2,1,0:T(8,128)S(1)}) custom-call(f32[57,8,128]{2,1,0:T(8,128)S(1)} %get-tuple-element.25.refs_0_, f32[57,8,128]{2,1,0:T(8,128)S(1)} %collective-permute-done.refs_1_, f32[2,14,8,128]{3,2,1,0:T(8,128)S(1)} %collective-permute-done.2.refs_2_, ...), custom_call_target="tpu_custom_call" | custom-call | tf_op jit(solution)/shard_map/pallas_call | solution.py:790
  17.0 0.0 collective-permute-done.5.second
  17.0 1.5 %shard_map.90 = (f32[19,2,4,256]{3,2,1,0:T(4,128)}, f32[6,2,1,2,128]{4,3,2,1,0:T(2,128)}) custom-call(f32[38,8,128]{2,1,0:T(8,128)S(1)} %get-tuple-element.30.bulk_pops, f32[6,4,128]{2,1,0:T(4,128)S(1)} %get-tuple-element.31.bulk_loads, f32[6,8,128]{2,1,0:T(8,128)S(1)} %get-tuple-element.33.bulk_contact, f32[57,8,128]{2,1,0:T(8,128)S(1)} %get-tuple-element.34.edge, ...), custom_call_target="tpu_custom_call" | custom-call | tf_op jit(solution)/shard_map/pallas_call | solution.py:790
  (1 shorter events, 0.0 us)
Async XLA Ops:
  1.7 1.4 %collective-permute-start.1 = (f32[14,8,128]{2,1,0:T(8,128)S(1)}, f32[14,8,128]{2,1,0:T(8,128)S(1)}, u32[]{:S(2)}, u32[]{:S(2)}) collective-permute-start(f32[14,8,128]{2,1,0:T(8,128)S(1)} %get-tuple-element.27), channel_id=1, source_target_pairs={{0,16},{1,17},{2,18},{3,19},{4,20},{5,21},{6,22},{7,23},{8,24},{9,... | collective-permute-start | bytes 172040 | tf_op jit(solution)/shard_map/ppermute | solution.py:813
  2.3 8.2 %collective-permute-start = (f32[57,8,128]{2,1,0:T(8,128)S(1)}, f32[57,8,128]{2,1,0:T(8,128)S(1)}, u32[]{:S(2)}, u32[]{:S(2)}) collective-permute-start(f32[57,8,128]{2,1,0:T(8,128)S(1)} %get-tuple-element.25.refs_0_), channel_id=1, source_target_pairs={{0,16},{1,17},{2,18},{3,19},{4,20},{5,21},{6,22},{7,23},{8,24},{9,... | collective-permute-start | bytes 700424 | tf_op jit(solution)/shard_map/ppermute | solution.py:813
  3.2 5.7 %collective-permute-start.2 = (f32[2,14,8,128]{3,2,1,0:T(8,128)S(1)}, f32[2,14,8,128]{3,2,1,0:T(8,128)S(1)}, u32[]{:S(2)}, u32[]{:S(2)}) collective-permute-start(f32[2,14,8,128]{3,2,1,0:T(8,128)S(1)} %bitcast_dynamic-update-slice_fusion), channel_id=1, source_target_pairs={{0,4},{1,5},{2,6},{3,7},{4,0},{5,1},{6,2},{7,3},{8,12},{9,13},{10,... | collective-permute-start | bytes 344072 | tf_op jit(solution)/shard_map/ppermute | solution.py:813
  8.8 2.6 %collective-permute-start.3 = (f32[2,14,8,128]{3,2,1,0:T(8,128)S(1)}, f32[2,14,8,128]{3,2,1,0:T(8,128)S(1)}, u32[]{:S(2)}, u32[]{:S(2)}) collective-permute-start(f32[2,14,8,128]{3,2,1,0:T(8,128)S(1)} %collective-permute-done.2.refs_2_), channel_id=1, source_target_pairs={{0,16},{1,17},{2,18},{3,19},{4,20},{5,21},{6,22},{7,23},{8,24},{9,... | collective-permute-start | bytes 344072 | tf_op jit(solution)/shard_map/ppermute | solution.py:813
  11.8 3.8 %collective-permute-start.4 = (f32[4,8,128]{2,1,0:T(8,128)S(1)}, f32[4,8,128]{2,1,0:T(8,128)S(1)}, u32[]{:S(2)}, u32[]{:S(2)}) collective-permute-start(f32[4,8,128]{2,1,0:T(8,128)S(1)} %shard_map.87), channel_id=1, source_target_pairs={{0,1},{1,0},{2,3},{3,2},{4,5},{5,4},{6,7},{7,6},{8,9},{9,8},{10,11... | collective-permute-start | bytes 49160 | tf_op jit(solution)/shard_map/ppermute | solution.py:813
  15.6 1.4 %collective-permute-start.5 = (f32[4,8,128]{2,1,0:T(8,128)S(1)}, f32[4,8,128]{2,1,0:T(8,128)S(1)}, u32[]{:S(2)}, u32[]{:S(2)}) collective-permute-start(f32[4,8,128]{2,1,0:T(8,128)S(1)} %collective-permute-done.4.refs_4_), channel_id=1, source_target_pairs={{0,16},{1,17},{2,18},{3,19},{4,20},{5,21},{6,22},{7,23},{8,24},{9,... | collective-permute-start | bytes 49160 | tf_op jit(solution)/shard_map/ppermute | solution.py:813

commit v8 on v6

--- a/solution.py
+++ b/solution.py
@@ -464,7 +464,7 @@
 
 
 POPS_PARTS = [(0, 5), (5, 5), (10, 5), (15, 4)]
-PARTS = [4, 9, 14, 18]
+PARTS = [18]
 AT_LAYER = {0: 0, 1: 1, 2: 2, -1: 3}
 
 

time: 18.6 us -> 18.6 us (level)
  no operation moved by 1% of the time
where the time goes in v8:
time: 18.6 us; the launch traced here: 18.4 us
  starting transfers between devices  7.18 us (39%)
  Pallas kernels  5.31 us (29%)
  waiting for transfers between devices  5.28 us (28%)
  between operations  0.67 us (4%)
    ppermute x6, starting transfers between devices, permute(): return lax.ppermute(value, axes, pairs)  7.18 us
    pallas_call x5, Pallas kernels, call(): pl.pallas_call(kernel, out_shape=[jax.ShapeDtypeStruct(shape, F32) for sh...  5.31 us
    ppermute x6, waiting for transfers between devices, permute(): return lax.ppermute(value, axes, pairs)  5.28 us
  transfers between devices with their start and end apart: 6, of which 4 were waited for; matrix products, arithmetic and copies ran while one was open for 0% of the time, Pallas kernels for 13%

profile of v8, /device:TPU:0, one launch (start us, length us, event | category | flops | bytes accessed | tf_op | source)
XLA Modules:
  0.0 18.4 jit_solution(1510139983514701175)
XLA Ops:
  0.6 1.1 %shard_map.86 = (f32[57,8,128]{2,1,0:T(8,128)S(1)}, f32[2,14,8,128]{3,2,1,0:T(8,128)S(1)}, f32[14,8,128]{2,1,0:T(8,128)S(1)}) custom-call(f32[19,2,4,256]{3,2,1,0:T(4,128)} %refs_0_.1, s32[2,1,2,128]{3,2,1,0:T(2,128)} %refs_1_.1, f32[3,2,1,2,128]{4,3,2,1,0:T(2,128)} %refs_2_.1, f32[2,1,2,128]{3,2,1,0:T(2,128)} %refs_3_.1, f32[3,2,1,2,128]{4,3,2,1,0:T(2,128)} %refs_4_.1, ...), custom_call_target="tpu_custom_call" | custom-call | tf_op jit(solution)/shard_map/pallas_call | solution.py:769
  1.7 0.5 %collective-permute-start.1 = (f32[14,8,128]{2,1,0:T(8,128)S(1)}, f32[14,8,128]{2,1,0:T(8,128)S(1)}, u32[]{:S(2)}, u32[]{:S(2)}) collective-permute-start(f32[14,8,128]{2,1,0:T(8,128)S(1)} %get-tuple-element.27), channel_id=1, source_target_pairs={{0,16},{1,17},{2,18},{3,19},{4,20},{5,21},{6,22},{7,23},{8,24},{9,... | collective-permute-start | bytes 172040 | tf_op jit(solution)/shard_map/ppermute | solution.py:792
  2.3 0.1 collective-permute-start
  2.3 0.8 %collective-permute-done.1 = f32[14,8,128]{2,1,0:T(8,128)S(1)} collective-permute-done((f32[14,8,128]{2,1,0:T(8,128)S(1)}, f32[14,8,128]{2,1,0:T(8,128)S(1)}, u32[]{:S(2)}, u32[]{:S(2)}) %collective-permute-start.1) | collective-permute-done | bytes 57376 | tf_op jit(solution)/shard_map/ppermute | solution.py:792
  3.2 2.9 %collective-permute-start.2 = (f32[2,14,8,128]{3,2,1,0:T(8,128)S(1)}, f32[2,14,8,128]{3,2,1,0:T(8,128)S(1)}, u32[]{:S(2)}, u32[]{:S(2)}) collective-permute-start(f32[2,14,8,128]{3,2,1,0:T(8,128)S(1)} %bitcast_dynamic-update-slice_fusion), channel_id=1, source_target_pairs={{0,4},{1,5},{2,6},{3,7},{4,0},{5,1},{6,2},{7,3},{8,12},{9,13},{10,... | collective-permute-start | bytes 344072 | tf_op jit(solution)/shard_map/ppermute | solution.py:792
  6.1 2.8 %collective-permute-done.2.refs_2_ = f32[2,14,8,128]{3,2,1,0:T(8,128)S(1)} collective-permute-done((f32[2,14,8,128]{3,2,1,0:T(8,128)S(1)}, f32[2,14,8,128]{3,2,1,0:T(8,128)S(1)}, u32[]{:S(2)}, u32[]{:S(2)}) %collective-permute-start.2) | collective-permute-done | bytes 114720 | tf_op jit(solution)/shard_map/ppermute | solution.py:792
  8.8 1.6 %collective-permute-start.3 = (f32[2,14,8,128]{3,2,1,0:T(8,128)S(1)}, f32[2,14,8,128]{3,2,1,0:T(8,128)S(1)}, u32[]{:S(2)}, u32[]{:S(2)}) collective-permute-start(f32[2,14,8,128]{3,2,1,0:T(8,128)S(1)} %collective-permute-done.2.refs_2_), channel_id=1, source_target_pairs={{0,16},{1,17},{2,18},{3,19},{4,20},{5,21},{6,22},{7,23},{8,24},{9,... | collective-permute-start | bytes 344072 | tf_op jit(solution)/shard_map/ppermute | solution.py:792
  10.5 0.0 collective-permute-done.refs_1_
  10.5 1.0 %collective-permute-done.3.refs_3_ = f32[2,14,8,128]{3,2,1,0:T(8,128)S(1)} collective-permute-done((f32[2,14,8,128]{3,2,1,0:T(8,128)S(1)}, f32[2,14,8,128]{3,2,1,0:T(8,128)S(1)}, u32[]{:S(2)}, u32[]{:S(2)}) %collective-permute-start.3) | collective-permute-done | bytes 114720 | tf_op jit(solution)/shard_map/ppermute | solution.py:792
  11.4 0.4 %shard_map.87 = f32[8,8,128]{2,1,0:T(8,128)S(1)} custom-call(f32[57,8,128]{2,1,0:T(8,128)S(1)} %get-tuple-element.25.refs_0_, f32[57,8,128]{2,1,0:T(8,128)S(1)} %collective-permute-done.refs_1_, f32[2,14,8,128]{3,2,1,0:T(8,128)S(1)} %collective-permute-done.2.refs_2_, f32[2,14,8,128]{3,2,1,0:T(8,128)S(1)} %collective-permute-done.3.refs_3_), custom_call_target="tpu_custom_call" | custom-call | tf_op jit(solution)/shard_map/pallas_call | solution.py:769
  11.8 1.8 %collective-permute-start.4 = (f32[8,8,128]{2,1,0:T(8,128)S(1)}, f32[8,8,128]{2,1,0:T(8,128)S(1)}, u32[]{:S(2)}, u32[]{:S(2)}) collective-permute-start(f32[8,8,128]{2,1,0:T(8,128)S(1)} %shard_map.87), channel_id=1, source_target_pairs={{0,1},{1,0},{2,3},{3,2},{4,5},{5,4},{6,7},{7,6},{8,9},{9,8},{10,11... | collective-permute-start | bytes 98312 | tf_op jit(solution)/shard_map/ppermute | solution.py:792
  13.7 1.4 %shard_map.88 = (f32[38,8,128]{2,1,0:T(8,128)S(1)}, f32[6,4,128]{2,1,0:T(4,128)S(1)}) custom-call(f32[57,8,128]{2,1,0:T(8,128)S(1)} %get-tuple-element.25.refs_0_, f32[57,8,128]{2,1,0:T(8,128)S(1)} %collective-permute-done.refs_1_, f32[2,14,8,128]{3,2,1,0:T(8,128)S(1)} %collective-permute-done.2.refs_2_, f32[2,14,8,128]{3,2,1,0:T(8,128)S(1)} %collective-permute-done.3.refs_3_), custom_call_target="tpu_custom_call" | custom-call | tf_op jit(solution)/shard_map/pallas_call | solution.py:769
  15.1 0.7 %collective-permute-done.4.refs_4_ = f32[8,8,128]{2,1,0:T(8,128)S(1)} collective-permute-done((f32[8,8,128]{2,1,0:T(8,128)S(1)}, f32[8,8,128]{2,1,0:T(8,128)S(1)}, u32[]{:S(2)}, u32[]{:S(2)}) %collective-permute-start.4) | collective-permute-done | bytes 32800 | tf_op jit(solution)/shard_map/ppermute | solution.py:792
  15.8 0.2 %collective-permute-start.5 = (f32[8,8,128]{2,1,0:T(8,128)S(1)}, f32[8,8,128]{2,1,0:T(8,128)S(1)}, u32[]{:S(2)}, u32[]{:S(2)}) collective-permute-start(f32[8,8,128]{2,1,0:T(8,128)S(1)} %collective-permute-done.4.refs_4_), channel_id=1, source_target_pairs={{0,16},{1,17},{2,18},{3,19},{4,20},{5,21},{6,22},{7,23},{8,24},{9,... | collective-permute-start | bytes 98312 | tf_op jit(solution)/shard_map/ppermute | solution.py:792
  16.0 1.0 %shard_map.89 = (f32[6,8,128]{2,1,0:T(8,128)S(1)}, f32[57,8,128]{2,1,0:T(8,128)S(1)}, f32[10,8,128]{2,1,0:T(8,128)S(1)}) custom-call(f32[57,8,128]{2,1,0:T(8,128)S(1)} %get-tuple-element.25.refs_0_, f32[57,8,128]{2,1,0:T(8,128)S(1)} %collective-permute-done.refs_1_, f32[2,14,8,128]{3,2,1,0:T(8,128)S(1)} %collective-permute-done.2.refs_2_, ...), custom_call_target="tpu_custom_call" | custom-call | tf_op jit(solution)/shard_map/pallas_call | solution.py:769
  17.0 0.0 collective-permute-done.5.second
  17.0 1.4 %shard_map.90 = (f32[19,2,4,256]{3,2,1,0:T(4,128)}, f32[6,2,1,2,128]{4,3,2,1,0:T(2,128)}) custom-call(f32[38,8,128]{2,1,0:T(8,128)S(1)} %get-tuple-element.30.bulk_pops, f32[6,4,128]{2,1,0:T(4,128)S(1)} %get-tuple-element.31.bulk_loads, f32[6,8,128]{2,1,0:T(8,128)S(1)} %get-tuple-element.33.bulk_contact, f32[57,8,128]{2,1,0:T(8,128)S(1)} %get-tuple-element.34.edge, ...), custom_call_target="tpu_custom_call" | custom-call | tf_op jit(solution)/shard_map/pallas_call | solution.py:769
  (1 shorter events, 0.0 us)
Async XLA Ops:
  1.7 1.4 %collective-permute-start.1 = (f32[14,8,128]{2,1,0:T(8,128)S(1)}, f32[14,8,128]{2,1,0:T(8,128)S(1)}, u32[]{:S(2)}, u32[]{:S(2)}) collective-permute-start(f32[14,8,128]{2,1,0:T(8,128)S(1)} %get-tuple-element.27), channel_id=1, source_target_pairs={{0,16},{1,17},{2,18},{3,19},{4,20},{5,21},{6,22},{7,23},{8,24},{9,... | collective-permute-start | bytes 172040 | tf_op jit(solution)/shard_map/ppermute | solution.py:792
  2.3 8.2 %collective-permute-start = (f32[57,8,128]{2,1,0:T(8,128)S(1)}, f32[57,8,128]{2,1,0:T(8,128)S(1)}, u32[]{:S(2)}, u32[]{:S(2)}) collective-permute-start(f32[57,8,128]{2,1,0:T(8,128)S(1)} %get-tuple-element.25.refs_0_), channel_id=1, source_target_pairs={{0,16},{1,17},{2,18},{3,19},{4,20},{5,21},{6,22},{7,23},{8,24},{9,... | collective-permute-start | bytes 700424 | tf_op jit(solution)/shard_map/ppermute | solution.py:792
  3.2 5.7 %collective-permute-start.2 = (f32[2,14,8,128]{3,2,1,0:T(8,128)S(1)}, f32[2,14,8,128]{3,2,1,0:T(8,128)S(1)}, u32[]{:S(2)}, u32[]{:S(2)}) collective-permute-start(f32[2,14,8,128]{3,2,1,0:T(8,128)S(1)} %bitcast_dynamic-update-slice_fusion), channel_id=1, source_target_pairs={{0,4},{1,5},{2,6},{3,7},{4,0},{5,1},{6,2},{7,3},{8,12},{9,13},{10,... | collective-permute-start | bytes 344072 | tf_op jit(solution)/shard_map/ppermute | solution.py:792
  8.8 2.6 %collective-permute-start.3 = (f32[2,14,8,128]{3,2,1,0:T(8,128)S(1)}, f32[2,14,8,128]{3,2,1,0:T(8,128)S(1)}, u32[]{:S(2)}, u32[]{:S(2)}) collective-permute-start(f32[2,14,8,128]{3,2,1,0:T(8,128)S(1)} %collective-permute-done.2.refs_2_), channel_id=1, source_target_pairs={{0,16},{1,17},{2,18},{3,19},{4,20},{5,21},{6,22},{7,23},{8,24},{9,... | collective-permute-start | bytes 344072 | tf_op jit(solution)/shard_map/ppermute | solution.py:792
  11.8 4.0 %collective-permute-start.4 = (f32[8,8,128]{2,1,0:T(8,128)S(1)}, f32[8,8,128]{2,1,0:T(8,128)S(1)}, u32[]{:S(2)}, u32[]{:S(2)}) collective-permute-start(f32[8,8,128]{2,1,0:T(8,128)S(1)} %shard_map.87), channel_id=1, source_target_pairs={{0,1},{1,0},{2,3},{3,2},{4,5},{5,4},{6,7},{7,6},{8,9},{9,8},{10,11... | collective-permute-start | bytes 98312 | tf_op jit(solution)/shard_map/ppermute | solution.py:792
  15.8 1.2 %collective-permute-start.5 = (f32[8,8,128]{2,1,0:T(8,128)S(1)}, f32[8,8,128]{2,1,0:T(8,128)S(1)}, u32[]{:S(2)}, u32[]{:S(2)}) collective-permute-start(f32[8,8,128]{2,1,0:T(8,128)S(1)} %collective-permute-done.4.refs_4_), channel_id=1, source_target_pairs={{0,16},{1,17},{2,18},{3,19},{4,20},{5,21},{6,22},{7,23},{8,24},{9,... | collective-permute-start | bytes 98312 | tf_op jit(solution)/shard_map/ppermute | solution.py:792
